TPU v7x, 32 devices: a whole 2x2x4 slice. The times are simulated.
32 devices in a mesh: loop: 8 (over z, y), dp: 4 (over x, core).
Axes of the slice: x: 2, y: 2, z: 4, core: 2. Of those that a mesh axis runs over, the one named last changes fastest.
Arguments:
- node_states: bfloat16 [8192, 512], P(('loop', 'dp')), may hold values from -24 to 24
- virtual_states: bfloat16 [64, 512], replicated, may hold values from -6 to 6
- projection: bfloat16 [3, 512, 512], replicated, may hold values from -0.25 to 0.25
- pattern: int32 [64, 5], P(('loop', 'dp')), may hold values from 0 to 63, as said below
- valid_counts: int32 [64], P(('loop', 'dp')), may hold values from 32 to 128, as said below
- node_cotangent: bfloat16 [8192, 512], P(('loop', 'dp')), may hold values from -6 to 6
- virtual_cotangent: bfloat16 [64, 512], replicated, may hold values from -6 to 6
Outputs:
- node_out: bfloat16 [8192, 512], P(('loop', 'dp'))
- virtual_out: bfloat16 [64, 512], replicated
- node_grad: bfloat16 [8192, 512], P(('loop', 'dp'))
- virtual_grad: bfloat16 [64, 512], replicated
- weight_grads: float32 [3, 512, 512], replicated
Inputs may be any that keep to these rules, and one draw needn't show every extreme that they name: `pattern`: entry 0 of row b is b. The entries of a row are distinct, and each names a block on the device that holds b or on one of the two devices with the same dp index next to it along the loop axis, which closes (its last index is next to its first). Block b lies on device b // 2, devices numbered with the loop index first. `valid_counts`: at least one block is full.
All inputs are finite; a program needn't handle non-finite values.
Results may differ from a plain program's by a relative error of at most 0.013.
The roundings to bfloat16 on the way count: a program that leaves them out, or rounds other values in their place, can miss the bound.
Values may be sent and summed in bfloat16 or wider, within the bound.
No kernel may reach another device: no remote copies, remote signals or barrier semaphores. Data moves between devices by JAX's collectives and lax.ppermute only.
A program may use at most 256 MiB of HBM per device.

v0:
```python
import jax
import jax.numpy as jnp
from jax import lax
from jax.sharding import PartitionSpec as P

H = 8


NEG_FILL = -1e30
HIGHEST = lax.Precision.HIGHEST


def passed_along(value, axis, steps):
    count = lax.axis_size(axis)
    pairs = [(source, (source + steps) % count) for source in range(count)]
    return lax.ppermute(value, axis, pairs)


def head_split(matrix):
    return matrix.reshape(matrix.shape[0], H, matrix.shape[1] // H)


def score_block(query_rows, key_rows, key_ok):
    score_scale = (query_rows.shape[1] // H) ** (-0.5)
    raw_scores = (
        jnp.einsum(
            "qhd,khd->hqk",
            head_split(query_rows),
            head_split(key_rows),
            preferred_element_type=jnp.float32,
        )
        * score_scale
    )
    return (jnp.where(key_ok[None, None, :], raw_scores, NEG_FILL), score_scale)


def key_side(attention, weights, weight_grad, delta_sum, score_scale, query_rows, grad_rows):
    feat_width = query_rows.shape[1]
    score_grad = (attention * (weight_grad - delta_sum[..., None]) * score_scale).astype(
        jnp.bfloat16
    )
    key_gradient = jnp.einsum(
        "hqk,qhd->khd", score_grad, head_split(query_rows), preferred_element_type=jnp.float32
    )
    value_grad = jnp.einsum(
        "hqk,qhd->khd", weights, head_split(grad_rows), preferred_element_type=jnp.float32
    )
    return (score_grad, key_gradient.reshape(-1, feat_width), value_grad.reshape(-1, feat_width))


def block_step(items):
    query_rows, grad_rows, query_ok, key_rows, value_rows, key_ok = items
    raw_scores, score_scale = score_block(query_rows, key_rows, key_ok)
    row_peak = jnp.max(raw_scores, axis=-1)
    exponent = jnp.exp(raw_scores - row_peak[..., None])
    row_total = jnp.sum(exponent, axis=-1)
    attention = exponent / row_total[..., None]
    weights = attention.astype(jnp.bfloat16)
    value_heads = head_split(value_rows)
    mixture = jnp.einsum(
        "hqk,khd->qhd", weights, value_heads, preferred_element_type=jnp.float32
    ).reshape(query_rows.shape)
    node_row_list = jnp.where(query_ok[:, None], mixture, 0.0).astype(jnp.bfloat16)
    weight_grad = jnp.einsum(
        "qhd,khd->hqk", head_split(grad_rows), value_heads, preferred_element_type=jnp.float32
    )
    delta_sum = jnp.sum(attention * weight_grad, axis=-1)
    score_grad, key_gradient, value_grad = key_side(
        attention, weights, weight_grad, delta_sum, score_scale, query_rows, grad_rows
    )
    query_gradient = jnp.einsum(
        "hqk,khd->qhd", score_grad, head_split(key_rows), preferred_element_type=jnp.float32
    ).reshape(query_rows.shape)
    log_total = row_peak + jnp.log(row_total)
    return (node_row_list, query_gradient, key_gradient, value_grad, log_total, delta_sum)


def window_slots(pattern, loop_of_rows, loop_size, lane_size, own_blocks):
    device_of = pattern // own_blocks
    circle_offset = (device_of // lane_size - loop_of_rows + 1 + 2 * loop_size) % loop_size
    return circle_offset * own_blocks + pattern % own_blocks


def select_keys(window_keys, window_values, window_ok, slot_index):
    own_blocks, pat_len = slot_index.shape
    block_rows = window_keys.shape[1]
    feat_width = window_keys.shape[2]
    key_rows = window_keys[slot_index].reshape(own_blocks, pat_len * block_rows, feat_width)
    value_rows = window_values[slot_index].reshape(own_blocks, pat_len * block_rows, feat_width)
    key_ok = window_ok[slot_index].reshape(own_blocks, pat_len * block_rows)
    return (key_rows, value_rows, key_ok)


def local(
    node_states,
    virtual_states,
    projection,
    pattern,
    valid_counts,
    node_cotangent,
    virtual_cotangent,
):
    node_row_list, feat_width = node_states.shape
    own_blocks, pat_len = pattern.shape
    block_rows = node_row_list // own_blocks
    virtual_rows = virtual_states.shape[0]
    loop_size = lax.axis_size("loop")
    lane_size = lax.axis_size("dp")
    loop_here = lax.axis_index("loop")
    triple = jnp.einsum(
        "nd,tde->tne", node_states, projection, preferred_element_type=jnp.float32
    ).astype(jnp.bfloat16)
    queries, keys_own, values_own = (triple[0], triple[1], triple[2])
    virt_triple = jnp.einsum(
        "ud,tde->tue", virtual_states, projection, preferred_element_type=jnp.float32
    ).astype(jnp.bfloat16)
    virt_queries, virt_keys, virt_values = (virt_triple[0], virt_triple[1], virt_triple[2])
    positions = jnp.arange(block_rows, dtype=jnp.int32)
    own_ok = positions[None, :] < valid_counts[:, None]
    node_ok = own_ok.reshape(node_row_list)
    grad_masked = jnp.where(node_ok[:, None], node_cotangent, jnp.zeros_like(node_cotangent))
    arrived = []
    for step_by in (1, -1):
        arrived.append(passed_along((keys_own, values_own, valid_counts), "loop", step_by))
    window_keys = jnp.concatenate([arrived[0][0], keys_own, arrived[1][0]], axis=0).reshape(
        3 * own_blocks, block_rows, feat_width
    )
    window_values = jnp.concatenate([arrived[0][1], values_own, arrived[1][1]], axis=0).reshape(
        3 * own_blocks, block_rows, feat_width
    )
    window_counts = jnp.concatenate([arrived[0][2], valid_counts, arrived[1][2]], axis=0)
    window_ok = positions[None, :] < window_counts[:, None]
    slot_index = window_slots(pattern, loop_here, loop_size, lane_size, own_blocks)
    key_rows, value_rows, key_ok = select_keys(window_keys, window_values, window_ok, slot_index)
    key_rows = jnp.concatenate(
        [key_rows, jnp.broadcast_to(virt_keys[None], (own_blocks, virtual_rows, feat_width))],
        axis=1,
    )
    value_rows = jnp.concatenate(
        [value_rows, jnp.broadcast_to(virt_values[None], (own_blocks, virtual_rows, feat_width))],
        axis=1,
    )
    key_ok = jnp.concatenate(
        [key_ok, jnp.ones((own_blocks, virtual_rows), dtype=jnp.bool_)], axis=1
    )
    query_blocks = queries.reshape(own_blocks, block_rows, feat_width)
    grad_blocks = grad_masked.reshape(own_blocks, block_rows, feat_width)
    results = lax.map(block_step, (query_blocks, grad_blocks, own_ok, key_rows, value_rows, key_ok))
    node_blocks, query_gradient, key_gradient, value_grad, log_total, delta_sum = results
    node_out = node_blocks.reshape(node_row_list, feat_width)
    real_node_count = pat_len * block_rows
    window_span = jnp.arange(3 * own_blocks, dtype=jnp.int32)
    onehot = (slot_index[:, :, None] == window_span[None, None, :]).astype(jnp.float32)
    window_kgrad = jnp.einsum(
        "pkw,pkbd->wbd",
        onehot,
        key_gradient[:, :real_node_count].reshape(own_blocks, pat_len, block_rows, feat_width),
        precision=HIGHEST,
    )
    window_vgrad = jnp.einsum(
        "pkw,pkbd->wbd",
        onehot,
        value_grad[:, :real_node_count].reshape(own_blocks, pat_len, block_rows, feat_width),
        precision=HIGHEST,
    )
    virtual_key_part = jnp.sum(key_gradient[:, real_node_count:], axis=0)
    virtual_value_part = jnp.sum(value_grad[:, real_node_count:], axis=0)
    virt_scores, score_scale = score_block(virt_queries, keys_own, node_ok)
    local_peak = jnp.max(virt_scores, axis=-1)
    value_float = head_split(values_own).astype(jnp.float32)
    glob_peak = lax.pmax(local_peak, ("loop", "dp"))
    glob_exp = jnp.exp(virt_scores - glob_peak[..., None])
    glob_mix, glob_total = lax.psum(
        (
            jnp.einsum("hun,nhd->hud", glob_exp, value_float, precision=HIGHEST),
            jnp.sum(glob_exp, axis=-1),
        ),
        ("loop", "dp"),
    )
    virt_mixed = glob_mix / glob_total[..., None]
    virtual_out = (
        jnp.transpose(virt_mixed, (1, 0, 2)).reshape(virtual_rows, feat_width).astype(jnp.bfloat16)
    )
    virt_attn = glob_exp / glob_total[..., None]
    virt_grad_heads = head_split(virtual_cotangent)
    virt_dw = jnp.einsum(
        "uhd,nhd->hun", virt_grad_heads, head_split(values_own), preferred_element_type=jnp.float32
    )
    virt_delta = jnp.sum(
        virt_grad_heads.astype(jnp.float32) * jnp.transpose(virt_mixed, (1, 0, 2)), axis=-1
    ).T
    virt_ds = (virt_attn * (virt_dw - virt_delta[..., None]) * score_scale).astype(jnp.bfloat16)
    virtual_query_part = jnp.einsum(
        "hun,nhd->uhd", virt_ds, head_split(keys_own), preferred_element_type=jnp.float32
    ).reshape(virtual_rows, feat_width)
    key_sum_total = window_kgrad[own_blocks : 2 * own_blocks].reshape(
        node_row_list, feat_width
    ) + jnp.einsum(
        "hun,uhd->nhd", virt_ds, head_split(virt_queries), preferred_element_type=jnp.float32
    ).reshape(
        node_row_list, feat_width
    )
    value_sum_total = window_vgrad[own_blocks : 2 * own_blocks].reshape(
        node_row_list, feat_width
    ) + jnp.einsum(
        "hun,uhd->nhd",
        virt_attn.astype(jnp.bfloat16),
        virt_grad_heads,
        preferred_element_type=jnp.float32,
    ).reshape(
        node_row_list, feat_width
    )
    for step_by, slot_start in ((-1, 0), (1, 2)):
        outgoing = (
            window_kgrad[slot_start * own_blocks : (slot_start + 1) * own_blocks].reshape(
                node_row_list, feat_width
            ),
            window_vgrad[slot_start * own_blocks : (slot_start + 1) * own_blocks].reshape(
                node_row_list, feat_width
            ),
        )
        incoming = passed_along((outgoing[0], outgoing[1]), "loop", step_by)
        key_sum_total = key_sum_total + incoming[0]
        value_sum_total = value_sum_total + incoming[1]
    grad_stack = jnp.stack(
        [query_gradient.reshape(node_row_list, feat_width), key_sum_total, value_sum_total]
    ).astype(jnp.bfloat16)
    node_grad = jnp.einsum(
        "tne,tde->nd", grad_stack, projection, preferred_element_type=jnp.float32
    ).astype(jnp.bfloat16)
    virtual_gradient_part = jnp.stack([virtual_query_part, virtual_key_part, virtual_value_part])
    weight_part = jnp.einsum(
        "nd,tne->tde", node_states, grad_stack, preferred_element_type=jnp.float32
    ) + jnp.einsum(
        "ud,tue->tde", virtual_states.astype(jnp.float32), virtual_gradient_part, precision=HIGHEST
    )
    weight_grads, vgrad_total = lax.psum((weight_part, virtual_gradient_part), ("loop", "dp"))
    virtual_grad = jnp.einsum(
        "tue,tde->ud", vgrad_total, projection.astype(jnp.float32), precision=HIGHEST
    ).astype(jnp.bfloat16)
    return (node_out, virtual_out, node_grad, virtual_grad, weight_grads)


def solution(mesh):
    return jax.shard_map(
        local,
        mesh=mesh,
        in_specs=(
            P(("loop", "dp"), None),
            P(),
            P(),
            P(("loop", "dp"), None),
            P(("loop", "dp")),
            P(("loop", "dp"), None),
            P(),
        ),
        out_specs=(P(("loop", "dp"), None), P(), P(("loop", "dp"), None), P(), P()),
        check_vma=False,
    )
```

profile of v0, /device:TPU:0, one launch (start us, length us, event | category | flops | bytes accessed | tf_op | source)
XLA Modules:
  0.0 492.5 jit_solution(12875194493630563070)
XLA Ops:
  7.2 1.3 copy-done
  8.6 1.6 fusion.41
  10.9 6.0 %collective-permute-start.1 = (bf16[256,512]{0,1:T(8,128)(2,1)}, bf16[256,512]{0,1:T(8,128)(2,1)}, u32[]{:S(2)}, u32[]{:S(2)}) collective-permute-start(bf16[256,512]{0,1:T(8,128)(2,1)} %get-tuple-element.154), channel_id=1, source_target_pairs={{0,28},{4,0},{8,4},{12,8},{16,12},{20,16},{24,20},{28,24},{1,29},{... | collective-permute-start | bytes 786440 | tf_op jit(solution)/shard_map/ppermute | solution.py:16
  17.0 4.7 collective-permute-start.5
  21.7 4.7 collective-permute-start.3
  26.4 1.3 fusion.81
  28.6 43.7 %pmax.7 = f32[8,64]{1,0:T(8,128)S(1)} all-reduce(f32[8,64]{1,0:T(8,128)S(1)} %get-tuple-element.163), channel_id=1, replica_groups=mesh['loop'=8,'dp'=4] {'loop','dp'}, use_global_device_ids=true, to_apply=%region_6.7 | all-reduce | flops 512 | bytes 4096 | tf_op jit(solution)/shard_map/pmax | solution.py:171
  72.3 1.2 fusion.58
  75.4 1.8 broadcast_select_fusion
  77.1 38.8 %psum.29 = f32[8,64]{1,0:T(8,128)S(1)} all-reduce(f32[8,64]{1,0:T(8,128)S(1)} %fusion.57), channel_id=1, replica_groups=mesh['loop'=8,'dp'=4] {'loop','dp'}, use_global_device_ids=true, to_apply=%region_9.10 | all-reduce | flops 512 | bytes 4096 | tf_op jit(solution)/shard_map/psum | solution.py:173
  116.9 1.2 fusion.62
  118.2 2.0 copy.80
  120.2 2.3 collective-permute-start.2
  122.5 4.1 collective-permute-done.2
  128.0 69.6 %all-reduce.5.cloned.1.call-done = f32[8,64,64]{2,1,0:T(8,128)} async-done(((f32[8,64,64]{2,1,0:T(8,128)}), f32[8,64,64]{2,1,0:T(8,128)}) %all-reduce.5.cloned.1.call-update) | async-done | bytes 131088 | tf_op jit(solution)/shard_map/psum | solution.py:173
  197.7 1.2 fusion.59
  201.4 1.2 pad_maximum_fusion.2
  202.8 1.8 gather_fusion
  204.6 1.1 pad_maximum_fusion.3
  206.0 1.8 gather_fusion.2
  207.8 3.6 pad_maximum_fusion
  211.4 67.3 %while.16 = (s32[]{:T(128)}, bf16[2,128,512]{2,1,0:T(8,128)(2,1)}, bf16[2,128,512]{1,2,0:T(8,128)(2,1)}, f32[2,704,512]{1,2,0:T(8,128)}, f32[2,704,512]{1,2,0:T(...) while((s32[]{:T(128)}, bf16[2,128,512]{2,1,0:T(8,128)(2,1)}, ...), condition=%wide.region_4.5_spmd, body=%wide.region_0.4_spmd.sunk | while | flops 569577536 | bytes 48388788 | solution.py:148
  211.4 1.2 constant_dynamic-slice_fusion.9
  213.8 1.2 constant_dynamic-slice_fusion.11
  215.0 1.2 copy.116
  216.2 4.0 fusion.147
  220.2 2.2 fusion.148
  224.3 2.3 fusion.151
  226.6 5.4 %fusion.152 = bf16[8,64,128]{2,1,0:T(8,128)(2,1)S(1)} fusion(bf16[704,8,64]{0,2,1:T(8,128)(2,1)S(1)} %bitcast.188, f32[8,128,704]{1,2,0:T(8,128)} %fusion.151, f32[8,128,704]{1,2,0:T(8,128)} %get-tuple-element.238, f32[8,128]{1,0:T(8,128)S(1)} %get-tuple-element.239), kind=kOutput, calls=%fused_computation.12.clone.1 | convolution fusion | flops 97322688 | bytes 6623232 | tf_op jit(solution)/shard_map/while/body/eval_jaxpr/hqk,khd->qhd/dot_general | solution.py:71
  232.7 2.5 fusion.153
  235.2 6.6 %fusion.154 = f32[8,64,704]{2,1,0:T(8,128)} fusion(bf16[128,8,64]{0,2,1:T(8,128)(2,1)S(1)} %bitcast.198, f32[8,128,704]{1,2,0:T(8,128)} %fusion.151, f32[8,128,704]{1,2,0:T(8,128)} %get-tuple-element.238, f32[8,128]{1,0:T(8,128)S(1)} %get-tuple-element.239), kind=kOutput, calls=%fused_computation.11.clone.1 | convolution fusion | flops 97322688 | bytes 7344128 | tf_op jit(solution)/shard_map/while/body/eval_jaxpr/hqk,qhd->khd/dot_general | solution.py:42
  241.8 3.3 constant_dynamic-update-slice_fusion.9
  245.0 1.2 constant_dynamic-slice_fusion.9
  247.4 1.2 constant_dynamic-slice_fusion.11
  248.6 1.2 copy.116
  249.8 4.0 fusion.147
  253.8 2.2 fusion.148
  257.9 2.3 fusion.151
  260.2 5.4 %fusion.152 = bf16[8,64,128]{2,1,0:T(8,128)(2,1)S(1)} fusion(bf16[704,8,64]{0,2,1:T(8,128)(2,1)S(1)} %bitcast.188, f32[8,128,704]{1,2,0:T(8,128)} %fusion.151, f32[8,128,704]{1,2,0:T(8,128)} %get-tuple-element.238, f32[8,128]{1,0:T(8,128)S(1)} %get-tuple-element.239), kind=kOutput, calls=%fused_computation.12.clone.1 | convolution fusion | flops 97322688 | bytes 6623232 | tf_op jit(solution)/shard_map/while/body/eval_jaxpr/hqk,khd->qhd/dot_general | solution.py:71
  266.4 2.5 fusion.153
  268.9 6.6 %fusion.154 = f32[8,64,704]{2,1,0:T(8,128)} fusion(bf16[128,8,64]{0,2,1:T(8,128)(2,1)S(1)} %bitcast.198, f32[8,128,704]{1,2,0:T(8,128)} %fusion.151, f32[8,128,704]{1,2,0:T(8,128)} %get-tuple-element.238, f32[8,128]{1,0:T(8,128)S(1)} %get-tuple-element.239), kind=kOutput, calls=%fused_computation.11.clone.1 | convolution fusion | flops 97322688 | bytes 7344128 | tf_op jit(solution)/shard_map/while/body/eval_jaxpr/hqk,qhd->khd/dot_general | solution.py:42
  275.4 3.3 constant_dynamic-update-slice_fusion.9
  278.7 3.5 copy.76
  282.2 1.3 slice_reduce_fusion
  284.1 4.3 fusion.38
  289.8 1.4 collective-permute-start.9
  292.1 3.3 collective-permute-start.8
  295.6 3.7 copy.67
  299.2 1.7 slice-done.1
  301.0 4.3 fusion.35
  307.7 4.7 collective-permute-start.6
  313.5 1.9 slice_reduce_fusion.1
  317.2 2.3 fusion.68
  319.6 6.8 %collective-permute-done.9 = f32[256,512]{1,0:T(8,128)} collective-permute-done((f32[256,512]{1,0:T(8,128)}, f32[256,512]{1,0:T(8,128)}, u32[]{:S(2)}, u32[]{:S(2)}) %collective-permute-start.9) | collective-permute-done | bytes 524320 | tf_op jit(solution)/shard_map/ppermute | solution.py:16
  326.4 2.0 collective-permute-done.8
  328.4 1.4 fusion.52
  329.8 6.0 %collective-permute-done.7 = f32[256,512]{1,0:T(8,128)} collective-permute-done((f32[256,512]{1,0:T(8,128)}, f32[256,512]{1,0:T(8,128)}, u32[]{:S(2)}, u32[]{:S(2)}) %collective-permute-start.7) | collective-permute-done | bytes 524320 | tf_op jit(solution)/shard_map/ppermute | solution.py:16
  335.7 3.1 collective-permute-done.6
  338.8 1.4 fusion.55
  340.2 2.3 add_bitcast_fusion
  344.5 1.3 fusion.47
  345.8 133.1 %all-reduce.7.cloned.1.call-done = (f32[3,64,512]{2,1,0:T(8,128)}, f32[3,512,512]{1,2,0:T(8,128)}) async-done(((f32[3,64,512]{2,1,0:T(8,128)}, f32[3,512,512]{1,2,0:T(8,128)}), (f32[3,64,512]{2,1,0:T(8,128)}, f32[3,512,512]{1,2,0:T(8,128)})) %all-reduce.7.cloned.1.call-update) | async-done | bytes 3538960 | tf_op jit(solution)/shard_map/psum | solution.py:237
  478.9 3.2 fusion.49
  482.1 3.5 copy.87
  (121 shorter events, 27.0 us)
Async XLA Ops:
  7.2 1.4 copy-start
  7.2 20.5 %copy-start.11 = (bf16[64,512]{1,0:T(8,128)(2,1)S(1)}, bf16[64,512]{1,0:T(8,128)(2,1)}, u32[]{:S(2)}) copy-start(bf16[64,512]{1,0:T(8,128)(2,1)} %param.10) | copy-start | bytes 196612
  7.2 190.5 %all-reduce.5.cloned.1.call-start = ((), (), s32[]{:S(2)}) async-start(), calls=%async_computation | async-start | bytes 524288 | tf_op jit(solution)/shard_map/psum | solution.py:173
  10.9 63.6 %copy-start.9 = (bf16[1,256,512]{1,2,0:T(8,128)(2,1)}, bf16[1,256,512]{1,2,0:T(8,128)(2,1)S(1)}, u32[]{:S(2)}) copy-start(bf16[1,256,512]{1,2,0:T(8,128)(2,1)S(1)} %get-tuple-element.157) | copy-start | bytes 786436
  10.9 62.9 %copy-start.16 = (s32[2,5]{1,0:T(2,128)S(1)}, s32[2,5]{1,0:T(2,128)}, u32[]{:S(2)}) copy-start(s32[2,5]{1,0:T(2,128)} %param.12) | copy-start | bytes 124
  10.9 190.4 %collective-permute-start.1 = (bf16[256,512]{0,1:T(8,128)(2,1)}, bf16[256,512]{0,1:T(8,128)(2,1)}, u32[]{:S(2)}, u32[]{:S(2)}) collective-permute-start(bf16[256,512]{0,1:T(8,128)(2,1)} %get-tuple-element.154), channel_id=1, source_target_pairs={{0,28},{4,0},{8,4},{12,8},{16,12},{20,16},{24,20},{28,24},{1,29},{... | collective-permute-start | bytes 786440 | tf_op jit(solution)/shard_map/ppermute | solution.py:16
  17.0 184.4 %collective-permute-start = (bf16[256,512]{0,1:T(8,128)(2,1)}, bf16[256,512]{0,1:T(8,128)(2,1)}, u32[]{:S(2)}, u32[]{:S(2)}) collective-permute-start(bf16[256,512]{0,1:T(8,128)(2,1)} %get-tuple-element.154), channel_id=1, source_target_pairs={{0,4},{4,8},{8,12},{12,16},{16,20},{20,24},{24,28},{28,0},{1,5},{5... | collective-permute-start | bytes 786440 | tf_op jit(solution)/shard_map/ppermute | solution.py:16
  17.0 187.7 %collective-permute-start.5 = (bf16[256,512]{0,1:T(8,128)(2,1)S(1)}, bf16[256,512]{0,1:T(8,128)(2,1)}, u32[]{:S(2)}, u32[]{:S(2)}) collective-permute-start(bf16[256,512]{0,1:T(8,128)(2,1)S(1)} %get-tuple-element.155), channel_id=1, source_target_pairs={{0,28},{4,0},{8,4},{12,8},{16,12},{20,16},{24,20},{28,24},{1,29},{... | collective-permute-start | bytes 786440 | tf_op jit(solution)/shard_map/ppermute | solution.py:16
  21.7 183.0 %collective-permute-start.4 = (bf16[256,512]{0,1:T(8,128)(2,1)S(1)}, bf16[256,512]{0,1:T(8,128)(2,1)}, u32[]{:S(2)}, u32[]{:S(2)}) collective-permute-start(bf16[256,512]{0,1:T(8,128)(2,1)S(1)} %get-tuple-element.155), channel_id=1, source_target_pairs={{0,4},{4,8},{8,12},{12,16},{16,20},{20,24},{24,28},{28,0},{1,5},{5... | collective-permute-start | bytes 786440 | tf_op jit(solution)/shard_map/ppermute | solution.py:16
  21.7 98.5 %collective-permute-start.3 = (s32[2]{0:T(128)}, s32[2]{0:T(128)}, u32[]{:S(2)}, u32[]{:S(2)}) collective-permute-start(s32[2]{0:T(128)} %param.13), channel_id=1, source_target_pairs={{0,28},{4,0},{8,4},{12,8},{16,12},{20,16},{24,20},{28,24},{1,29},{... | collective-permute-start | bytes 32 | tf_op jit(solution)/shard_map/ppermute | solution.py:16
  73.5 405.5 %all-reduce.7.cloned.1.call-start = ((), (), s32[]{:S(2)}) async-start(), calls=%async_computation.1 | async-start | bytes 7077888 | tf_op jit(solution)/shard_map/psum | solution.py:237
  74.6 124.3 %copy-start.10 = (bf16[1,256,512]{1,2,0:T(8,128)(2,1)S(1)}, bf16[1,256,512]{1,2,0:T(8,128)(2,1)}, u32[]{:S(2)}) copy-start(bf16[1,256,512]{1,2,0:T(8,128)(2,1)} %copy-done.9) | copy-start | bytes 786436
  120.2 6.4 %collective-permute-start.2 = (s32[2]{0:T(128)}, s32[2]{0:T(128)S(1)}, u32[]{:S(2)}, u32[]{:S(2)}) collective-permute-start(s32[2]{0:T(128)} %param.13), channel_id=1, source_target_pairs={{0,4},{4,8},{8,12},{12,16},{16,20},{20,24},{24,28},{28,0},{1,5},{5... | collective-permute-start | bytes 32 | tf_op jit(solution)/shard_map/ppermute | solution.py:16
  207.8 3.6 copy-start.17
  222.4 4.2 copy-start.1
  226.6 5.4 %copy-start.12 = (bf16[2,128,512]{1,2,0:T(8,128)(2,1)S(1)}, bf16[2,128,512]{1,2,0:T(8,128)(2,1)}, u32[]{:S(2)}) copy-start(bf16[2,128,512]{1,2,0:T(8,128)(2,1)} %get-tuple-element.256) | copy-start | bytes 786436 | tf_op jit(solution)/shard_map/while
  232.0 0.7 copy-start.13
  256.0 4.2 copy-start.1
  260.2 5.4 %copy-start.12 = (bf16[2,128,512]{1,2,0:T(8,128)(2,1)S(1)}, bf16[2,128,512]{1,2,0:T(8,128)(2,1)}, u32[]{:S(2)}) copy-start(bf16[2,128,512]{1,2,0:T(8,128)(2,1)} %get-tuple-element.256) | copy-start | bytes 786436 | tf_op jit(solution)/shard_map/while
  265.7 0.7 copy-start.13
  282.2 1.9 slice-start
  282.2 1.9 copy-start.15
  289.8 36.6 %collective-permute-start.9 = (f32[256,512]{1,0:T(8,128)}, f32[256,512]{1,0:T(8,128)}, u32[]{:S(2)}, u32[]{:S(2)}) collective-permute-start(f32[256,512]{1,0:T(8,128)} %bitcast.51), channel_id=1, source_target_pairs={{0,4},{4,8},{8,12},{12,16},{16,20},{20,24},{24,28},{28,0},{1,5},{5... | collective-permute-start | bytes 1572872 | tf_op jit(solution)/shard_map/ppermute | solution.py:16
  292.1 36.2 %collective-permute-start.8 = (f32[256,512]{1,0:T(8,128)}, f32[256,512]{1,0:T(8,128)}, u32[]{:S(2)}, u32[]{:S(2)}) collective-permute-start(f32[256,512]{1,0:T(8,128)} %bitcast.50), channel_id=1, source_target_pairs={{0,28},{4,0},{8,4},{12,8},{16,12},{20,16},{24,20},{28,24},{1,29},{... | collective-permute-start | bytes 1572872 | tf_op jit(solution)/shard_map/ppermute | solution.py:16
  299.2 1.7 slice-start.1
  305.3 7.2 %copy-start.14 = (bf16[2,128,512]{1,2,0:T(8,128)(2,1)S(1)}, bf16[2,128,512]{1,2,0:T(8,128)(2,1)}, u32[]{:S(2)}) copy-start(bf16[2,128,512]{1,2,0:T(8,128)(2,1)} %get-tuple-element.66) | copy-start | bytes 786436
  305.9 10.6 %copy-start.4 = (f32[1,64,512]{2,1,0:T(8,128)S(1)}, f32[1,64,512]{2,1,0:T(8,128)}, u32[]{:S(2)}) copy-start(f32[1,64,512]{2,1,0:T(8,128)} %copy.85) | copy-start | bytes 393220
  306.8 28.9 %collective-permute-start.7 = (f32[256,512]{1,0:T(8,128)}, f32[256,512]{1,0:T(8,128)}, u32[]{:S(2)}, u32[]{:S(2)}) collective-permute-start(f32[256,512]{1,0:T(8,128)} %bitcast.42), channel_id=1, source_target_pairs={{0,4},{4,8},{8,12},{12,16},{16,20},{20,24},{24,28},{28,0},{1,5},{5... | collective-permute-start | bytes 1572872 | tf_op jit(solution)/shard_map/ppermute | solution.py:16
  307.7 31.1 %collective-permute-start.6 = (f32[256,512]{1,0:T(8,128)}, f32[256,512]{1,0:T(8,128)}, u32[]{:S(2)}, u32[]{:S(2)}) collective-permute-start(f32[256,512]{1,0:T(8,128)} %bitcast.41), channel_id=1, source_target_pairs={{0,28},{4,0},{8,4},{12,8},{16,12},{20,16},{24,20},{28,24},{1,29},{... | collective-permute-start | bytes 1572872 | tf_op jit(solution)/shard_map/ppermute | solution.py:16
  313.5 14.9 %copy-start.2 = (f32[256,512]{1,0:T(8,128)S(1)}, f32[256,512]{1,0:T(8,128)}, u32[]{:S(2)}) copy-start(f32[256,512]{1,0:T(8,128)} %copy.80) | copy-start | bytes 1572868
  317.2 21.6 %copy-start.3 = (f32[256,512]{1,0:T(8,128)S(1)}, f32[256,512]{1,0:T(8,128)}, u32[]{:S(2)}) copy-start(f32[256,512]{1,0:T(8,128)} %copy.73) | copy-start | bytes 1572868
  319.6 20.6 %copy-start.5 = (bf16[256,512]{1,0:T(8,128)(2,1)S(1)}, bf16[256,512]{1,0:T(8,128)(2,1)}, u32[]{:S(2)}) copy-start(bf16[256,512]{1,0:T(8,128)(2,1)} %param.9) | copy-start | bytes 786436
  319.6 20.6 %copy-start.6 = (bf16[2,128,512]{2,1,0:T(8,128)(2,1)S(1)}, bf16[2,128,512]{2,1,0:T(8,128)(2,1)}, u32[]{:S(2)}) copy-start(bf16[2,128,512]{2,1,0:T(8,128)(2,1)} %copy.66) | copy-start | bytes 786436
  342.5 0.9 copy-start.8
  342.5 2.0 copy-start.7
Sparse Core Ops, SparseCore 0:
  73.6 124.0 all-reduce.4
  342.7 136.2 all-reduce.6
where the time goes:
time: 494 us; the launch traced here: 492 us
  waiting for transfers between devices  225 us (46%)
  blocking collectives  82.6 us (17%)
  matrix products  69 us (14%)
  local copies, waits for them, and re-layouts  55.7 us (11%)
  starting transfers between devices  27.2 us (6%)
  other arithmetic  18.6 us (4%)
  between operations  14.4 us (3%)
    psum x1, waiting for transfers between devices, local(): lax.psum((weight_part, virtual_gradient_part), ('loop', 'dp'))  133 us
    psum x1, waiting for transfers between devices, local(): lax.psum((jnp.einsum('hun,nhd->hud', glob_exp, value_float, precision=HIG...  69.6 us
    pmax x1, blocking collectives, local(): glob_peak = lax.pmax(local_peak, ('loop', 'dp'))  43.7 us
    psum x1, blocking collectives, local(): lax.psum((jnp.einsum('hun,nhd->hud', glob_exp, value_float, precision=HIG...  38.8 us
    ppermute x10, starting transfers between devices, passed_along(): return lax.ppermute(value, axis, pairs)  27.2 us
    ppermute x10, waiting for transfers between devices, passed_along(): return lax.ppermute(value, axis, pairs)  21.9 us
    dot_general x2, matrix products, key_side(): jnp.einsum('hqk,qhd->khd', score_grad, head_split(query_rows), preferred_...  13.1 us
    dynamic_slice x18, local copies, waits for them, and re-layouts, local(): lax.map(block_step, (query_blocks, grad_blocks, own_ok, key_rows, value_r...  11.6 us
  transfers between devices with their start and end apart: 12, of which 7 were waited for; matrix products, arithmetic and copies ran while one was open for 8% of the time, Pallas kernels for 0%

commit v1 on v0

v1 whole, which is shorter than its diff:
```python
import functools

import jax
import jax.numpy as jnp
from jax import lax
from jax.experimental import pallas as pl
from jax.experimental.pallas import tpu as pltpu
from jax.sharding import PartitionSpec as P

H = 8
NEG_FILL = -1e30
SHARDS = 32
BF = jnp.bfloat16
F32 = jnp.float32


def nn(a, b):
    return lax.dot_general(a, b, (((1,), (0,)), ((), ())), preferred_element_type=F32)


def nt(a, b):
    return lax.dot_general(a, b, (((1,), (1,)), ((), ())), preferred_element_type=F32)


def tn(a, b):
    return lax.dot_general(a, b, (((0,), (0,)), ((), ())), preferred_element_type=F32)


def lane_half(pair, half):
    lane = lax.broadcasted_iota(jnp.int32, pair.shape, 1)
    width = pair.shape[1] // 2
    keep = lane < width if half == 0 else lane >= width
    return jnp.where(keep, pair, jnp.zeros_like(pair))


def both_heads(pair):
    return jnp.concatenate([lane_half(pair, 0), lane_half(pair, 1)], axis=0)


def own_row_ok(counts_ref, blocks, block_rows, shape):
    row = lax.broadcasted_iota(jnp.int32, shape, 0)
    limit = jnp.full(shape, counts_ref[0], jnp.int32)
    for b in range(1, blocks):
        limit = jnp.where(row < b * block_rows, limit, b * block_rows + counts_ref[b])
    return row < limit


def project_kernel(blocks, block_rows, score_scale, counts_ref, x_ref, vs_ref, vcot_ref, w_ref,
                   q_ref, k_ref, v_ref, virt_ref, stats_ref):
    x = x_ref[...]
    k = nn(x, w_ref[1]).astype(BF)
    v = nn(x, w_ref[2]).astype(BF)
    k_ref[...] = k
    v_ref[...] = v
    virt = [nn(vs_ref[...], w_ref[t]).astype(BF) for t in range(3)]
    for t in range(3):
        virt_ref[t] = virt[t]
    virt_q = virt[0] * score_scale
    n, width = x.shape
    ok = own_row_ok(counts_ref, blocks, block_rows, (n, 128))
    peaks, totals, deltas = [], [], []
    for c in range(0, width, 128):
        scores = nt(k[:, c:c + 128], both_heads(virt_q[:, c:c + 128]))
        scores = jnp.where(ok, scores, NEG_FILL)
        peak = jnp.max(scores, axis=0, keepdims=True)
        e = jnp.where(ok, jnp.exp(scores - peak), 0.0)
        dw = nt(v[:, c:c + 128], both_heads(vcot_ref[:, c:c + 128]))
        peaks.append(peak)
        totals.append(jnp.sum(e, axis=0, keepdims=True))
        deltas.append(jnp.sum(e * dw, axis=0, keepdims=True))
    rows = jnp.concatenate(peaks + totals + deltas + peaks, axis=0)
    stats_ref[...] = jnp.broadcast_to(rows[None], stats_ref.shape)
    q_ref[...] = nn(x, w_ref[0]).astype(BF) * score_scale


def attention_kernel(blocks, block_rows, lanes, score_scale, place_ref, pat_ref, cl_ref, co_ref, cr_ref, xl_ref, xr_ref,
                     w_ref, q_ref, k_ref, v_ref, g_ref, virt_ref, out_ref, dq_ref, dk_ref, dv_ref,
                     key_s, val_s, bias_s, ot_s, dqt_s):
    n, width = q_ref.shape
    virtual_rows = virt_ref.shape[1]
    loop_here, loop_size = place_ref[0], place_ref[1]
    for at, ref in ((0, xl_ref), (2, xr_ref)):
        x = ref[...]
        key_s[at * n:(at + 1) * n, :] = nn(x, w_ref[1]).astype(BF)
        val_s[at * n:(at + 1) * n, :] = nn(x, w_ref[2]).astype(BF)
    key_s[n:2 * n, :] = k_ref[...]
    val_s[n:2 * n, :] = v_ref[...]
    key_s[3 * n:3 * n + virtual_rows, :] = virt_ref[1]
    val_s[3 * n:3 * n + virtual_rows, :] = virt_ref[2]
    row = lax.broadcasted_iota(jnp.int32, (block_rows, block_rows), 0)
    for i in range(blocks):
        slots = []
        for j in range(pat_ref.shape[1]):
            block = pat_ref[i, j]
            ring = (block // blocks) // lanes
            offset = lax.rem(ring - loop_here + 1 + 2 * loop_size, loop_size)
            slots.append(offset * blocks + lax.rem(block, blocks))
        for b in range(3 * blocks):
            count = (cl_ref, co_ref, cr_ref)[b // blocks][b % blocks]
            listed = slots[0] == b
            for s in slots[1:]:
                listed = jnp.logical_or(listed, s == b)
            count = jnp.where(listed, count, 0)
            bias_s[b * block_rows:(b + 1) * block_rows, i * block_rows:(i + 1) * block_rows] = jnp.where(
                row < count, 0.0, NEG_FILL)
    bias_s[3 * n:3 * n + virtual_rows, :] = jnp.zeros((virtual_rows, n), F32)
    ok = own_row_ok(co_ref, blocks, block_rows, (n, 128))
    for c in range(0, width, 128):
        k_pair, v_pair = key_s[:, c:c + 128], val_s[:, c:c + 128]
        q_pair = q_ref[:, c:c + 128]
        g_pair = jnp.where(ok, g_ref[:, c:c + 128], jnp.zeros((n, 128), BF))
        dk_pair = dv_pair = None
        for half in range(2):
            qm, gm = lane_half(q_pair, half), lane_half(g_pair, half)
            s = nt(k_pair, qm) + bias_s[...]
            e = jnp.exp(s - jnp.max(s, axis=0, keepdims=True))
            a = e * (1.0 / jnp.sum(e, axis=0, keepdims=True))
            wt = a.astype(BF)
            dw = nt(v_pair, gm)
            delta = jnp.sum(a * dw, axis=0, keepdims=True)
            ds = (a * (dw - delta)).astype(BF)
            at = c + half * 64
            ot_s[at:at + 64, :] = tn(v_pair, wt)[half * 64:half * 64 + 64]
            dqt_s[at:at + 64, :] = tn(k_pair, ds)[half * 64:half * 64 + 64]
            dk, dv = nn(ds, qm), nn(wt, gm)
            dk_pair = dk if dk_pair is None else dk_pair + dk
            dv_pair = dv if dv_pair is None else dv_pair + dv
        dk_ref[:, c:c + 128] = dk_pair
        dv_ref[:, c:c + 128] = dv_pair
    okw = own_row_ok(co_ref, blocks, block_rows, (n, width))
    out_ref[...] = jnp.where(okw, ot_s[...].T, 0.0).astype(BF)
    dq_ref[...] = (dqt_s[...].T * score_scale).astype(BF)


def weight_kernel(blocks, block_rows, score_scale, counts_ref, ids_ref, x_ref, xl_ref, xr_ref, vs_ref, vcot_ref, w_ref,
                  k_ref, v_ref, virt_ref, stats_ref, dq_ref, dk_ref, dv_ref,
                  keep_a, send_a, keep_b, send_b, kown_ref, vown_ref, wg_s, vg_s, vo_s, vgrad_s, dkw_s, dvw_s):
    n, width = x_ref.shape
    virtual_rows = vs_ref.shape[0]
    ok = own_row_ok(counts_ref, blocks, block_rows, (n, 128))
    pairs = width // 128
    stats = stats_ref[...]
    peak = jnp.max(stats[:, 0:pairs], axis=0)
    factor = jnp.exp(stats[:, 0:pairs] - peak[None])
    total = jnp.sum(stats[:, pairs:2 * pairs] * factor, axis=0)
    delta = jnp.sum(stats[:, 2 * pairs:3 * pairs] * factor, axis=0) / total
    inv_total = 1.0 / total
    lane_low = lax.broadcasted_iota(jnp.int32, (virtual_rows, 128), 1) < 64

    def diagonal(square):
        return jnp.where(lane_low, square[:virtual_rows], square[virtual_rows:])

    dkw_s[...] = dk_ref[0:3 * n, :].astype(BF)
    dvw_s[...] = dv_ref[0:3 * n, :].astype(BF)
    for p in range(pairs):
        c = p * 128
        k_pair, v_pair = k_ref[:, c:c + 128], v_ref[:, c:c + 128]
        vq = both_heads(virt_ref[0, :, c:c + 128])
        vcot = both_heads(vcot_ref[:, c:c + 128])
        scores = jnp.where(ok, nt(k_pair, vq * score_scale), NEG_FILL)
        attn = jnp.exp(scores - peak[p:p + 1]) * inv_total[p:p + 1]
        attn_hi = attn.astype(BF)
        attn_lo = (attn - attn_hi.astype(F32)).astype(BF)
        dw = nt(v_pair, vcot)
        ds = (attn * (dw - delta[p:p + 1]) * score_scale).astype(BF)
        vo_s[:, c:c + 128] = diagonal(tn(attn_hi, v_pair) + tn(attn_lo, v_pair))
        vgrad_s[0, :, c:c + 128] = diagonal(tn(ds, k_pair))
        dkw_s[n:2 * n, c:c + 128] = (dk_ref[n:2 * n, c:c + 128] + nn(ds, vq)).astype(BF)
        dvw_s[n:2 * n, c:c + 128] = (dv_ref[n:2 * n, c:c + 128] + nn(attn_hi, vcot)).astype(BF)
    vgrad_s[1] = dk_ref[3 * n:3 * n + virtual_rows, :]
    vgrad_s[2] = dv_ref[3 * n:3 * n + virtual_rows, :]
    xs = jnp.concatenate([xl_ref[...], x_ref[...], xr_ref[...]], axis=0)
    vs = vs_ref[...]
    vg = None
    for t in range(3):
        part = vgrad_s[t]
        hi = part.astype(BF)
        lo = (part - hi.astype(F32)).astype(BF)
        if t == 0:
            wg = tn(x_ref[...], dq_ref[...])
        else:
            wg = tn(xs, (dkw_s if t == 1 else dvw_s)[...])
        wg_s[t] = wg + (tn(vs, hi) + tn(vs, lo))
        back = nt(hi, w_ref[t]) + nt(lo, w_ref[t])
        vg = back if vg is None else vg + back
    vg_s[...] = vg
    row_groups = width // 64
    for name, refs in ((0, (keep_a, send_a)), (1, (keep_b, send_b))):
        me = ids_ref[name]
        for p in range(SHARDS):
            ref, at = refs[p // (SHARDS // 2)], p % (SHARDS // 2)
            shard = jnp.bitwise_xor(me, p)
            cols = pl.ds(pl.multiple_of((shard // row_groups) * 128, 128), 128)
            group = lax.rem(shard, row_groups)
            for t in range(3):
                rows = pl.ds(pl.multiple_of(group * 64 + name * 32, 32), 32)
                ref[at, t * 32:(t + 1) * 32, :] = wg_s[t, rows, cols].astype(BF)
            if name == 0:
                rows = pl.ds(pl.multiple_of(group * 8, 8), 8)
                ref[at, 96:112, :] = jnp.concatenate([vg_s[rows, cols], vo_s[rows, cols]], axis=0).astype(BF)
    kown_ref[...] = dkw_s[...]
    vown_ref[...] = dvw_s[...]


def node_kernel(w_ref, dq_ref, dk_ref, dv_ref, left_ref, right_ref, own_ref):
    n = dq_ref.shape[0]
    for at, ref in ((0, left_ref), (2, right_ref), (1, own_ref)):
        rows = slice(at * n, (at + 1) * n)
        part = nt(dk_ref[rows, :], w_ref[1]) + nt(dv_ref[rows, :], w_ref[2])
        if at == 1:
            part = part + nt(dq_ref[...], w_ref[0])
        ref[...] = part.astype(ref.dtype)


def unpack_kernel(ids_ref, a0_ref, a1_ref, b0_ref, b1_ref, wg_ref, vg_ref, vo_ref):
    width = wg_ref.shape[2]
    row_groups = width // 64
    for name, refs in ((0, (a0_ref, a1_ref)), (1, (b0_ref, b1_ref))):
        me = ids_ref[name]
        for p in range(SHARDS):
            ref, at = refs[p // (SHARDS // 2)], p % (SHARDS // 2)
            shard = jnp.bitwise_xor(me, p)
            cols = pl.ds(pl.multiple_of((shard // row_groups) * 128, 128), 128)
            group = lax.rem(shard, row_groups)
            for t in range(3):
                rows = pl.ds(pl.multiple_of(group * 64 + name * 32, 32), 32)
                wg_ref[t, rows, cols] = ref[at, t * 32:(t + 1) * 32, :].astype(F32)
            if name == 0:
                rows = pl.ds(pl.multiple_of(group * 8, 8), 8)
                both = ref[at, 96:112, :].astype(F32)
                vg_ref[rows, cols] = both[0:8]
                vo_ref[rows, cols] = both[8:16]


SMEM = pl.BlockSpec(memory_space=pltpu.SMEM)
VMEM = pl.BlockSpec(memory_space=pltpu.VMEM)


def call(body, args, specs, outs, scratch=(), flops=1e8, name=None):
    return pl.pallas_call(
        body,
        out_shape=[jax.ShapeDtypeStruct(s, d) for s, d in outs],
        in_specs=specs,
        out_specs=[VMEM] * len(outs),
        scratch_shapes=[pltpu.VMEM(s, d) for s, d in scratch],
        compiler_params=pltpu.CompilerParams(vmem_limit_bytes=40 << 20),
        cost_estimate=pl.CostEstimate(flops=int(flops), bytes_accessed=4 << 20, transcendentals=0),
        name=name,
    )(*args)


def ring(value, steps):
    count = lax.axis_size("loop")
    return lax.ppermute(value, "loop", [(s, (s + steps) % count) for s in range(count)])


def swap(value, axis, bit):
    return lax.ppermute(value, axis, [(s, s ^ bit) for s in range(lax.axis_size(axis))])


def add(a, b):
    return (a.astype(F32) + b.astype(F32)).astype(BF)


def reduce_all(keep_a, send_a, keep_b, send_b):
    loop_size = lax.axis_size("loop")
    x_bit, y_bit = ("dp", 2), ("loop", 1)
    orders = {"a": (x_bit, y_bit), "b": (y_bit, x_bit)}
    held = {"a": add(keep_a, swap(send_a, "dp", 1)), "b": add(keep_b, swap(send_b, "dp", 1))}
    for step in range(2):
        halves = {k: h.shape[0] // 2 for k, h in held.items()}
        got = {k: swap(h[halves[k]:], *orders[k][step]) for k, h in held.items()}
        held = {k: add(h[:halves[k]], got[k]) for k, h in held.items()}
    both = jnp.concatenate([held["a"], held["b"]], axis=1)
    got = [swap(both[j], "loop", 2 * j) for j in range(1, 4)]
    piece = both[0].astype(F32)
    for g in got:
        piece = piece + g.astype(F32)
    piece = piece.astype(BF)
    bit = 8
    while bit < loop_size:
        piece = add(piece, swap(piece, "loop", bit))
        bit *= 2
    full = jnp.stack([piece] + [swap(piece, "loop", 2 * j) for j in range(1, 4)])
    rows_a = keep_a.shape[1]
    held = {"a": full[:, :rows_a], "b": full[:, rows_a:]}
    for step in (1, 0):
        got = {k: swap(h, *orders[k][step]) for k, h in held.items()}
        held = {k: jnp.concatenate([h, got[k]], axis=0) for k, h in held.items()}
    return held["a"], swap(held["a"], "dp", 1), held["b"], swap(held["b"], "dp", 1)


def local(node_states, virtual_states, projection, pattern, valid_counts, node_cotangent, virtual_cotangent):
    n, width = node_states.shape
    blocks = pattern.shape[0]
    block_rows = n // blocks
    virtual_rows = virtual_states.shape[0]
    loop_size, lanes = lax.axis_size("loop"), lax.axis_size("dp")
    devices = loop_size * lanes
    loop_here, lane_here = lax.axis_index("loop"), lax.axis_index("dp")
    score_scale = (width // H) ** -0.5
    keys = 3 * n + virtual_rows

    x_left, x_right = ring(node_states, 1), ring(node_states, -1)
    c_left, c_right = ring(valid_counts, 1), ring(valid_counts, -1)

    place = jnp.stack([loop_here, jnp.int32(loop_size)]).astype(jnp.int32)
    core, x_at = lane_here & 1, (lane_here >> 1) & 1
    y_at, z_at = loop_here & 1, (loop_here >> 1) & 3
    ids = jnp.stack([core * 16 + x_at * 8 + y_at * 4 + z_at, core * 16 + y_at * 8 + x_at * 4 + z_at]).astype(jnp.int32)

    q, k, v, virt, stats = call(
        functools.partial(project_kernel, blocks, block_rows, score_scale),
        (valid_counts, node_states, virtual_states, virtual_cotangent, projection),
        [SMEM] + [VMEM] * 4,
        [((n, width), BF)] * 3 + [((3, virtual_rows, width), BF), ((devices, 16, 128), F32)],
        name="project")
    stats = lax.all_to_all(stats, ("loop", "dp"), 0, 0, tiled=True)

    node_out, dq, dk, dv = call(
        functools.partial(attention_kernel, blocks, block_rows, lanes, score_scale),
        (place, pattern, c_left, valid_counts, c_right, x_left, x_right, projection, q, k, v, node_cotangent, virt),
        [SMEM] * 5 + [VMEM] * 8,
        [((n, width), BF)] * 2 + [((keys, width), F32)] * 2,
        [((keys, width), BF)] * 2 + [((keys, n), F32)] + [((width, n), F32)] * 2,
        flops=4e9, name="attention")

    keep_a, send_a, keep_b, send_b, dk_all, dv_all = call(
        functools.partial(weight_kernel, blocks, block_rows, score_scale),
        (valid_counts, ids, node_states, x_left, x_right, virtual_states, virtual_cotangent, projection, k, v, virt, stats,
         dq, dk, dv),
        [SMEM] * 2 + [VMEM] * 13,
        [((SHARDS // 2, 112, 128), BF)] * 2 + [((SHARDS // 2, 96, 128), BF)] * 2 + [((3 * n, width), BF)] * 2,
        [((3, width, width), F32)] + [((virtual_rows, width), F32)] * 2 + [((3, virtual_rows, width), F32)]
        + [((3 * n, width), BF)] * 2,
        flops=1.2e9, name="weight_grads")

    to_left, to_right, own_part = call(
        node_kernel, (projection, dq, dk_all, dv_all), [VMEM] * 4,
        [((n, width), BF)] * 2 + [((n, width), F32)], flops=1e9, name="node_grads")
    from_right, from_left = ring(to_left, -1), ring(to_right, 1)

    pieces = reduce_all(keep_a, send_a, keep_b, send_b)
    node_grad = (own_part + from_right.astype(F32) + from_left.astype(F32)).astype(BF)
    weight_grads, virtual_grad, virtual_out = call(
        unpack_kernel, (ids,) + tuple(pieces), [SMEM] + [VMEM] * 4,
        [((3, width, width), F32)] + [((virtual_rows, width), F32)] * 2, name="unpack")
    return node_out, virtual_out.astype(BF), node_grad, virtual_grad.astype(BF), weight_grads


def solution(mesh):
    return jax.shard_map(
        local,
        mesh=mesh,
        in_specs=(
            P(("loop", "dp"), None),
            P(),
            P(),
            P(("loop", "dp"), None),
            P(("loop", "dp")),
            P(("loop", "dp"), None),
            P(),
        ),
        out_specs=(P(("loop", "dp"), None), P(), P(("loop", "dp"), None), P(), P()),
        check_vma=False,
    )
```

time: 494 us -> 124 us (0.25)
  waiting for transfers between devices: 225 us -> 27.9 us
  blocking collectives: 82.6 us -> 0 us
  matrix products: 69 us -> 0 us
  local copies, waits for them, and re-layouts: 55.7 us -> 27.5 us
  Pallas kernels: 0 us -> 22 us
  other arithmetic: 18.6 us -> 2.88 us
  starting transfers between devices: 27.2 us -> 42.2 us
  between operations: 14.4 us -> 0.86 us
    psum x2 -> x0, waiting for transfers between devices: 203 us -> none  [the longest x1 133 us: local(): lax.psum((weight_part, virtual_gradient_part), ('loop', 'dp'))]
    dot_general x24 -> x0, matrix products: 61.1 us -> none  [the longest x2 13.1 us: key_side(): jnp.einsum('hqk,qhd->khd', score_grad, head_split(query_rows), preferred_...]
    pmax x1 -> x0, blocking collectives: 43.7 us -> none  [local(): glob_peak = lax.pmax(local_peak, ('loop', 'dp'))]
    psum x1 -> x0, blocking collectives: 38.8 us -> none  [local(): lax.psum((jnp.einsum('hun,nhd->hud', glob_exp, value_float, precision=HIG...]
    pallas_call x0 -> x5, Pallas kernels: none -> 22 us  [call(): pl.pallas_call(body, out_shape=[jax.ShapeDtypeStruct(s, d) for s, d in ou...]
    unnamed x31 -> x72, local copies, waits for them, and re-layouts: 5.87 us -> 27.4 us
    dynamic_slice x18 -> x0, local copies, waits for them, and re-layouts: 11.6 us -> none  [local(): lax.map(block_step, (query_blocks, grad_blocks, own_ok, key_rows, value_r...]
    while x15 -> x0, local copies, waits for them, and re-layouts: 9.3 us -> none  [the longest x3 7.89 us: local(): lax.map(block_step, (query_blocks, grad_blocks, own_ok, key_rows, value_r...]
  transfers between devices with their start and end apart: 12 -> 25, of which waited for: 7 -> 14; matrix products, arithmetic and copies ran while one was open for 8% -> 1% of each run, Pallas kernels for 0% -> 11%
where the time goes in v1:
time: 124 us; the launch traced here: 123 us
  starting transfers between devices  42.2 us (34%)
  waiting for transfers between devices  27.9 us (22%)
  local copies, waits for them, and re-layouts  27.5 us (22%)
  Pallas kernels  22 us (18%)
  other arithmetic  2.88 us (2%)
    unnamed x72, local copies, waits for them, and re-layouts  27.4 us
    ppermute x18, starting transfers between devices, swap(): lax.ppermute(value, axis, [(s, s ^ bit) for s in range(lax.axis_size(axis...  23.2 us
    pallas_call x5, Pallas kernels, call(): pl.pallas_call(body, out_shape=[jax.ShapeDtypeStruct(s, d) for s, d in ou...  22 us
    ppermute x18, waiting for transfers between devices, swap(): lax.ppermute(value, axis, [(s, s ^ bit) for s in range(lax.axis_size(axis...  21.4 us
    ppermute x6, starting transfers between devices, ring(): lax.ppermute(value, 'loop', [(s, (s + steps) % count) for s in range(coun...  12.9 us
    ppermute x6, waiting for transfers between devices, ring(): lax.ppermute(value, 'loop', [(s, (s + steps) % count) for s in range(coun...  6.42 us
    all_to_all x1, starting transfers between devices, local(): stats = lax.all_to_all(stats, ('loop', 'dp'), 0, 0, tiled=True)  6.14 us
  transfers between devices with their start and end apart: 25, of which 14 were waited for; matrix products, arithmetic and copies ran while one was open for 1% of the time, Pallas kernels for 11%

profile of v1, /device:TPU:0, one launch (start us, length us, event | category | flops | bytes accessed | tf_op | source)
XLA Modules:
  0.0 123.2 jit_solution(15454736663910057745)
XLA Ops:
  0.6 6.1 %collective-permute-start.3 = (bf16[256,512]{1,0:T(8,128)(2,1)}, bf16[256,512]{1,0:T(8,128)(2,1)S(1)}, u32[]{:S(2)}, u32[]{:S(2)}) collective-permute-start(bf16[256,512]{1,0:T(8,128)(2,1)} %x_ref.3), channel_id=1, source_target_pairs={{0,28},{4,0},{8,4},{12,8},{16,12},{20,16},{24,20},{28,24},{1,29},{... | collective-permute-start | bytes 786440 | tf_op jit(solution)/shard_map/ppermute | solution.py:254
  6.7 4.7 %collective-permute-start.1 = (s32[2]{0:T(128)}, s32[2]{0:T(128)S(1)}, u32[]{:S(2)}, u32[]{:S(2)}) collective-permute-start(s32[2]{0:T(128)} %counts_ref.3), channel_id=1, source_target_pairs={{0,28},{4,0},{8,4},{12,8},{16,12},{20,16},{24,20},{28,24},{1,29},{... | collective-permute-start | bytes 32 | tf_op jit(solution)/shard_map/ppermute | solution.py:254
  11.4 1.4 %copy-done = bf16[3,512,512]{2,1,0:T(8,128)(2,1)S(1)} copy-done((bf16[3,512,512]{2,1,0:T(8,128)(2,1)S(1)}, bf16[3,512,512]{2,1,0:T(8,128)(2,1)}, u32[]{:S(2)}) %copy-start) | copy-done | bytes 1572888
  12.8 0.9 copy-done.4
  13.8 0.8 copy-done.6
  14.6 0.8 copy-done.8
  15.5 0.7 copy-done.28
  16.1 2.3 %project.1 = (bf16[256,512]{1,0:T(8,128)(2,1)S(1)}, bf16[256,512]{1,0:T(8,128)(2,1)S(1)}, bf16[256,512]{1,0:T(8,128)(2,1)S(1)}, bf16[3,64,512]{2,1,0:T(8,128)(2,1)S(1)}, f32[32,16,128]{2,1,0:T(8,128)}) custom-call(s32[2]{0:T(128)S(1)} %copy-done.28, bf16[256,512]{1,0:T(8,128)(2,1)S(1)} %copy-done.4, bf16[64,512]{1,0:T(8,128)(2,1)S(1)} %copy-done.6, ...), custom_call_target="tpu_custom_call" | custom-call | flops 100000000 | bytes 4194304 | tf_op jit(solution)/shard_map/project/pallas_call | solution.py:240
  18.4 0.7 copy-done.19
  19.1 0.7 copy-done.22
  19.9 0.7 copy-done.25
  20.5 0.7 copy-done.31
  21.2 6.1 %all-to-all-start = ((f32[32,16,128]{2,1,0:T(8,128)}), f32[32,16,128]{2,1,0:T(8,128)}, u32[]{:S(2)}, u32[]{:S(2)}) async-start(f32[32,16,128]{2,1,0:T(8,128)} %get-tuple-element.31), calls=%async_computation | async-start | bytes 524288 | tf_op jit(solution)/shard_map/all_to_all | solution.py:318
  28.1 0.7 copy-done.13
  28.8 0.7 copy-done.16
  29.5 0.9 copy-done.14
  30.4 0.9 copy-done.17
  31.4 0.9 copy-done.20
  32.3 0.9 copy-done.23
  33.3 0.9 copy-done.26
  34.2 0.9 copy-done.30
  35.2 0.9 copy-done.32
  36.1 0.7 copy-done.35
  36.8 10.3 %attention.1 = (bf16[256,512]{1,0:T(8,128)(2,1)}, bf16[256,512]{1,0:T(8,128)(2,1)S(1)}, f32[832,512]{1,0:T(8,128)S(1)}, f32[832,512]{1,0:T(8,128)S(1)}) custom-call(s32[2]{0:T(128)S(1)} %pad_add_fusion.place_ref, s32[2,5]{1,0:T(2,128)S(1)} %copy-done.33, s32[2]{0:T(128)S(1)} %copy-done.35, s32[2]{0:T(128)S(1)} %copy-done.29, ...), custom_call_target="tpu_custom_call" | custom-call | flops 4000000000 | bytes 4194304 | tf_op jit(solution)/shard_map/attention/pallas_call | solution.py:240
  47.1 1.2 copy-done.2
  48.3 0.7 copy-done.10
  49.0 1.5 %copy-done.3 = f32[832,512]{1,0:T(8,128)S(1)} copy-done((f32[832,512]{1,0:T(8,128)S(1)}, f32[832,512]{1,0:T(8,128)}, u32[]{:S(2)}) %copy-start.3) | copy-done | bytes 1703960
  50.5 0.8 copy-done.7
  51.3 0.8 copy-done.9
  52.2 0.9 copy-done.11
  53.1 0.9 copy-done.15
  54.1 0.9 copy-done.18
  55.0 0.9 copy-done.21
  56.0 0.9 copy-done.24
  56.9 0.9 copy-done.27
  57.8 5.4 %weight_grads.1 = (bf16[16,112,128]{2,1,0:T(8,128)(2,1)S(1)}, bf16[16,112,128]{2,1,0:T(8,128)(2,1)S(1)}, bf16[16,96,128]{2,1,0:T(8,128)(2,1)S(1)}, bf16[16,96,12...) custom-call(s32[2]{0:T(128)S(1)} %copy-done.29, s32[2]{0:T(128)S(1)} %pad_add_fusion.1.ids_ref, ...), custom_call_target="tpu_custom_call" | custom-call | flops 1200000000 | bytes 4194304 | tf_op jit(solution)/shard_map/weight_grads/pallas_call | solution.py:240
  63.8 1.2 collective-permute-done.7
  65.2 1.8 %collective-permute-start.8 = (bf16[8,96,128]{2,1,0:T(8,128)(2,1)S(1)}, bf16[8,96,128]{2,1,0:T(8,128)(2,1)S(1)}, u32[]{:S(2)}, u32[]{:S(2)}) collective-permute-start(bf16[8,96,128]{2,1,0:T(8,128)(2,1)S(1)} %slice.61), channel_id=1, source_target_pairs={{0,4},{4,0},{8,12},{12,8},{16,20},{20,16},{24,28},{28,24},{1,5},{5... | collective-permute-start | bytes 589832 | tf_op jit(solution)/shard_map/ppermute | solution.py:258
  67.1 1.5 %collective-permute-start.5 = (bf16[8,112,128]{2,1,0:T(8,128)(2,1)S(1)}, bf16[8,112,128]{2,1,0:T(8,128)(2,1)S(1)}, u32[]{:S(2)}, u32[]{:S(2)}) collective-permute-start(bf16[8,112,128]{2,1,0:T(8,128)(2,1)S(1)} %slice.57), channel_id=1, source_target_pairs={{0,2},{1,3},{2,0},{3,1},{4,6},{5,7},{6,4},{7,5},{8,10},{9,11},{10,... | collective-permute-start | bytes 688136 | tf_op jit(solution)/shard_map/ppermute | solution.py:258
  68.6 3.6 %collective-permute-done.8 = bf16[8,96,128]{2,1,0:T(8,128)(2,1)S(1)} collective-permute-done((bf16[8,96,128]{2,1,0:T(8,128)(2,1)S(1)}, bf16[8,96,128]{2,1,0:T(8,128)(2,1)S(1)}, u32[]{:S(2)}, u32[]{:S(2)}) %collective-permute-start.8) | collective-permute-done | bytes 196640 | tf_op jit(solution)/shard_map/ppermute | solution.py:258
  72.3 1.7 %collective-permute-start.9 = (bf16[4,96,128]{2,1,0:T(8,128)(2,1)S(1)}, bf16[4,96,128]{2,1,0:T(8,128)(2,1)S(1)}, u32[]{:S(2)}, u32[]{:S(2)}) collective-permute-start(bf16[4,96,128]{2,1,0:T(8,128)(2,1)S(1)} %slice.63), channel_id=1, source_target_pairs={{0,2},{1,3},{2,0},{3,1},{4,6},{5,7},{6,4},{7,5},{8,10},{9,11},{10,... | collective-permute-start | bytes 294920 | tf_op jit(solution)/shard_map/ppermute | solution.py:258
  74.8 0.9 collective-permute-start.6
  75.7 1.3 %collective-permute-done.9 = bf16[4,96,128]{2,1,0:T(8,128)(2,1)S(1)} collective-permute-done((bf16[4,96,128]{2,1,0:T(8,128)(2,1)S(1)}, bf16[4,96,128]{2,1,0:T(8,128)(2,1)S(1)}, u32[]{:S(2)}, u32[]{:S(2)}) %collective-permute-start.9) | collective-permute-done | bytes 98336 | tf_op jit(solution)/shard_map/ppermute | solution.py:258
  77.0 2.6 %collective-permute-done.6 = bf16[4,112,128]{2,1,0:T(8,128)(2,1)S(1)} collective-permute-done((bf16[4,112,128]{2,1,0:T(8,128)(2,1)S(1)}, bf16[4,112,128]{2,1,0:T(8,128)(2,1)S(1)}, u32[]{:S(2)}, u32[]{:S(2)}) %collective-permute-start.6) | collective-permute-done | bytes 114720 | tf_op jit(solution)/shard_map/ppermute | solution.py:258
  79.7 1.4 %collective-permute-start.10 = (bf16[208,128]{1,0:T(8,128)(2,1)S(1)}, bf16[208,128]{1,0:T(8,128)(2,1)S(1)}, u32[]{:S(2)}, u32[]{:S(2)}) collective-permute-start(bf16[208,128]{1,0:T(8,128)(2,1)S(1)} %get-tuple-element.47), channel_id=1, source_target_pairs={{0,8},{4,12},{8,0},{12,4},{16,24},{20,28},{24,16},{28,20},{1,9},{5... | collective-permute-start | bytes 159752 | tf_op jit(solution)/shard_map/ppermute | solution.py:258
  81.1 2.4 %collective-permute-start.12 = (bf16[208,128]{1,0:T(8,128)(2,1)S(1)}, bf16[208,128]{1,0:T(8,128)(2,1)S(1)}, u32[]{:S(2)}, u32[]{:S(2)}) collective-permute-start(bf16[208,128]{1,0:T(8,128)(2,1)S(1)} %get-tuple-element.48), channel_id=1, source_target_pairs={{0,24},{4,28},{8,16},{12,20},{16,8},{20,12},{24,0},{28,4},{1,25},{... | collective-permute-start | bytes 159752 | tf_op jit(solution)/shard_map/ppermute | solution.py:258
  84.2 2.8 %collective-permute-done.12 = bf16[208,128]{1,0:T(8,128)(2,1)S(1)} collective-permute-done((bf16[208,128]{1,0:T(8,128)(2,1)S(1)}, bf16[208,128]{1,0:T(8,128)(2,1)S(1)}, u32[]{:S(2)}, u32[]{:S(2)}) %collective-permute-start.12) | collective-permute-done | bytes 53280 | tf_op jit(solution)/shard_map/ppermute | solution.py:258
  87.0 2.2 %collective-permute-done.11 = bf16[208,128]{1,0:T(8,128)(2,1)S(1)} collective-permute-done((bf16[208,128]{1,0:T(8,128)(2,1)S(1)}, bf16[208,128]{1,0:T(8,128)(2,1)S(1)}, u32[]{:S(2)}, u32[]{:S(2)}) %collective-permute-start.11) | collective-permute-done | bytes 53280 | tf_op jit(solution)/shard_map/ppermute | solution.py:258
  89.3 1.9 %collective-permute-start.15 = (bf16[208,128]{1,0:T(8,128)(2,1)S(1)}, bf16[208,128]{1,0:T(8,128)(2,1)S(1)}, u32[]{:S(2)}, u32[]{:S(2)}) collective-permute-start(bf16[208,128]{1,0:T(8,128)(2,1)S(1)} %fusion.2), channel_id=1, source_target_pairs={{0,24},{4,28},{8,16},{12,20},{16,8},{20,12},{24,0},{28,4},{1,25},{... | collective-permute-start | bytes 159752 | tf_op jit(solution)/shard_map/ppermute | solution.py:258
  91.2 2.5 %collective-permute-start.13 = (bf16[208,128]{1,0:T(8,128)(2,1)S(1)}, bf16[208,128]{1,0:T(8,128)(2,1)S(1)}, u32[]{:S(2)}, u32[]{:S(2)}) collective-permute-start(bf16[208,128]{1,0:T(8,128)(2,1)S(1)} %fusion.2), channel_id=1, source_target_pairs={{0,8},{4,12},{8,0},{12,4},{16,24},{20,28},{24,16},{28,20},{1,9},{5... | collective-permute-start | bytes 159752 | tf_op jit(solution)/shard_map/ppermute | solution.py:258
  93.7 1.5 %collective-permute-done.15 = bf16[208,128]{1,0:T(8,128)(2,1)S(1)} collective-permute-done((bf16[208,128]{1,0:T(8,128)(2,1)S(1)}, bf16[208,128]{1,0:T(8,128)(2,1)S(1)}, u32[]{:S(2)}, u32[]{:S(2)}) %collective-permute-start.15) | collective-permute-done | bytes 53280 | tf_op jit(solution)/shard_map/ppermute | solution.py:258
  95.3 1.1 collective-permute-done.14
  96.5 1.4 %collective-permute-start.16 = (bf16[4,112,128]{2,1,0:T(8,128)(2,1)S(1)}, bf16[4,112,128]{2,1,0:T(8,128)(2,1)S(1)}, u32[]{:S(2)}, u32[]{:S(2)}) collective-permute-start(bf16[4,112,128]{2,1,0:T(8,128)(2,1)S(1)} %slice.70), channel_id=1, source_target_pairs={{0,4},{4,0},{8,12},{12,8},{16,20},{20,16},{24,28},{28,24},{1,5},{5... | collective-permute-start | bytes 344072 | tf_op jit(solution)/shard_map/ppermute | solution.py:258
  97.9 1.2 collective-permute-start.19
  99.1 3.4 %collective-permute-done.16 = bf16[4,112,128]{2,1,0:T(8,128)(2,1)S(1)} collective-permute-done((bf16[4,112,128]{2,1,0:T(8,128)(2,1)S(1)}, bf16[4,112,128]{2,1,0:T(8,128)(2,1)S(1)}, u32[]{:S(2)}, u32[]{:S(2)}) %collective-permute-start.16) | collective-permute-done | bytes 114720 | tf_op jit(solution)/shard_map/ppermute | solution.py:258
  102.5 2.8 %collective-permute-start.17 = (bf16[8,112,128]{2,1,0:T(8,128)(2,1)S(1)}, bf16[8,112,128]{2,1,0:T(8,128)(2,1)S(1)}, u32[]{:S(2)}, u32[]{:S(2)}) collective-permute-start(bf16[8,112,128]{2,1,0:T(8,128)(2,1)S(1)} %pad_maximum_fusion.2), channel_id=1, source_target_pairs={{0,2},{1,3},{2,0},{3,1},{4,6},{5,7},{6,4},{7,5},{8,10},{9,11},{10,... | collective-permute-start | bytes 688136 | tf_op jit(solution)/shard_map/ppermute | solution.py:258
  105.3 2.7 %collective-permute-start.20 = (bf16[8,96,128]{2,1,0:T(8,128)(2,1)S(1)}, bf16[8,96,128]{2,1,0:T(8,128)(2,1)S(1)}, u32[]{:S(2)}, u32[]{:S(2)}) collective-permute-start(bf16[8,96,128]{2,1,0:T(8,128)(2,1)S(1)} %pad_maximum_fusion.4), channel_id=1, source_target_pairs={{0,4},{4,0},{8,12},{12,8},{16,20},{20,16},{24,28},{28,24},{1,5},{5... | collective-permute-start | bytes 589832 | tf_op jit(solution)/shard_map/ppermute | solution.py:258
  108.0 1.2 node_grads.1
  109.2 2.0 %collective-permute-start.23 = (bf16[256,512]{1,0:T(8,128)(2,1)S(1)}, bf16[256,512]{1,0:T(8,128)(2,1)S(1)}, u32[]{:S(2)}, u32[]{:S(2)}) collective-permute-start(bf16[256,512]{1,0:T(8,128)(2,1)S(1)} %get-tuple-element.44), channel_id=1, source_target_pairs={{0,4},{4,8},{8,12},{12,16},{16,20},{20,24},{24,28},{28,0},{1,5},{5... | collective-permute-start | bytes 786440 | tf_op jit(solution)/shard_map/ppermute | solution.py:254
  112.0 3.6 %collective-permute-done.22 = bf16[256,512]{1,0:T(8,128)(2,1)S(1)} collective-permute-done((bf16[256,512]{1,0:T(8,128)(2,1)S(1)}, bf16[256,512]{1,0:T(8,128)(2,1)S(1)}, u32[]{:S(2)}, u32[]{:S(2)}) %collective-permute-start.22) | collective-permute-done | bytes 262176 | tf_op jit(solution)/shard_map/ppermute | solution.py:254
  115.6 2.8 %collective-permute-done.23 = bf16[256,512]{1,0:T(8,128)(2,1)S(1)} collective-permute-done((bf16[256,512]{1,0:T(8,128)(2,1)S(1)}, bf16[256,512]{1,0:T(8,128)(2,1)S(1)}, u32[]{:S(2)}, u32[]{:S(2)}) %collective-permute-start.23) | collective-permute-done | bytes 262176 | tf_op jit(solution)/shard_map/ppermute | solution.py:254
  118.4 0.8 add_convert_fusion.2
  119.2 2.7 %unpack.1 = (f32[3,512,512]{2,1,0:T(8,128)}, f32[64,512]{1,0:T(8,128)S(1)}, f32[64,512]{1,0:T(8,128)S(1)}) custom-call(s32[2]{0:T(128)S(1)} %pad_add_fusion.1.ids_ref, bf16[16,112,128]{2,1,0:T(8,128)(2,1)S(1)} %pad_maximum_fusion.a0_ref, bf16[16,112,128]{2,1,0:T(8,128)(2,1)S(1)} %collective-permute-done.18.a1_ref, ...), custom_call_target="tpu_custom_call" | custom-call | flops 100000000 | bytes 4194304 | tf_op jit(solution)/shard_map/unpack/pallas_call | solution.py:240
  122.0 0.6 convert_element_type.111
  (87 shorter events, 4.7 us)
Async XLA Ops:
  0.6 27.4 %collective-permute-start.3 = (bf16[256,512]{1,0:T(8,128)(2,1)}, bf16[256,512]{1,0:T(8,128)(2,1)S(1)}, u32[]{:S(2)}, u32[]{:S(2)}) collective-permute-start(bf16[256,512]{1,0:T(8,128)(2,1)} %x_ref.3), channel_id=1, source_target_pairs={{0,28},{4,0},{8,4},{12,8},{16,12},{20,16},{24,20},{28,24},{1,29},{... | collective-permute-start | bytes 786440 | tf_op jit(solution)/shard_map/ppermute | solution.py:254
  6.7 22.1 %collective-permute-start.2 = (bf16[256,512]{1,0:T(8,128)(2,1)}, bf16[256,512]{1,0:T(8,128)(2,1)S(1)}, u32[]{:S(2)}, u32[]{:S(2)}) collective-permute-start(bf16[256,512]{1,0:T(8,128)(2,1)} %x_ref.3), channel_id=1, source_target_pairs={{0,4},{4,8},{8,12},{12,16},{16,20},{20,24},{24,28},{28,0},{1,5},{5... | collective-permute-start | bytes 786440 | tf_op jit(solution)/shard_map/ppermute | solution.py:254
  6.7 20.9 %collective-permute-start.1 = (s32[2]{0:T(128)}, s32[2]{0:T(128)S(1)}, u32[]{:S(2)}, u32[]{:S(2)}) collective-permute-start(s32[2]{0:T(128)} %counts_ref.3), channel_id=1, source_target_pairs={{0,28},{4,0},{8,4},{12,8},{16,12},{20,16},{24,20},{28,24},{1,29},{... | collective-permute-start | bytes 32 | tf_op jit(solution)/shard_map/ppermute | solution.py:254
  11.4 16.1 %collective-permute-start = (s32[2]{0:T(128)}, s32[2]{0:T(128)S(1)}, u32[]{:S(2)}, u32[]{:S(2)}) collective-permute-start(s32[2]{0:T(128)} %counts_ref.3), channel_id=1, source_target_pairs={{0,4},{4,8},{8,12},{12,16},{16,20},{20,24},{24,28},{28,0},{1,5},{5... | collective-permute-start | bytes 32 | tf_op jit(solution)/shard_map/ppermute | solution.py:254
  11.4 1.4 %copy-start = (bf16[3,512,512]{2,1,0:T(8,128)(2,1)S(1)}, bf16[3,512,512]{2,1,0:T(8,128)(2,1)}, u32[]{:S(2)}) copy-start(bf16[3,512,512]{2,1,0:T(8,128)(2,1)} %w_ref.7) | copy-start | bytes 4718596
  12.8 0.9 copy-start.4
  13.8 0.8 copy-start.6
  14.6 0.8 copy-start.8
  15.5 0.7 copy-start.28
  16.1 13.4 %copy-start.1 = (bf16[3,512,512]{2,1,0:T(8,128)(2,1)S(1)}, bf16[3,512,512]{2,1,0:T(8,128)(2,1)}, u32[]{:S(2)}) copy-start(bf16[3,512,512]{2,1,0:T(8,128)(2,1)} %w_ref.7) | copy-start | bytes 4718596
  16.1 13.4 %copy-start.29 = (s32[2]{0:T(128)S(1)}, s32[2]{0:T(128)}, u32[]{:S(2)}) copy-start(s32[2]{0:T(128)} %counts_ref.3) | copy-start | bytes 28
  16.1 13.4 %copy-start.33 = (s32[2,5]{1,0:T(2,128)S(1)}, s32[2,5]{1,0:T(2,128)}, u32[]{:S(2)}) copy-start(s32[2,5]{1,0:T(2,128)} %pat_ref.1) | copy-start | bytes 124
  18.4 0.7 copy-start.19
  19.1 0.7 copy-start.22
  19.9 0.7 copy-start.25
  20.5 0.7 copy-start.31
  21.2 27.8 %all-to-all-start = ((f32[32,16,128]{2,1,0:T(8,128)}), f32[32,16,128]{2,1,0:T(8,128)}, u32[]{:S(2)}, u32[]{:S(2)}) async-start(f32[32,16,128]{2,1,0:T(8,128)} %get-tuple-element.31), calls=%async_computation | async-start | bytes 524288 | tf_op jit(solution)/shard_map/all_to_all | solution.py:318
  27.6 0.5 copy-start.34
  28.1 0.7 copy-start.13
  28.8 0.7 copy-start.16
  29.5 1.0 copy-start.14
  30.4 0.9 copy-start.17
  31.4 0.9 copy-start.20
  32.3 0.9 copy-start.23
  33.3 0.9 copy-start.26
  34.2 0.9 copy-start.30
  35.2 0.9 copy-start.32
  36.1 0.7 copy-start.35
  36.8 12.3 %copy-start.5 = (bf16[256,512]{1,0:T(8,128)(2,1)S(1)}, bf16[256,512]{1,0:T(8,128)(2,1)}, u32[]{:S(2)}) copy-start(bf16[256,512]{1,0:T(8,128)(2,1)} %x_ref.3) | copy-start | bytes 786436
  47.1 1.2 copy-start.2
  48.3 0.7 copy-start.10
  49.0 1.5 %copy-start.3 = (f32[832,512]{1,0:T(8,128)S(1)}, f32[832,512]{1,0:T(8,128)}, u32[]{:S(2)}) copy-start(f32[832,512]{1,0:T(8,128)} %copy-done.2) | copy-start | bytes 5111812
  50.5 0.8 copy-start.7
  51.3 0.8 copy-start.9
  52.2 0.9 copy-start.11
  53.1 0.9 copy-start.15
  54.1 0.9 copy-start.18
  55.0 0.9 copy-start.21
  56.0 0.9 copy-start.24
  56.9 0.9 copy-start.27
  63.3 1.8 %collective-permute-start.7 = (bf16[16,96,128]{2,1,0:T(8,128)(2,1)S(1)}, bf16[16,96,128]{2,1,0:T(8,128)(2,1)S(1)}, u32[]{:S(2)}, u32[]{:S(2)}) collective-permute-start(bf16[16,96,128]{2,1,0:T(8,128)(2,1)S(1)} %get-tuple-element.38), channel_id=1, source_target_pairs={{0,1},{1,0},{2,3},{3,2},{4,5},{5,4},{6,7},{7,6},{8,9},{9,8},{10,11... | collective-permute-start | bytes 1179656 | tf_op jit(solution)/shard_map/ppermute | solution.py:258
  63.5 3.4 %collective-permute-start.4 = (bf16[16,112,128]{2,1,0:T(8,128)(2,1)S(1)}, bf16[16,112,128]{2,1,0:T(8,128)(2,1)S(1)}, u32[]{:S(2)}, u32[]{:S(2)}) collective-permute-start(bf16[16,112,128]{2,1,0:T(8,128)(2,1)S(1)} %get-tuple-element.36), channel_id=1, source_target_pairs={{0,1},{1,0},{2,3},{3,2},{4,5},{5,4},{6,7},{7,6},{8,9},{9,8},{10,11... | collective-permute-start | bytes 1376264 | tf_op jit(solution)/shard_map/ppermute | solution.py:258
  65.2 7.1 %collective-permute-start.8 = (bf16[8,96,128]{2,1,0:T(8,128)(2,1)S(1)}, bf16[8,96,128]{2,1,0:T(8,128)(2,1)S(1)}, u32[]{:S(2)}, u32[]{:S(2)}) collective-permute-start(bf16[8,96,128]{2,1,0:T(8,128)(2,1)S(1)} %slice.61), channel_id=1, source_target_pairs={{0,4},{4,0},{8,12},{12,8},{16,20},{20,16},{24,28},{28,24},{1,5},{5... | collective-permute-start | bytes 589832 | tf_op jit(solution)/shard_map/ppermute | solution.py:258
  67.1 7.6 %collective-permute-start.5 = (bf16[8,112,128]{2,1,0:T(8,128)(2,1)S(1)}, bf16[8,112,128]{2,1,0:T(8,128)(2,1)S(1)}, u32[]{:S(2)}, u32[]{:S(2)}) collective-permute-start(bf16[8,112,128]{2,1,0:T(8,128)(2,1)S(1)} %slice.57), channel_id=1, source_target_pairs={{0,2},{1,3},{2,0},{3,1},{4,6},{5,7},{6,4},{7,5},{8,10},{9,11},{10,... | collective-permute-start | bytes 688136 | tf_op jit(solution)/shard_map/ppermute | solution.py:258
  72.3 4.7 %collective-permute-start.9 = (bf16[4,96,128]{2,1,0:T(8,128)(2,1)S(1)}, bf16[4,96,128]{2,1,0:T(8,128)(2,1)S(1)}, u32[]{:S(2)}, u32[]{:S(2)}) collective-permute-start(bf16[4,96,128]{2,1,0:T(8,128)(2,1)S(1)} %slice.63), channel_id=1, source_target_pairs={{0,2},{1,3},{2,0},{3,1},{4,6},{5,7},{6,4},{7,5},{8,10},{9,11},{10,... | collective-permute-start | bytes 294920 | tf_op jit(solution)/shard_map/ppermute | solution.py:258
  74.8 33.2 %copy-start.12 = (bf16[256,512]{1,0:T(8,128)(2,1)S(1)}, bf16[256,512]{1,0:T(8,128)(2,1)}, u32[]{:S(2)}) copy-start(bf16[256,512]{1,0:T(8,128)(2,1)} %copy-done.10) | copy-start | bytes 786436
  74.8 4.9 %collective-permute-start.6 = (bf16[4,112,128]{2,1,0:T(8,128)(2,1)S(1)}, bf16[4,112,128]{2,1,0:T(8,128)(2,1)S(1)}, u32[]{:S(2)}, u32[]{:S(2)}) collective-permute-start(bf16[4,112,128]{2,1,0:T(8,128)(2,1)S(1)} %slice.59), channel_id=1, source_target_pairs={{0,4},{4,0},{8,12},{12,8},{16,20},{20,16},{24,28},{28,24},{1,5},{5... | collective-permute-start | bytes 344072 | tf_op jit(solution)/shard_map/ppermute | solution.py:258
  79.7 4.5 %collective-permute-start.10 = (bf16[208,128]{1,0:T(8,128)(2,1)S(1)}, bf16[208,128]{1,0:T(8,128)(2,1)S(1)}, u32[]{:S(2)}, u32[]{:S(2)}) collective-permute-start(bf16[208,128]{1,0:T(8,128)(2,1)S(1)} %get-tuple-element.47), channel_id=1, source_target_pairs={{0,8},{4,12},{8,0},{12,4},{16,24},{20,28},{24,16},{28,20},{1,9},{5... | collective-permute-start | bytes 159752 | tf_op jit(solution)/shard_map/ppermute | solution.py:258
  81.1 5.9 %collective-permute-start.12 = (bf16[208,128]{1,0:T(8,128)(2,1)S(1)}, bf16[208,128]{1,0:T(8,128)(2,1)S(1)}, u32[]{:S(2)}, u32[]{:S(2)}) collective-permute-start(bf16[208,128]{1,0:T(8,128)(2,1)S(1)} %get-tuple-element.48), channel_id=1, source_target_pairs={{0,24},{4,28},{8,16},{12,20},{16,8},{20,12},{24,0},{28,4},{1,25},{... | collective-permute-start | bytes 159752 | tf_op jit(solution)/shard_map/ppermute | solution.py:258
  83.5 5.8 %collective-permute-start.11 = (bf16[208,128]{1,0:T(8,128)(2,1)S(1)}, bf16[208,128]{1,0:T(8,128)(2,1)S(1)}, u32[]{:S(2)}, u32[]{:S(2)}) collective-permute-start(bf16[208,128]{1,0:T(8,128)(2,1)S(1)} %get-tuple-element.49), channel_id=1, source_target_pairs={{0,16},{4,20},{8,24},{12,28},{16,0},{20,4},{24,8},{28,12},{1,17},{... | collective-permute-start | bytes 159752 | tf_op jit(solution)/shard_map/ppermute | solution.py:258
  89.3 6.0 %collective-permute-start.15 = (bf16[208,128]{1,0:T(8,128)(2,1)S(1)}, bf16[208,128]{1,0:T(8,128)(2,1)S(1)}, u32[]{:S(2)}, u32[]{:S(2)}) collective-permute-start(bf16[208,128]{1,0:T(8,128)(2,1)S(1)} %fusion.2), channel_id=1, source_target_pairs={{0,24},{4,28},{8,16},{12,20},{16,8},{20,12},{24,0},{28,4},{1,25},{... | collective-permute-start | bytes 159752 | tf_op jit(solution)/shard_map/ppermute | solution.py:258
  91.2 5.2 %collective-permute-start.14 = (bf16[208,128]{1,0:T(8,128)(2,1)S(1)}, bf16[208,128]{1,0:T(8,128)(2,1)S(1)}, u32[]{:S(2)}, u32[]{:S(2)}) collective-permute-start(bf16[208,128]{1,0:T(8,128)(2,1)S(1)} %fusion.2), channel_id=1, source_target_pairs={{0,16},{4,20},{8,24},{12,28},{16,0},{20,4},{24,8},{28,12},{1,17},{... | collective-permute-start | bytes 159752 | tf_op jit(solution)/shard_map/ppermute | solution.py:258
  91.2 5.2 %collective-permute-start.13 = (bf16[208,128]{1,0:T(8,128)(2,1)S(1)}, bf16[208,128]{1,0:T(8,128)(2,1)S(1)}, u32[]{:S(2)}, u32[]{:S(2)}) collective-permute-start(bf16[208,128]{1,0:T(8,128)(2,1)S(1)} %fusion.2), channel_id=1, source_target_pairs={{0,8},{4,12},{8,0},{12,4},{16,24},{20,28},{24,16},{28,20},{1,9},{5... | collective-permute-start | bytes 159752 | tf_op jit(solution)/shard_map/ppermute | solution.py:258
  96.5 6.0 %collective-permute-start.16 = (bf16[4,112,128]{2,1,0:T(8,128)(2,1)S(1)}, bf16[4,112,128]{2,1,0:T(8,128)(2,1)S(1)}, u32[]{:S(2)}, u32[]{:S(2)}) collective-permute-start(bf16[4,112,128]{2,1,0:T(8,128)(2,1)S(1)} %slice.70), channel_id=1, source_target_pairs={{0,4},{4,0},{8,12},{12,8},{16,20},{20,16},{24,28},{28,24},{1,5},{5... | collective-permute-start | bytes 344072 | tf_op jit(solution)/shard_map/ppermute | solution.py:258
  97.9 7.4 %collective-permute-start.19 = (bf16[4,96,128]{2,1,0:T(8,128)(2,1)S(1)}, bf16[4,96,128]{2,1,0:T(8,128)(2,1)S(1)}, u32[]{:S(2)}, u32[]{:S(2)}) collective-permute-start(bf16[4,96,128]{2,1,0:T(8,128)(2,1)S(1)} %pad_maximum_fusion.5), channel_id=1, source_target_pairs={{0,2},{1,3},{2,0},{3,1},{4,6},{5,7},{6,4},{7,5},{8,10},{9,11},{10,... | collective-permute-start | bytes 294920 | tf_op jit(solution)/shard_map/ppermute | solution.py:258
  102.5 8.7 %collective-permute-start.17 = (bf16[8,112,128]{2,1,0:T(8,128)(2,1)S(1)}, bf16[8,112,128]{2,1,0:T(8,128)(2,1)S(1)}, u32[]{:S(2)}, u32[]{:S(2)}) collective-permute-start(bf16[8,112,128]{2,1,0:T(8,128)(2,1)S(1)} %pad_maximum_fusion.2), channel_id=1, source_target_pairs={{0,2},{1,3},{2,0},{3,1},{4,6},{5,7},{6,4},{7,5},{8,10},{9,11},{10,... | collective-permute-start | bytes 688136 | tf_op jit(solution)/shard_map/ppermute | solution.py:258
  105.3 6.3 %collective-permute-start.20 = (bf16[8,96,128]{2,1,0:T(8,128)(2,1)S(1)}, bf16[8,96,128]{2,1,0:T(8,128)(2,1)S(1)}, u32[]{:S(2)}, u32[]{:S(2)}) collective-permute-start(bf16[8,96,128]{2,1,0:T(8,128)(2,1)S(1)} %pad_maximum_fusion.4), channel_id=1, source_target_pairs={{0,4},{4,0},{8,12},{12,8},{16,20},{20,16},{24,28},{28,24},{1,5},{5... | collective-permute-start | bytes 589832 | tf_op jit(solution)/shard_map/ppermute | solution.py:258
  109.2 6.4 %collective-permute-start.22 = (bf16[256,512]{1,0:T(8,128)(2,1)S(1)}, bf16[256,512]{1,0:T(8,128)(2,1)S(1)}, u32[]{:S(2)}, u32[]{:S(2)}) collective-permute-start(bf16[256,512]{1,0:T(8,128)(2,1)S(1)} %get-tuple-element.43), channel_id=1, source_target_pairs={{0,28},{4,0},{8,4},{12,8},{16,12},{20,16},{24,20},{28,24},{1,29},{... | collective-permute-start | bytes 786440 | tf_op jit(solution)/shard_map/ppermute | solution.py:254
  109.2 9.2 %collective-permute-start.23 = (bf16[256,512]{1,0:T(8,128)(2,1)S(1)}, bf16[256,512]{1,0:T(8,128)(2,1)S(1)}, u32[]{:S(2)}, u32[]{:S(2)}) collective-permute-start(bf16[256,512]{1,0:T(8,128)(2,1)S(1)} %get-tuple-element.44), channel_id=1, source_target_pairs={{0,4},{4,8},{8,12},{12,16},{16,20},{20,24},{24,28},{28,0},{1,5},{5... | collective-permute-start | bytes 786440 | tf_op jit(solution)/shard_map/ppermute | solution.py:254
  111.3 7.9 %collective-permute-start.18 = (bf16[16,112,128]{2,1,0:T(8,128)(2,1)S(1)}, bf16[16,112,128]{2,1,0:T(8,128)(2,1)S(1)}, u32[]{:S(2)}, u32[]{:S(2)}) collective-permute-start(bf16[16,112,128]{2,1,0:T(8,128)(2,1)S(1)} %pad_maximum_fusion.a0_ref), channel_id=1, source_target_pairs={{0,1},{1,0},{2,3},{3,2},{4,5},{5,4},{6,7},{7,6},{8,9},{9,8},{10,11... | collective-permute-start | bytes 1376264 | tf_op jit(solution)/shard_map/ppermute | solution.py:258
  111.7 7.5 %collective-permute-start.21 = (bf16[16,96,128]{2,1,0:T(8,128)(2,1)S(1)}, bf16[16,96,128]{2,1,0:T(8,128)(2,1)S(1)}, u32[]{:S(2)}, u32[]{:S(2)}) collective-permute-start(bf16[16,96,128]{2,1,0:T(8,128)(2,1)S(1)} %pad_maximum_fusion.1.b0_ref), channel_id=1, source_target_pairs={{0,1},{1,0},{2,3},{3,2},{4,5},{5,4},{6,7},{7,6},{8,9},{9,8},{10,11... | collective-permute-start | bytes 1179656 | tf_op jit(solution)/shard_map/ppermute | solution.py:258

commit v2 on v1

v2 whole, which is shorter than its diff:
```python
import functools

import jax
import jax.numpy as jnp
from jax import lax
from jax.experimental import pallas as pl
from jax.experimental.pallas import tpu as pltpu
from jax.sharding import PartitionSpec as P

H = 8
NEG_FILL = -1e30
SHARDS = 32
ABSENT = 1000.0
VMEM_BYTES = 60 << 20
BF = jnp.bfloat16
F32 = jnp.float32


def nn(a, b):
    return lax.dot_general(a, b, (((1,), (0,)), ((), ())), preferred_element_type=F32)


def nt(a, b):
    return lax.dot_general(a, b, (((1,), (1,)), ((), ())), preferred_element_type=F32)


def tn(a, b):
    return lax.dot_general(a, b, (((0,), (0,)), ((), ())), preferred_element_type=F32)


def lane_half(pair, half):
    lane = lax.broadcasted_iota(jnp.int32, pair.shape, 1)
    width = pair.shape[1] // 2
    keep = lane < width if half == 0 else lane >= width
    return jnp.where(keep, pair, jnp.zeros_like(pair))


def both_heads(pair):
    return jnp.concatenate([lane_half(pair, 0), lane_half(pair, 1)], axis=0)


def own_row_ok(counts_ref, blocks, block_rows, shape):
    row = lax.broadcasted_iota(jnp.int32, shape, 0)
    limit = jnp.full(shape, counts_ref[0], jnp.int32)
    for b in range(1, blocks):
        limit = jnp.where(row < b * block_rows, limit, b * block_rows + counts_ref[b])
    return row < limit


def loader(srcs, dsts, sems):
    copies = [pltpu.make_async_copy(src, dst, sems.at[i]) for i, (src, dst) in enumerate(zip(srcs, dsts))]
    for copy in copies:
        copy.start()

    def ready(*which):
        for i in which:
            copies[i].wait()

    return ready


class Writer:
    def __init__(self, sems, base):
        self.sems, self.base, self.copies = sems, base, []

    def send(self, src, dst):
        copy = pltpu.make_async_copy(src, dst, self.sems.at[self.base + len(self.copies)])
        copy.start()
        self.copies.append(copy)

    def finish(self):
        for copy in self.copies:
            copy.wait()


def place():
    loop_here, lane_here = lax.axis_index("loop"), lax.axis_index("dp")
    core, x_at = lane_here & 1, (lane_here >> 1) & 1
    y_at, z_at = loop_here & 1, (loop_here >> 1) & 3
    return core * 16 + x_at * 8 + y_at * 4 + z_at


def project_kernel(blocks, block_rows, score_scale, counts_h, x_h, w_h, vs_h, vcot_h,
                   q_h, k_h, v_h, virt_h, stats_h, x_ref, w_ref, vs_ref, vcot_ref, q_s, k_s, v_s, virt_s, stats_s, counts_ref, sems):
    ready = loader((x_h, w_h.at[1], w_h.at[2], vs_h, w_h.at[0], vcot_h, counts_h),
                   (x_ref, w_ref.at[1], w_ref.at[2], vs_ref, w_ref.at[0], vcot_ref, counts_ref), sems)
    out = Writer(sems, 7)
    ready(0, 1, 2)
    x = x_ref[...]
    k = nn(x, w_ref[1]).astype(BF)
    v = nn(x, w_ref[2]).astype(BF)
    k_s[...] = k
    v_s[...] = v
    out.send(k_s, k_h)
    out.send(v_s, v_h)
    ready(3, 4, 5, 6)
    virt_q = nn(vs_ref[...], w_ref[0]).astype(BF)
    virt_s[0] = virt_q
    virt_s[1] = nn(vs_ref[...], w_ref[1]).astype(BF)
    virt_s[2] = nn(vs_ref[...], w_ref[2]).astype(BF)
    out.send(virt_s, virt_h)
    virt_q = virt_q * score_scale
    n, width = x.shape
    ok = own_row_ok(counts_ref, blocks, block_rows, (n, 128))
    peaks, totals, deltas = [], [], []
    for c in range(0, width, 128):
        scores = nt(k[:, c:c + 128], both_heads(virt_q[:, c:c + 128]))
        scores = jnp.where(ok, scores, NEG_FILL)
        peak = jnp.max(scores, axis=0, keepdims=True)
        e = jnp.where(ok, jnp.exp(scores - peak), 0.0)
        dw = nt(v[:, c:c + 128], both_heads(vcot_ref[:, c:c + 128]))
        peaks.append(peak)
        totals.append(jnp.sum(e, axis=0, keepdims=True))
        deltas.append(jnp.sum(e * dw, axis=0, keepdims=True))
    rows = jnp.concatenate(peaks + totals + deltas + peaks, axis=0)
    stats_s[...] = jnp.broadcast_to(rows[None], stats_s.shape)
    out.send(stats_s, stats_h)
    q_s[...] = nn(x, w_ref[0]).astype(BF) * score_scale
    out.send(q_s, q_h)
    out.finish()


def attention_kernel(blocks, block_rows, score_scale, pat_h, co_h, xl_h, xr_h,
                     w_h, q_h, k_h, v_h, g_h, virt_h,
                     out_h, dq_h, left_h, right_h, dkn_h, dvn_h, dko_h, dvo_h,
                     xl_ref, xr_ref, w_ref, q_ref, g_ref,
                     key_s, val_s, bias_s, ot_s, dqt_s, out_s, dq_s, dkn_s, dvn_s, dko_s, dvo_s, left_s, right_s, pat_ref, co_ref, sems):
    n, width = q_ref.shape
    virtual_rows = virt_h.shape[1]
    loop_here, loop_size, lanes = lax.axis_index("loop"), lax.axis_size("loop"), lax.axis_size("dp")
    own, virt = pl.ds(n, n), pl.ds(3 * n, virtual_rows)
    ready = loader((xl_h, xr_h, w_h.at[1], w_h.at[2], k_h, v_h, virt_h.at[1], virt_h.at[2], q_h, g_h, pat_h, co_h),
                   (xl_ref, xr_ref, w_ref.at[0], w_ref.at[1], key_s.at[own], val_s.at[own],
                    key_s.at[virt], val_s.at[virt], q_ref, g_ref, pat_ref, co_ref), sems)
    out = Writer(sems, 12)
    row = lax.broadcasted_iota(jnp.int32, (block_rows, block_rows), 0)
    bias_s[3 * n:3 * n + virtual_rows, :] = jnp.zeros((virtual_rows, n), F32)
    ready(0, 1, 10, 11)
    for i in range(blocks):
        slots = []
        for j in range(pat_ref.shape[1]):
            block = pat_ref[i, j]
            ring_at = (block // blocks) // lanes
            offset = lax.rem(ring_at - loop_here + 1 + 2 * loop_size, loop_size)
            slots.append(offset * blocks + lax.rem(block, blocks))
        for b in range(3 * blocks):
            listed = slots[0] == b
            for s in slots[1:]:
                listed = jnp.logical_or(listed, s == b)
            at, inner = b // blocks, b % blocks
            if at == 1:
                okb = row < jnp.where(listed, co_ref[inner], 0)
            else:
                x_ref = (xl_ref, None, xr_ref)[at]
                mark = x_ref[inner * block_rows:(inner + 1) * block_rows, 0:128].astype(F32)[:, 0:1]
                okb = jnp.broadcast_to(mark, (block_rows, block_rows)) < jnp.where(listed, 0.5 * ABSENT, -ABSENT)
            bias_s[b * block_rows:(b + 1) * block_rows, i * block_rows:(i + 1) * block_rows] = jnp.where(
                okb, 0.0, NEG_FILL)
    ready(2, 3)
    for at, ref in ((0, xl_ref), (2, xr_ref)):
        x = ref[...]
        key_s[at * n:(at + 1) * n, :] = nn(x, w_ref[0]).astype(BF)
        val_s[at * n:(at + 1) * n, :] = nn(x, w_ref[1]).astype(BF)
    ready(4, 5, 6, 7, 8, 9)
    ok = own_row_ok(co_ref, blocks, block_rows, (n, 128))
    for c in range(0, width, 128):
        k_pair, v_pair = key_s[:, c:c + 128], val_s[:, c:c + 128]
        q_pair = q_ref[:, c:c + 128]
        g_pair = jnp.where(ok, g_ref[:, c:c + 128], jnp.zeros((n, 128), BF))
        dk_pair = dv_pair = None
        for half in range(2):
            qm, gm = lane_half(q_pair, half), lane_half(g_pair, half)
            s = nt(k_pair, qm) + bias_s[...]
            e = jnp.exp(s - jnp.max(s, axis=0, keepdims=True))
            a = e * (1.0 / jnp.sum(e, axis=0, keepdims=True))
            wt = a.astype(BF)
            dw = nt(v_pair, gm)
            delta = jnp.sum(a * dw, axis=0, keepdims=True)
            ds = (a * (dw - delta)).astype(BF)
            at = c + half * 64
            ot_s[at:at + 64, :] = tn(v_pair, wt)[half * 64:half * 64 + 64]
            dqt_s[at:at + 64, :] = tn(k_pair, ds)[half * 64:half * 64 + 64]
            dk, dv = nn(ds, qm), nn(wt, gm)
            dk_pair = dk if dk_pair is None else dk_pair + dk
            dv_pair = dv if dv_pair is None else dv_pair + dv
        for near, mine, part in ((dkn_s, dko_s, dk_pair), (dvn_s, dvo_s, dv_pair)):
            near[0:n, c:c + 128] = part[0:n].astype(BF)
            near[n:2 * n, c:c + 128] = part[2 * n:3 * n].astype(BF)
            mine[0:n, c:c + 128] = part[n:2 * n]
            mine[n:n + virtual_rows, c:c + 128] = part[3 * n:3 * n + virtual_rows]
    for rows, ref, dst in ((slice(0, n), left_s, left_h), (slice(n, 2 * n), right_s, right_h)):
        ref[...] = (nt(dkn_s[rows, :], w_ref[0]) + nt(dvn_s[rows, :], w_ref[1])).astype(BF)
        out.send(ref, dst)
    out.send(dkn_s, dkn_h)
    out.send(dvn_s, dvn_h)
    out.send(dko_s, dko_h)
    out.send(dvo_s, dvo_h)
    dq_s[...] = (dqt_s[...].T * score_scale).astype(BF)
    out.send(dq_s, dq_h)
    okw = own_row_ok(co_ref, blocks, block_rows, (n, width))
    out_s[...] = jnp.where(okw, ot_s[...].T, 0.0).astype(BF)
    out.send(out_s, out_h)
    out.finish()


def weight_kernel(blocks, block_rows, score_scale, counts_h, x_h, xl_h, xr_h, vs_h, vcot_h, w_h,
                  k_h, v_h, virt_h, stats_h, dq_h, dkn_h, dvn_h, dko_h, dvo_h,
                  keep_h, send_h, kown_h, vown_h,
                  xs_ref, vs_ref, vcot_ref, w_ref, k_ref, v_ref, virt_ref, stats_ref, dq_ref, dk_ref, dv_ref,
                  keep_s, send_s, wg_s, vg_s, vo_s, vgrad_s, dkw_s, dvw_s, counts_ref, sems):
    n, width = x_h.shape
    virtual_rows = vs_ref.shape[0]
    low, own, high = pl.ds(0, n), pl.ds(n, n), pl.ds(2 * n, n)
    ready = loader((stats_h, k_h, v_h, virt_h.at[0], vcot_h, dko_h, dvo_h, dq_h,
                    x_h, xl_h, xr_h, vs_h, w_h, counts_h, dkn_h.at[low], dkn_h.at[own], dvn_h.at[low], dvn_h.at[own]),
                   (stats_ref, k_ref, v_ref, virt_ref, vcot_ref, dk_ref, dv_ref, dq_ref,
                    xs_ref.at[own], xs_ref.at[low], xs_ref.at[high], vs_ref, w_ref, counts_ref,
                    dkw_s.at[low], dkw_s.at[high], dvw_s.at[low], dvw_s.at[high]), sems)
    out = Writer(sems, 18)
    pairs = width // 128
    ready(0, 13)
    ok = own_row_ok(counts_ref, blocks, block_rows, (n, 128))
    stats = stats_ref[...]
    peak = jnp.max(stats[:, 0:pairs], axis=0)
    factor = jnp.exp(stats[:, 0:pairs] - peak[None])
    total = jnp.sum(stats[:, pairs:2 * pairs] * factor, axis=0)
    delta = jnp.sum(stats[:, 2 * pairs:3 * pairs] * factor, axis=0) / total
    inv_total = 1.0 / total
    lane_low = lax.broadcasted_iota(jnp.int32, (virtual_rows, 128), 1) < 64

    def diagonal(square):
        return jnp.where(lane_low, square[:virtual_rows], square[virtual_rows:])

    ready(1, 2, 3, 4, 5, 6)
    for p in range(pairs):
        c = p * 128
        k_pair, v_pair = k_ref[:, c:c + 128], v_ref[:, c:c + 128]
        vq = both_heads(virt_ref[:, c:c + 128])
        vcot = both_heads(vcot_ref[:, c:c + 128])
        scores = jnp.where(ok, nt(k_pair, vq * score_scale), NEG_FILL)
        attn = jnp.exp(scores - peak[p:p + 1]) * inv_total[p:p + 1]
        attn_hi = attn.astype(BF)
        attn_lo = (attn - attn_hi.astype(F32)).astype(BF)
        dw = nt(v_pair, vcot)
        ds = (attn * (dw - delta[p:p + 1]) * score_scale).astype(BF)
        vo_s[:, c:c + 128] = diagonal(tn(attn_hi, v_pair) + tn(attn_lo, v_pair))
        vgrad_s[0, :, c:c + 128] = diagonal(tn(ds, k_pair))
        dkw_s[n:2 * n, c:c + 128] = (dk_ref[0:n, c:c + 128] + nn(ds, vq)).astype(BF)
        dvw_s[n:2 * n, c:c + 128] = (dv_ref[0:n, c:c + 128] + nn(attn_hi, vcot)).astype(BF)
    out.send(dkw_s.at[own], kown_h)
    out.send(dvw_s.at[own], vown_h)
    vgrad_s[1] = dk_ref[n:n + virtual_rows, :]
    vgrad_s[2] = dv_ref[n:n + virtual_rows, :]
    ready(7, 8, 9, 10, 11, 12, 14, 15, 16, 17)
    vs = vs_ref[...]
    vg = None
    for t in range(3):
        part = vgrad_s[t]
        hi = part.astype(BF)
        lo = (part - hi.astype(F32)).astype(BF)
        if t == 0:
            wg = tn(xs_ref[n:2 * n, :], dq_ref[...])
        else:
            wg = tn(xs_ref[...], (dkw_s if t == 1 else dvw_s)[...])
        wg_s[t] = wg + (tn(vs, hi) + tn(vs, lo))
        back = nt(hi, w_ref[t]) + nt(lo, w_ref[t])
        vg = back if vg is None else vg + back
    vg_s[...] = vg
    row_groups = width // 64
    me = place()
    for half, ref, dst in ((1, send_s, send_h), (0, keep_s, keep_h)):
        for at in range(SHARDS // 2):
            shard = jnp.bitwise_xor(me, half * (SHARDS // 2) + at)
            cols = pl.ds(pl.multiple_of((shard // row_groups) * 128, 128), 128)
            group = lax.rem(shard, row_groups)
            for t in range(3):
                rows = pl.ds(pl.multiple_of(group * 64, 64), 64)
                ref[at, t * 64:(t + 1) * 64, :] = wg_s[t, rows, cols].astype(BF)
            rows = pl.ds(pl.multiple_of(group * 8, 8), 8)
            ref[at, 192:208, :] = jnp.concatenate([vg_s[rows, cols], vo_s[rows, cols]], axis=0).astype(BF)
        out.send(ref, dst)
    out.finish()


def node_kernel(w_h, dq_h, dk_h, dv_h, from_right_h, from_left_h, grad_h,
                w_ref, dq_ref, dk_ref, dv_ref, from_right, from_left, grad_s, sems):
    ready = loader((w_h, dq_h, dk_h, dv_h, from_right_h, from_left_h),
                   (w_ref, dq_ref, dk_ref, dv_ref, from_right, from_left), sems)
    out = Writer(sems, 6)
    ready(0, 1, 2, 3)
    part = nt(dq_ref[...], w_ref[0]) + nt(dk_ref[...], w_ref[1]) + nt(dv_ref[...], w_ref[2])
    ready(4, 5)
    grad_s[...] = (part + from_right[...].astype(F32) + from_left[...].astype(F32)).astype(BF)
    out.send(grad_s, grad_h)
    out.finish()


def unpack_kernel(p0_h, p1_h, wg_h, vg_h, vo_h, p0_ref, p1_ref, wg_s, vg_s, vo_s, vgb_s, vob_s, sems):
    width = wg_s.shape[2]
    row_groups = width // 64
    ready = loader((p0_h, p1_h), (p0_ref, p1_ref), sems)
    out = Writer(sems, 2)
    ready(0, 1)
    me = place()
    for t in range(3):
        for p in range(SHARDS):
            ref, at = (p0_ref, p1_ref)[p // (SHARDS // 2)], p % (SHARDS // 2)
            shard = jnp.bitwise_xor(me, p)
            cols = pl.ds(pl.multiple_of((shard // row_groups) * 128, 128), 128)
            group = lax.rem(shard, row_groups)
            rows = pl.ds(pl.multiple_of(group * 64, 64), 64)
            wg_s[t, rows, cols] = ref[at, t * 64:(t + 1) * 64, :].astype(F32)
            if t == 0:
                rows = pl.ds(pl.multiple_of(group * 8, 8), 8)
                both = ref[at, 192:208, :].astype(F32)
                vg_s[rows, cols] = both[0:8]
                vo_s[rows, cols] = both[8:16]
        out.send(wg_s.at[t], wg_h.at[t])
    vgb_s[...] = vg_s[...].astype(BF)
    vob_s[...] = vo_s[...].astype(BF)
    out.send(vgb_s, vg_h)
    out.send(vob_s, vo_h)
    out.finish()


ANY = pl.BlockSpec(memory_space=pl.ANY)


def call(body, args, outs, scratch, sems, flops=1e8, name=None, vmem=VMEM_BYTES):
    return pl.pallas_call(
        body,
        out_shape=[jax.ShapeDtypeStruct(s, d) for s, d in outs],
        in_specs=[ANY] * len(args),
        out_specs=[ANY] * len(outs),
        scratch_shapes=[pltpu.SMEM(s, d) if d == jnp.int32 else pltpu.VMEM(s, d) for s, d in scratch] + [pltpu.SemaphoreType.DMA((sems,))],
        compiler_params=pltpu.CompilerParams(vmem_limit_bytes=vmem),
        cost_estimate=pl.CostEstimate(flops=int(flops), bytes_accessed=4 << 20, transcendentals=0),
        name=name,
    )(*args)


def ring(value, steps):
    count = lax.axis_size("loop")
    return lax.ppermute(value, "loop", [(s, (s + steps) % count) for s in range(count)])


def swap(value, loop_bits, lane_bits):
    lanes = lax.axis_size("dp")
    count = lax.axis_size("loop") * lanes
    other = loop_bits * lanes + lane_bits
    return lax.ppermute(value, ("loop", "dp"), [(s, s ^ other) for s in range(count)])


def together(tree):
    return lax.optimization_barrier(tree)


PLANE = ((1, 2), (0, 2), (1, 0))
LINE = ((6, 0), (4, 0), (2, 0))


def total(parts):
    summed = parts[0].astype(F32)
    for part in parts[1:]:
        summed = summed + part.astype(F32)
    return summed.astype(BF)


def reduce_all(keep, send, node_step, middle):
    loop_size = lax.axis_size("loop")
    held = total([keep, swap(send, 0, 1)])
    held, middle = together((held, middle))
    quarters = [held[4 * j:4 * j + 4] for j in range(4)]
    got = [swap(quarters[3 - j], *bits) for j, bits in enumerate(PLANE)]
    got, middle = together((got, node_step(*middle)))
    held = together(total([quarters[0]] + got))
    got = together([swap(held[3 - j], *bits) for j, bits in enumerate(LINE)])
    piece = total([held[0]] + got)
    bit = 8
    while bit < loop_size:
        piece = total([piece, swap(piece, bit, 0)])
        bit *= 2
    piece = together(piece)
    got = together([swap(piece, *bits) for bits in LINE])
    held = together(jnp.stack([piece] + got[::-1]))
    got = together([swap(held, *bits) for bits in PLANE])
    held = together(jnp.concatenate([held] + got[::-1], axis=0))
    return held, swap(held, 0, 1), middle


def local(node_states, virtual_states, projection, pattern, valid_counts, node_cotangent, virtual_cotangent):
    n, width = node_states.shape
    blocks = pattern.shape[0]
    block_rows = n // blocks
    virtual_rows = virtual_states.shape[0]
    loop_size, lanes = lax.axis_size("loop"), lax.axis_size("dp")
    devices = loop_size * lanes
    score_scale = (width // H) ** -0.5
    keys = 3 * n + virtual_rows

    shape = (blocks, block_rows, width)
    valid = lax.broadcasted_iota(jnp.int32, shape, 1) < lax.broadcast_in_dim(valid_counts, shape, (0,))
    marked = jnp.where(valid, node_states.reshape(shape), jnp.asarray(ABSENT, BF)).reshape(n, width)
    x_left, x_right = ring(marked, 1), ring(marked, -1)

    counts_i, pattern_i = ((blocks,), jnp.int32), (pattern.shape, jnp.int32)
    rows_bf, rows_f = ((n, width), BF), ((n, width), F32)
    wide = ((3, width, width), BF)
    virt_bf, virt_f = ((virtual_rows, width), BF), ((virtual_rows, width), F32)
    triple = ((3, virtual_rows, width), BF)
    stats_f = ((devices, 16, 128), F32)
    q, k, v, virt, stats = call(
        functools.partial(project_kernel, blocks, block_rows, score_scale),
        (valid_counts, node_states, projection, virtual_states, virtual_cotangent),
        [rows_bf] * 3 + [triple, stats_f],
        [rows_bf, wide, virt_bf, virt_bf] + [rows_bf] * 3 + [triple, stats_f, counts_i], 12, name="project")
    stats = lax.all_to_all(stats, ("loop", "dp"), 0, 0, tiled=True)

    keys_bf = ((keys, width), BF)
    across = ((width, n), F32)
    near_bf, mine_f = ((2 * n, width), BF), ((n + virtual_rows, width), F32)
    node_out, dq, to_left, to_right, dkn, dvn, dko, dvo = call(
        functools.partial(attention_kernel, blocks, block_rows, score_scale),
        (pattern, valid_counts, x_left, x_right, projection, q, k, v, node_cotangent, virt),
        [rows_bf] * 4 + [near_bf] * 2 + [mine_f] * 2,
        [rows_bf] * 2 + [((2, width, width), BF)] + [rows_bf] * 2
        + [keys_bf] * 2 + [((keys, n), F32), across, across] + [rows_bf] * 2 + [near_bf] * 2 + [mine_f] * 2 + [rows_bf] * 2
        + [pattern_i, counts_i], 20,
        flops=4e9, name="attention")
    from_right, from_left = ring(to_left, -1), ring(to_right, 1)

    window_bf = ((3 * n, width), BF)
    half = ((SHARDS // 2, 3 * 64 + 16, 128), BF)
    keep, send, dk, dv = call(
        functools.partial(weight_kernel, blocks, block_rows, score_scale),
        (valid_counts, node_states, x_left, x_right, virtual_states, virtual_cotangent, projection, k, v, virt, stats,
         dq, dkn, dvn, dko, dvo),
        [half] * 2 + [rows_bf] * 2,
        [window_bf, virt_bf, virt_bf, wide, rows_bf, rows_bf, virt_bf, stats_f, rows_bf, mine_f, mine_f]
        + [half] * 2 + [((3, width, width), F32), virt_f, virt_f, ((3, virtual_rows, width), F32), window_bf, window_bf, counts_i], 24,
        flops=8e9, name="weight_grads")
    def node_step(*args):
        return call(node_kernel, args, [rows_bf], [wide] + [rows_bf] * 6, 7, flops=1e9, name="node_grads")[0]

    send, from_right, from_left = together((send, from_right, from_left))
    mine, other, node_grad = reduce_all(keep, send, node_step, (projection, dq, dk, dv, from_right, from_left))
    weight_grads, virtual_grad, virtual_out = call(
        unpack_kernel, (mine, other), [((3, width, width), F32), virt_bf, virt_bf],
        [half, half, ((3, width, width), F32), virt_f, virt_f, virt_bf, virt_bf], 7, name="unpack",
        vmem=16 << 20)
    return node_out, virtual_out, node_grad, virtual_grad, weight_grads


def solution(mesh):
    return jax.shard_map(
        local,
        mesh=mesh,
        in_specs=(
            P(("loop", "dp"), None),
            P(),
            P(),
            P(("loop", "dp"), None),
            P(("loop", "dp")),
            P(("loop", "dp"), None),
            P(),
        ),
        out_specs=(P(("loop", "dp"), None), P(), P(("loop", "dp"), None), P(), P()),
        check_vma=False,
    )
```

time: 124 us -> 96.7 us (0.78)
  local copies, waits for them, and re-layouts: 27.5 us -> 1.48 us
  starting transfers between devices: 42.2 us -> 31.8 us
  Pallas kernels: 22 us -> 29 us
  waiting for transfers between devices: 27.9 us -> 29.7 us
    unnamed x72 -> x10, local copies, waits for them, and re-layouts: 27.4 us -> 1.42 us
    ppermute x18 -> x14, starting transfers between devices: 23.2 us -> 16.1 us  [swap(): lax.ppermute(value, ('loop', 'dp'), [(s, s ^ other) for s in range(count)])]
    pallas_call x5, Pallas kernels: 22 us -> 29 us  [call(): pl.pallas_call(body, out_shape=[jax.ShapeDtypeStruct(s, d) for s, d in ou...]
    ppermute x18 -> x14, waiting for transfers between devices: 21.4 us -> 25.7 us  [swap(): lax.ppermute(value, ('loop', 'dp'), [(s, s ^ other) for s in range(count)])]
    ppermute x6 -> x4, starting transfers between devices: 12.9 us -> 9.68 us  [ring(): lax.ppermute(value, 'loop', [(s, (s + steps) % count) for s in range(coun...]
    ppermute x6 -> x4, waiting for transfers between devices: 6.42 us -> 3.97 us  [ring(): lax.ppermute(value, 'loop', [(s, (s + steps) % count) for s in range(coun...]
    convert_element_type x10 -> x3, other arithmetic: 2.55 us -> 1.53 us  [total(): return summed.astype(BF)]
  transfers between devices with their start and end apart: 25 -> 19, of which waited for: 14 -> 14; matrix products, arithmetic and copies ran while one was open for 1% -> 0% of each run, Pallas kernels for 11% -> 28%
where the time goes in v2:
time: 96.7 us; the launch traced here: 96.3 us
  starting transfers between devices  31.8 us (33%)
  waiting for transfers between devices  29.7 us (31%)
  Pallas kernels  29 us (30%)
  other arithmetic  3.44 us (4%)
  local copies, waits for them, and re-layouts  1.48 us (2%)
    pallas_call x5, Pallas kernels, call(): pl.pallas_call(body, out_shape=[jax.ShapeDtypeStruct(s, d) for s, d in ou...  29 us
    ppermute x14, waiting for transfers between devices, swap(): lax.ppermute(value, ('loop', 'dp'), [(s, s ^ other) for s in range(count)])  25.7 us
    ppermute x14, starting transfers between devices, swap(): lax.ppermute(value, ('loop', 'dp'), [(s, s ^ other) for s in range(count)])  16.1 us
    ppermute x4, starting transfers between devices, ring(): lax.ppermute(value, 'loop', [(s, (s + steps) % count) for s in range(coun...  9.68 us
    all_to_all x1, starting transfers between devices, local(): stats = lax.all_to_all(stats, ('loop', 'dp'), 0, 0, tiled=True)  6.01 us
    ppermute x4, waiting for transfers between devices, ring(): lax.ppermute(value, 'loop', [(s, (s + steps) % count) for s in range(coun...  3.97 us
  transfers between devices with their start and end apart: 19, of which 14 were waited for; matrix products, arithmetic and copies ran while one was open for 0% of the time, Pallas kernels for 28%

profile of v2, /device:TPU:0, one launch (start us, length us, event | category | flops | bytes accessed | tf_op | source)
XLA Modules:
  0.0 96.3 jit_solution(17192432042644328342)
XLA Ops:
  0.6 0.7 compare_bitcast_fusion
  1.4 1.0 %broadcast_select_fusion = bf16[256,512]{1,0:T(8,128)(2,1)S(1)} fusion(bf16[256,512]{1,0:T(8,128)(2,1)} %x_h.3, pred[256]{0:T(512)(128)(4,1)S(1)} %compare_bitcast_fusion), kind=kLoop, calls=%fused_computation.3 | loop fusion | flops 131072 | bytes 524544 | tf_op jit(solution)/shard_map/jit(_where)/select_n | solution.py:403
  2.4 6.1 %collective-permute-start.1 = (bf16[256,512]{1,0:T(8,128)(2,1)S(1)}, bf16[256,512]{1,0:T(8,128)(2,1)S(1)}, u32[]{:S(2)}, u32[]{:S(2)}) collective-permute-start(bf16[256,512]{1,0:T(8,128)(2,1)S(1)} %broadcast_select_fusion), channel_id=1, source_target_pairs={{0,28},{4,0},{8,4},{12,8},{16,12},{20,16},{24,20},{28,24},{1,29},{... | collective-permute-start | bytes 786440 | tf_op jit(solution)/shard_map/ppermute | solution.py:344
  8.5 0.0 collective-permute-start
  8.5 3.3 %project.1 = (bf16[256,512]{1,0:T(8,128)(2,1)}, bf16[256,512]{1,0:T(8,128)(2,1)}, bf16[256,512]{1,0:T(8,128)(2,1)}, bf16[3,64,512]{2,1,0:T(8,128)(2,1)}, f32[32,16,128]{2,1,0:T(8,128)}) custom-call(s32[2]{0:T(128)} %counts_h.3, bf16[256,512]{1,0:T(8,128)(2,1)} %x_h.3, bf16[3,512,512]{2,1,0:T(8,128)(2,1)} %w_h.6, bf16[64,512]{1,0:T(8,128)(2,1)} %vs_h.3, ...), custom_call_target="tpu_custom_call" | custom-call | flops 100000000 | bytes 4194304 | tf_op jit(solution)/shard_map/project/pallas_call | solution.py:330
  11.8 6.0 %all-to-all-start = ((f32[32,16,128]{2,1,0:T(8,128)}), f32[32,16,128]{2,1,0:T(8,128)S(1)}, u32[]{:S(2)}, u32[]{:S(2)}) async-start(f32[32,16,128]{2,1,0:T(8,128)} %get-tuple-element.53), calls=%async_computation | async-start | bytes 524288 | tf_op jit(solution)/shard_map/all_to_all | solution.py:417
  17.8 0.0 collective-permute-done.1.xr_h
  17.9 0.0 copy-start.3
  17.9 1.1 %collective-permute-done.xl_h = bf16[256,512]{1,0:T(8,128)(2,1)S(1)} collective-permute-done((bf16[256,512]{1,0:T(8,128)(2,1)S(1)}, bf16[256,512]{1,0:T(8,128)(2,1)S(1)}, u32[]{:S(2)}, u32[]{:S(2)}) %collective-permute-start) | collective-permute-done | bytes 262176 | tf_op jit(solution)/shard_map/ppermute | solution.py:344
  18.9 0.0 copy-start.4
  18.9 0.0 copy-done.3
  18.9 0.7 copy-done.4
  19.6 12.9 %attention.1 = (bf16[256,512]{1,0:T(8,128)(2,1)}, bf16[256,512]{1,0:T(8,128)(2,1)}, bf16[256,512]{1,0:T(8,128)(2,1)}, bf16[256,512]{1,0:T(8,128)(2,1)}, bf16[512...) custom-call(s32[2,5]{1,0:T(2,128)} %pat_h.1, s32[2]{0:T(128)} %counts_h.3, ...), custom_call_target="tpu_custom_call" | custom-call | flops 4000000000 | bytes 4194304 | tf_op jit(solution)/shard_map/attention/pallas_call | solution.py:330
  32.6 3.6 %collective-permute-start.2 = (bf16[256,512]{1,0:T(8,128)(2,1)}, bf16[256,512]{1,0:T(8,128)(2,1)S(1)}, u32[]{:S(2)}, u32[]{:S(2)}) collective-permute-start(bf16[256,512]{1,0:T(8,128)(2,1)} %get-tuple-element.61), channel_id=1, source_target_pairs={{0,28},{4,0},{8,4},{12,8},{16,12},{20,16},{24,20},{28,24},{1,29},{... | collective-permute-start | bytes 786440 | tf_op jit(solution)/shard_map/ppermute | solution.py:344
  36.2 0.0 collective-permute-start.3
  36.2 0.0 all-to-all-done.stats_h
  36.2 0.0 copy-start
  36.2 0.7 copy-done
  36.9 7.3 %weight_grads.1 = (bf16[16,208,128]{2,1,0:T(8,128)(2,1)}, bf16[16,208,128]{2,1,0:T(8,128)(2,1)}, bf16[256,512]{1,0:T(8,128)(2,1)}, bf16[256,512]{1,0:T(8,128)(2,1)}) custom-call(s32[2]{0:T(128)} %counts_h.3, bf16[256,512]{1,0:T(8,128)(2,1)} %x_h.3, bf16[256,512]{1,0:T(8,128)(2,1)} %copy-done.4, bf16[256,512]{1,0:T(8,128)(2,1)} %copy-done.3, ...), custom_call_target="tpu_custom_call" | custom-call | flops 8000000000 | bytes 4194304 | tf_op jit(solution)/shard_map/weight_grads/pallas_call | solution.py:330
  44.2 0.0 collective-permute-done.2.from_right_h
  44.2 0.0 copy-start.1
  44.3 2.9 %collective-permute-done.3.from_left_h = bf16[256,512]{1,0:T(8,128)(2,1)S(1)} collective-permute-done((bf16[256,512]{1,0:T(8,128)(2,1)}, bf16[256,512]{1,0:T(8,128)(2,1)S(1)}, u32[]{:S(2)}, u32[]{:S(2)}) %collective-permute-start.3) | collective-permute-done | bytes 262176 | tf_op jit(solution)/shard_map/ppermute | solution.py:344
  47.2 0.0 copy-start.2
  47.2 0.0 collective-permute-start.4
  47.2 2.6 %collective-permute-done.4 = bf16[16,208,128]{2,1,0:T(8,128)(2,1)S(1)} collective-permute-done((bf16[16,208,128]{2,1,0:T(8,128)(2,1)}, bf16[16,208,128]{2,1,0:T(8,128)(2,1)S(1)}, u32[]{:S(2)}, u32[]{:S(2)}) %collective-permute-start.4) | collective-permute-done | bytes 852000 | tf_op jit(solution)/shard_map/ppermute | solution.py:351
  49.7 1.4 %add_convert_fusion = bf16[16,208,128]{2,1,0:T(8,128)(2,1)S(1)} fusion(bf16[16,208,128]{2,1,0:T(8,128)(2,1)S(1)} %collective-permute-done.4, bf16[16,208,128]{2,1,0:T(8,128)(2,1)} %get-tuple-element.59), kind=kLoop, calls=%fused_computation | loop fusion | flops 1703936 | bytes 2555904 | tf_op jit(solution)/shard_map/convert_element_type | solution.py:366
  51.2 0.0 copy-done.1
  51.2 0.0 copy-done.2
  51.2 1.5 %collective-permute-start.7 = (bf16[4,208,128]{2,1,0:T(8,128)(2,1)S(1)}, bf16[4,208,128]{2,1,0:T(8,128)(2,1)S(1)}, u32[]{:S(2)}, u32[]{:S(2)}) collective-permute-start(bf16[4,208,128]{2,1,0:T(8,128)(2,1)S(1)} %get-tuple-element.91), channel_id=1, source_target_pairs={{0,4},{1,5},{2,6},{3,7},{4,0},{5,1},{6,2},{7,3},{8,12},{9,13},{10,... | collective-permute-start | bytes 638984 | tf_op jit(solution)/shard_map/ppermute | solution.py:351
  52.7 1.5 %collective-permute-start.6 = (bf16[4,208,128]{2,1,0:T(8,128)(2,1)S(1)}, bf16[4,208,128]{2,1,0:T(8,128)(2,1)S(1)}, u32[]{:S(2)}, u32[]{:S(2)}) collective-permute-start(bf16[4,208,128]{2,1,0:T(8,128)(2,1)S(1)} %get-tuple-element.92), channel_id=1, source_target_pairs={{0,2},{1,3},{2,0},{3,1},{4,6},{5,7},{6,4},{7,5},{8,10},{9,11},{10,... | collective-permute-start | bytes 638984 | tf_op jit(solution)/shard_map/ppermute | solution.py:351
  54.2 0.5 collective-permute-start.5
  54.8 3.0 %node_grads.1 = bf16[256,512]{1,0:T(8,128)(2,1)} custom-call(bf16[3,512,512]{2,1,0:T(8,128)(2,1)} %w_h.6, bf16[256,512]{1,0:T(8,128)(2,1)} %get-tuple-element.70.dq_h, bf16[256,512]{1,0:T(8,128)(2,1)} %get-tuple-element.71.dk_h, bf16[256,512]{1,0:T(8,128)(2,1)} %get-tuple-element.72.dv_h, bf16[256,512]{1,0:T(8,128)(2,1)} %copy-done.1, bf16[256,512]{1,0:T(8,128)(2,1)} %copy-done.2), custom_call_target="tpu_custom_call" | custom-call | flops 1000000000 | bytes 4194304 | tf_op jit(solution)/shard_map/node_grads/pallas_call | solution.py:330
  57.8 0.8 collective-permute-done.7
  58.6 2.3 %collective-permute-done.6 = bf16[4,208,128]{2,1,0:T(8,128)(2,1)S(1)} collective-permute-done((bf16[4,208,128]{2,1,0:T(8,128)(2,1)S(1)}, bf16[4,208,128]{2,1,0:T(8,128)(2,1)S(1)}, u32[]{:S(2)}, u32[]{:S(2)}) %collective-permute-start.6) | collective-permute-done | bytes 213024 | tf_op jit(solution)/shard_map/ppermute | solution.py:351
  60.9 3.4 %collective-permute-done.5 = bf16[4,208,128]{2,1,0:T(8,128)(2,1)S(1)} collective-permute-done((bf16[4,208,128]{2,1,0:T(8,128)(2,1)S(1)}, bf16[4,208,128]{2,1,0:T(8,128)(2,1)S(1)}, u32[]{:S(2)}, u32[]{:S(2)}) %collective-permute-start.5) | collective-permute-done | bytes 213024 | tf_op jit(solution)/shard_map/ppermute | solution.py:351
  64.3 0.1 add_convert_fusion.1
  64.4 0.6 collective-permute-start.10
  65.0 2.4 %collective-permute-start.9 = (bf16[208,128]{1,0:T(8,128)(2,1)S(1)}, bf16[208,128]{1,0:T(8,128)(2,1)S(1)}, u32[]{:S(2)}, u32[]{:S(2)}) collective-permute-start(bf16[208,128]{1,0:T(8,128)(2,1)S(1)} %get-tuple-element.95), channel_id=1, source_target_pairs={{0,16},{1,17},{2,18},{3,19},{4,20},{5,21},{6,22},{7,23},{8,24},{9,... | collective-permute-start | bytes 159752 | tf_op jit(solution)/shard_map/ppermute | solution.py:351
  67.4 1.5 %collective-permute-start.8 = (bf16[208,128]{1,0:T(8,128)(2,1)S(1)}, bf16[208,128]{1,0:T(8,128)(2,1)S(1)}, u32[]{:S(2)}, u32[]{:S(2)}) collective-permute-start(bf16[208,128]{1,0:T(8,128)(2,1)S(1)} %get-tuple-element.96), channel_id=1, source_target_pairs={{0,24},{1,25},{2,26},{3,27},{4,28},{5,29},{6,30},{7,31},{8,16},{9,... | collective-permute-start | bytes 159752 | tf_op jit(solution)/shard_map/ppermute | solution.py:351
  68.9 0.0 collective-permute-done.10
  68.9 1.1 %collective-permute-done.9 = bf16[208,128]{1,0:T(8,128)(2,1)S(1)} collective-permute-done((bf16[208,128]{1,0:T(8,128)(2,1)S(1)}, bf16[208,128]{1,0:T(8,128)(2,1)S(1)}, u32[]{:S(2)}, u32[]{:S(2)}) %collective-permute-start.9) | collective-permute-done | bytes 53280 | tf_op jit(solution)/shard_map/ppermute | solution.py:351
  70.1 3.6 %collective-permute-done.8 = bf16[208,128]{1,0:T(8,128)(2,1)S(1)} collective-permute-done((bf16[208,128]{1,0:T(8,128)(2,1)S(1)}, bf16[208,128]{1,0:T(8,128)(2,1)S(1)}, u32[]{:S(2)}, u32[]{:S(2)}) %collective-permute-start.8) | collective-permute-done | bytes 53280 | tf_op jit(solution)/shard_map/ppermute | solution.py:351
  73.7 0.1 collective-permute-start.13
  73.7 1.8 %collective-permute-start.12 = (bf16[208,128]{1,0:T(8,128)(2,1)S(1)}, bf16[208,128]{1,0:T(8,128)(2,1)S(1)}, u32[]{:S(2)}, u32[]{:S(2)}) collective-permute-start(bf16[208,128]{1,0:T(8,128)(2,1)S(1)} %fusion.2), channel_id=1, source_target_pairs={{0,16},{1,17},{2,18},{3,19},{4,20},{5,21},{6,22},{7,23},{8,24},{9,... | collective-permute-start | bytes 159752 | tf_op jit(solution)/shard_map/ppermute | solution.py:351
  75.5 2.6 %collective-permute-start.11 = (bf16[208,128]{1,0:T(8,128)(2,1)S(1)}, bf16[208,128]{1,0:T(8,128)(2,1)S(1)}, u32[]{:S(2)}, u32[]{:S(2)}) collective-permute-start(bf16[208,128]{1,0:T(8,128)(2,1)S(1)} %fusion.2), channel_id=1, source_target_pairs={{0,24},{1,25},{2,26},{3,27},{4,28},{5,29},{6,30},{7,31},{8,16},{9,... | collective-permute-start | bytes 159752 | tf_op jit(solution)/shard_map/ppermute | solution.py:351
  78.1 0.0 collective-permute-done.13
  78.1 0.7 collective-permute-done.12
  78.8 2.6 %collective-permute-done.11 = bf16[208,128]{1,0:T(8,128)(2,1)S(1)} collective-permute-done((bf16[208,128]{1,0:T(8,128)(2,1)S(1)}, bf16[208,128]{1,0:T(8,128)(2,1)S(1)}, u32[]{:S(2)}, u32[]{:S(2)}) %collective-permute-start.11) | collective-permute-done | bytes 53280 | tf_op jit(solution)/shard_map/ppermute | solution.py:351
  81.5 1.5 %collective-permute-start.16 = (bf16[4,208,128]{2,1,0:T(8,128)(2,1)S(1)}, bf16[4,208,128]{2,1,0:T(8,128)(2,1)S(1)}, u32[]{:S(2)}, u32[]{:S(2)}) collective-permute-start(bf16[4,208,128]{2,1,0:T(8,128)(2,1)S(1)} %pad_maximum_fusion.1), channel_id=1, source_target_pairs={{0,4},{1,5},{2,6},{3,7},{4,0},{5,1},{6,2},{7,3},{8,12},{9,13},{10,... | collective-permute-start | bytes 638984 | tf_op jit(solution)/shard_map/ppermute | solution.py:351
  83.0 1.5 %collective-permute-start.15 = (bf16[4,208,128]{2,1,0:T(8,128)(2,1)S(1)}, bf16[4,208,128]{2,1,0:T(8,128)(2,1)S(1)}, u32[]{:S(2)}, u32[]{:S(2)}) collective-permute-start(bf16[4,208,128]{2,1,0:T(8,128)(2,1)S(1)} %pad_maximum_fusion.1), channel_id=1, source_target_pairs={{0,2},{1,3},{2,0},{3,1},{4,6},{5,7},{6,4},{7,5},{8,10},{9,11},{10,... | collective-permute-start | bytes 638984 | tf_op jit(solution)/shard_map/ppermute | solution.py:351
  84.5 0.5 collective-permute-start.14
  85.0 3.3 %collective-permute-done.16 = bf16[4,208,128]{2,1,0:T(8,128)(2,1)S(1)} collective-permute-done((bf16[4,208,128]{2,1,0:T(8,128)(2,1)S(1)}, bf16[4,208,128]{2,1,0:T(8,128)(2,1)S(1)}, u32[]{:S(2)}, u32[]{:S(2)}) %collective-permute-start.16) | collective-permute-done | bytes 213024 | tf_op jit(solution)/shard_map/ppermute | solution.py:351
  88.3 0.5 collective-permute-done.15
  88.9 2.4 %collective-permute-done.14 = bf16[4,208,128]{2,1,0:T(8,128)(2,1)S(1)} collective-permute-done((bf16[4,208,128]{2,1,0:T(8,128)(2,1)S(1)}, bf16[4,208,128]{2,1,0:T(8,128)(2,1)S(1)}, u32[]{:S(2)}, u32[]{:S(2)}) %collective-permute-start.14) | collective-permute-done | bytes 213024 | tf_op jit(solution)/shard_map/ppermute | solution.py:351
  91.2 0.1 pad_maximum_fusion.p0_h
  91.4 0.1 collective-permute-start.17
  91.4 2.4 %collective-permute-done.17.p1_h = bf16[16,208,128]{2,1,0:T(8,128)(2,1)S(1)} collective-permute-done((bf16[16,208,128]{2,1,0:T(8,128)(2,1)S(1)}, bf16[16,208,128]{2,1,0:T(8,128)(2,1)S(1)}, u32[]{:S(2)}, u32[]{:S(2)}) %collective-permute-start.17) | collective-permute-done | bytes 852000 | tf_op jit(solution)/shard_map/ppermute | solution.py:351
  93.8 2.4 %unpack.1 = (f32[3,512,512]{2,1,0:T(8,128)}, bf16[64,512]{1,0:T(8,128)(2,1)}, bf16[64,512]{1,0:T(8,128)(2,1)}) custom-call(bf16[16,208,128]{2,1,0:T(8,128)(2,1)S(1)} %pad_maximum_fusion.p0_h, bf16[16,208,128]{2,1,0:T(8,128)(2,1)S(1)} %collective-permute-done.17.p1_h), custom_call_target="tpu_custom_call" | custom-call | flops 100000000 | bytes 4194304 | tf_op jit(solution)/shard_map/unpack/pallas_call | solution.py:330
  (4 shorter events, 0.1 us)
Async XLA Ops:
  2.4 15.4 %collective-permute-start.1 = (bf16[256,512]{1,0:T(8,128)(2,1)S(1)}, bf16[256,512]{1,0:T(8,128)(2,1)S(1)}, u32[]{:S(2)}, u32[]{:S(2)}) collective-permute-start(bf16[256,512]{1,0:T(8,128)(2,1)S(1)} %broadcast_select_fusion), channel_id=1, source_target_pairs={{0,28},{4,0},{8,4},{12,8},{16,12},{20,16},{24,20},{28,24},{1,29},{... | collective-permute-start | bytes 786440 | tf_op jit(solution)/shard_map/ppermute | solution.py:344
  8.5 10.5 %collective-permute-start = (bf16[256,512]{1,0:T(8,128)(2,1)S(1)}, bf16[256,512]{1,0:T(8,128)(2,1)S(1)}, u32[]{:S(2)}, u32[]{:S(2)}) collective-permute-start(bf16[256,512]{1,0:T(8,128)(2,1)S(1)} %broadcast_select_fusion), channel_id=1, source_target_pairs={{0,4},{4,8},{8,12},{12,16},{16,20},{20,24},{24,28},{28,0},{1,5},{5... | collective-permute-start | bytes 786440 | tf_op jit(solution)/shard_map/ppermute | solution.py:344
  11.8 24.4 %all-to-all-start = ((f32[32,16,128]{2,1,0:T(8,128)}), f32[32,16,128]{2,1,0:T(8,128)S(1)}, u32[]{:S(2)}, u32[]{:S(2)}) async-start(f32[32,16,128]{2,1,0:T(8,128)} %get-tuple-element.53), calls=%async_computation | async-start | bytes 524288 | tf_op jit(solution)/shard_map/all_to_all | solution.py:417
  17.9 1.1 %copy-start.3 = (bf16[256,512]{1,0:T(8,128)(2,1)}, bf16[256,512]{1,0:T(8,128)(2,1)S(1)}, u32[]{:S(2)}) copy-start(bf16[256,512]{1,0:T(8,128)(2,1)S(1)} %collective-permute-done.1.xr_h) | copy-start | bytes 786436
  18.9 0.7 copy-start.4
  32.6 11.7 %collective-permute-start.2 = (bf16[256,512]{1,0:T(8,128)(2,1)}, bf16[256,512]{1,0:T(8,128)(2,1)S(1)}, u32[]{:S(2)}, u32[]{:S(2)}) collective-permute-start(bf16[256,512]{1,0:T(8,128)(2,1)} %get-tuple-element.61), channel_id=1, source_target_pairs={{0,28},{4,0},{8,4},{12,8},{16,12},{20,16},{24,20},{28,24},{1,29},{... | collective-permute-start | bytes 786440 | tf_op jit(solution)/shard_map/ppermute | solution.py:344
  36.2 11.0 %collective-permute-start.3 = (bf16[256,512]{1,0:T(8,128)(2,1)}, bf16[256,512]{1,0:T(8,128)(2,1)S(1)}, u32[]{:S(2)}, u32[]{:S(2)}) collective-permute-start(bf16[256,512]{1,0:T(8,128)(2,1)} %get-tuple-element.62), channel_id=1, source_target_pairs={{0,4},{4,8},{8,12},{12,16},{16,20},{20,24},{24,28},{28,0},{1,5},{5... | collective-permute-start | bytes 786440 | tf_op jit(solution)/shard_map/ppermute | solution.py:344
  36.2 0.7 copy-start
  44.2 6.9 %copy-start.1 = (bf16[256,512]{1,0:T(8,128)(2,1)}, bf16[256,512]{1,0:T(8,128)(2,1)S(1)}, u32[]{:S(2)}) copy-start(bf16[256,512]{1,0:T(8,128)(2,1)S(1)} %collective-permute-done.2.from_right_h) | copy-start | bytes 786436
  47.2 4.0 %copy-start.2 = (bf16[256,512]{1,0:T(8,128)(2,1)}, bf16[256,512]{1,0:T(8,128)(2,1)S(1)}, u32[]{:S(2)}) copy-start(bf16[256,512]{1,0:T(8,128)(2,1)S(1)} %collective-permute-done.3.from_left_h) | copy-start | bytes 786436
  47.2 2.6 %collective-permute-start.4 = (bf16[16,208,128]{2,1,0:T(8,128)(2,1)}, bf16[16,208,128]{2,1,0:T(8,128)(2,1)S(1)}, u32[]{:S(2)}, u32[]{:S(2)}) collective-permute-start(bf16[16,208,128]{2,1,0:T(8,128)(2,1)} %get-tuple-element.63), channel_id=1, source_target_pairs={{0,1},{1,0},{2,3},{3,2},{4,5},{5,4},{6,7},{7,6},{8,9},{9,8},{10,11... | collective-permute-start | bytes 2555912 | tf_op jit(solution)/shard_map/ppermute | solution.py:351
  51.2 7.4 %collective-permute-start.7 = (bf16[4,208,128]{2,1,0:T(8,128)(2,1)S(1)}, bf16[4,208,128]{2,1,0:T(8,128)(2,1)S(1)}, u32[]{:S(2)}, u32[]{:S(2)}) collective-permute-start(bf16[4,208,128]{2,1,0:T(8,128)(2,1)S(1)} %get-tuple-element.91), channel_id=1, source_target_pairs={{0,4},{1,5},{2,6},{3,7},{4,0},{5,1},{6,2},{7,3},{8,12},{9,13},{10,... | collective-permute-start | bytes 638984 | tf_op jit(solution)/shard_map/ppermute | solution.py:351
  52.7 8.1 %collective-permute-start.6 = (bf16[4,208,128]{2,1,0:T(8,128)(2,1)S(1)}, bf16[4,208,128]{2,1,0:T(8,128)(2,1)S(1)}, u32[]{:S(2)}, u32[]{:S(2)}) collective-permute-start(bf16[4,208,128]{2,1,0:T(8,128)(2,1)S(1)} %get-tuple-element.92), channel_id=1, source_target_pairs={{0,2},{1,3},{2,0},{3,1},{4,6},{5,7},{6,4},{7,5},{8,10},{9,11},{10,... | collective-permute-start | bytes 638984 | tf_op jit(solution)/shard_map/ppermute | solution.py:351
  54.2 10.1 %collective-permute-start.5 = (bf16[4,208,128]{2,1,0:T(8,128)(2,1)S(1)}, bf16[4,208,128]{2,1,0:T(8,128)(2,1)S(1)}, u32[]{:S(2)}, u32[]{:S(2)}) collective-permute-start(bf16[4,208,128]{2,1,0:T(8,128)(2,1)S(1)} %get-tuple-element.93), channel_id=1, source_target_pairs={{0,6},{1,7},{2,4},{3,5},{4,2},{5,3},{6,0},{7,1},{8,14},{9,15},{10,... | collective-permute-start | bytes 638984 | tf_op jit(solution)/shard_map/ppermute | solution.py:351
  64.4 4.5 %collective-permute-start.10 = (bf16[208,128]{1,0:T(8,128)(2,1)S(1)}, bf16[208,128]{1,0:T(8,128)(2,1)S(1)}, u32[]{:S(2)}, u32[]{:S(2)}) collective-permute-start(bf16[208,128]{1,0:T(8,128)(2,1)S(1)} %get-tuple-element.94), channel_id=1, source_target_pairs={{0,8},{1,9},{2,10},{3,11},{4,12},{5,13},{6,14},{7,15},{8,0},{9,1},... | collective-permute-start | bytes 159752 | tf_op jit(solution)/shard_map/ppermute | solution.py:351
  65.0 5.0 %collective-permute-start.9 = (bf16[208,128]{1,0:T(8,128)(2,1)S(1)}, bf16[208,128]{1,0:T(8,128)(2,1)S(1)}, u32[]{:S(2)}, u32[]{:S(2)}) collective-permute-start(bf16[208,128]{1,0:T(8,128)(2,1)S(1)} %get-tuple-element.95), channel_id=1, source_target_pairs={{0,16},{1,17},{2,18},{3,19},{4,20},{5,21},{6,22},{7,23},{8,24},{9,... | collective-permute-start | bytes 159752 | tf_op jit(solution)/shard_map/ppermute | solution.py:351
  67.4 6.2 %collective-permute-start.8 = (bf16[208,128]{1,0:T(8,128)(2,1)S(1)}, bf16[208,128]{1,0:T(8,128)(2,1)S(1)}, u32[]{:S(2)}, u32[]{:S(2)}) collective-permute-start(bf16[208,128]{1,0:T(8,128)(2,1)S(1)} %get-tuple-element.96), channel_id=1, source_target_pairs={{0,24},{1,25},{2,26},{3,27},{4,28},{5,29},{6,30},{7,31},{8,16},{9,... | collective-permute-start | bytes 159752 | tf_op jit(solution)/shard_map/ppermute | solution.py:351
  73.7 4.5 %collective-permute-start.13 = (bf16[208,128]{1,0:T(8,128)(2,1)S(1)}, bf16[208,128]{1,0:T(8,128)(2,1)S(1)}, u32[]{:S(2)}, u32[]{:S(2)}) collective-permute-start(bf16[208,128]{1,0:T(8,128)(2,1)S(1)} %fusion.2), channel_id=1, source_target_pairs={{0,8},{1,9},{2,10},{3,11},{4,12},{5,13},{6,14},{7,15},{8,0},{9,1},... | collective-permute-start | bytes 159752 | tf_op jit(solution)/shard_map/ppermute | solution.py:351
  73.7 5.1 %collective-permute-start.12 = (bf16[208,128]{1,0:T(8,128)(2,1)S(1)}, bf16[208,128]{1,0:T(8,128)(2,1)S(1)}, u32[]{:S(2)}, u32[]{:S(2)}) collective-permute-start(bf16[208,128]{1,0:T(8,128)(2,1)S(1)} %fusion.2), channel_id=1, source_target_pairs={{0,16},{1,17},{2,18},{3,19},{4,20},{5,21},{6,22},{7,23},{8,24},{9,... | collective-permute-start | bytes 159752 | tf_op jit(solution)/shard_map/ppermute | solution.py:351
  75.5 5.9 %collective-permute-start.11 = (bf16[208,128]{1,0:T(8,128)(2,1)S(1)}, bf16[208,128]{1,0:T(8,128)(2,1)S(1)}, u32[]{:S(2)}, u32[]{:S(2)}) collective-permute-start(bf16[208,128]{1,0:T(8,128)(2,1)S(1)} %fusion.2), channel_id=1, source_target_pairs={{0,24},{1,25},{2,26},{3,27},{4,28},{5,29},{6,30},{7,31},{8,16},{9,... | collective-permute-start | bytes 159752 | tf_op jit(solution)/shard_map/ppermute | solution.py:351
  81.5 6.8 %collective-permute-start.16 = (bf16[4,208,128]{2,1,0:T(8,128)(2,1)S(1)}, bf16[4,208,128]{2,1,0:T(8,128)(2,1)S(1)}, u32[]{:S(2)}, u32[]{:S(2)}) collective-permute-start(bf16[4,208,128]{2,1,0:T(8,128)(2,1)S(1)} %pad_maximum_fusion.1), channel_id=1, source_target_pairs={{0,4},{1,5},{2,6},{3,7},{4,0},{5,1},{6,2},{7,3},{8,12},{9,13},{10,... | collective-permute-start | bytes 638984 | tf_op jit(solution)/shard_map/ppermute | solution.py:351
  83.0 5.8 %collective-permute-start.15 = (bf16[4,208,128]{2,1,0:T(8,128)(2,1)S(1)}, bf16[4,208,128]{2,1,0:T(8,128)(2,1)S(1)}, u32[]{:S(2)}, u32[]{:S(2)}) collective-permute-start(bf16[4,208,128]{2,1,0:T(8,128)(2,1)S(1)} %pad_maximum_fusion.1), channel_id=1, source_target_pairs={{0,2},{1,3},{2,0},{3,1},{4,6},{5,7},{6,4},{7,5},{8,10},{9,11},{10,... | collective-permute-start | bytes 638984 | tf_op jit(solution)/shard_map/ppermute | solution.py:351
  84.5 6.7 %collective-permute-start.14 = (bf16[4,208,128]{2,1,0:T(8,128)(2,1)S(1)}, bf16[4,208,128]{2,1,0:T(8,128)(2,1)S(1)}, u32[]{:S(2)}, u32[]{:S(2)}) collective-permute-start(bf16[4,208,128]{2,1,0:T(8,128)(2,1)S(1)} %pad_maximum_fusion.1), channel_id=1, source_target_pairs={{0,6},{1,7},{2,4},{3,5},{4,2},{5,3},{6,0},{7,1},{8,14},{9,15},{10,... | collective-permute-start | bytes 638984 | tf_op jit(solution)/shard_map/ppermute | solution.py:351
  91.4 2.4 %collective-permute-start.17 = (bf16[16,208,128]{2,1,0:T(8,128)(2,1)S(1)}, bf16[16,208,128]{2,1,0:T(8,128)(2,1)S(1)}, u32[]{:S(2)}, u32[]{:S(2)}) collective-permute-start(bf16[16,208,128]{2,1,0:T(8,128)(2,1)S(1)} %pad_maximum_fusion.p0_h), channel_id=1, source_target_pairs={{0,1},{1,0},{2,3},{3,2},{4,5},{5,4},{6,7},{7,6},{8,9},{9,8},{10,11... | collective-permute-start | bytes 2555912 | tf_op jit(solution)/shard_map/ppermute | solution.py:351

commit v3 on v2

--- a/solution.py
+++ b/solution.py
@@ -124,9 +124,9 @@
                      w_h, q_h, k_h, v_h, g_h, virt_h,
                      out_h, dq_h, left_h, right_h, dkn_h, dvn_h, dko_h, dvo_h,
                      xl_ref, xr_ref, w_ref, q_ref, g_ref,
-                     key_s, val_s, bias_s, ot_s, dqt_s, out_s, dq_s, dkn_s, dvn_s, dko_s, dvo_s, left_s, right_s, pat_ref, co_ref, sems):
+                     key_s, val_s, bias_s, ot_s, dqt_s, out_s, dq_s, dkn_s, dvn_s, dko_s, dvo_s, left_s, right_s, s_s, dw_s, wt_s, ds_s, pat_ref, co_ref, sems):
     n, width = q_ref.shape
-    virtual_rows = virt_h.shape[1]
+    virtual_rows, keys = virt_h.shape[1], key_s.shape[0]
     loop_here, loop_size, lanes = lax.axis_index("loop"), lax.axis_size("loop"), lax.axis_size("dp")
     own, virt = pl.ds(n, n), pl.ds(3 * n, virtual_rows)
     ready = loader((xl_h, xr_h, w_h.at[1], w_h.at[2], k_h, v_h, virt_h.at[1], virt_h.at[2], q_h, g_h, pat_h, co_h),
@@ -167,19 +167,33 @@
         k_pair, v_pair = key_s[:, c:c + 128], val_s[:, c:c + 128]
         q_pair = q_ref[:, c:c + 128]
         g_pair = jnp.where(ok, g_ref[:, c:c + 128], jnp.zeros((n, 128), BF))
+        k_t, v_t = k_pair.T, v_pair.T
+        masked = [(lane_half(q_pair, half), lane_half(g_pair, half)) for half in range(2)]
+        for half, (qm, gm) in enumerate(masked):
+            s_s[half] = nt(k_pair, qm) + bias_s[...]
+            dw_s[half] = nt(v_pair, gm)
         dk_pair = dv_pair = None
-        for half in range(2):
-            qm, gm = lane_half(q_pair, half), lane_half(g_pair, half)
-            s = nt(k_pair, qm) + bias_s[...]
-            e = jnp.exp(s - jnp.max(s, axis=0, keepdims=True))
-            a = e * (1.0 / jnp.sum(e, axis=0, keepdims=True))
-            wt = a.astype(BF)
-            dw = nt(v_pair, gm)
-            delta = jnp.sum(a * dw, axis=0, keepdims=True)
-            ds = (a * (dw - delta)).astype(BF)
+        for half, (qm, gm) in enumerate(masked):
+            peak = jnp.full((8, n), NEG_FILL, F32)
+            for r in range(0, keys, 64):
+                peak = jnp.maximum(peak, jnp.max(s_s[half, r:r + 64, :].reshape(64 // 8, 8, n), axis=0))
+            peak = jnp.max(peak, axis=0, keepdims=True)
+            total8 = delta8 = jnp.zeros((8, n), F32)
+            for r in range(0, keys, 64):
+                e = jnp.exp(s_s[half, r:r + 64, :] - peak)
+                s_s[half, r:r + 64, :] = e
+                total8 = total8 + jnp.sum(e.reshape(64 // 8, 8, n), axis=0)
+                delta8 = delta8 + jnp.sum((e * dw_s[half, r:r + 64, :]).reshape(64 // 8, 8, n), axis=0)
+            inv = 1.0 / jnp.sum(total8, axis=0, keepdims=True)
+            delta = jnp.sum(delta8, axis=0, keepdims=True) * inv
+            for r in range(0, keys, 64):
+                a = s_s[half, r:r + 64, :] * inv
+                wt_s[half, r:r + 64, :] = a.astype(BF)
+                ds_s[half, r:r + 64, :] = (a * (dw_s[half, r:r + 64, :] - delta)).astype(BF)
+            wt, ds = wt_s[half], ds_s[half]
             at = c + half * 64
-            ot_s[at:at + 64, :] = tn(v_pair, wt)[half * 64:half * 64 + 64]
-            dqt_s[at:at + 64, :] = tn(k_pair, ds)[half * 64:half * 64 + 64]
+            ot_s[at:at + 64, :] = nn(v_t[half * 64:half * 64 + 64], wt)
+            dqt_s[at:at + 64, :] = nn(k_t[half * 64:half * 64 + 64], ds)
             dk, dv = nn(ds, qm), nn(wt, gm)
             dk_pair = dk if dk_pair is None else dk_pair + dk
             dv_pair = dv if dv_pair is None else dv_pair + dv
@@ -188,37 +202,36 @@
             near[n:2 * n, c:c + 128] = part[2 * n:3 * n].astype(BF)
             mine[0:n, c:c + 128] = part[n:2 * n]
             mine[n:n + virtual_rows, c:c + 128] = part[3 * n:3 * n + virtual_rows]
+        dq_s[:, c:c + 128] = (dqt_s[c:c + 128, :] * score_scale).astype(BF).T
+        out_s[:, c:c + 128] = jnp.where(ok, ot_s[c:c + 128, :].astype(BF).T, jnp.zeros((n, 128), BF))
+        cols = pl.ds(c, 128)
+        for src, dst in ((dkn_s, dkn_h), (dvn_s, dvn_h), (dko_s, dko_h), (dvo_s, dvo_h), (dq_s, dq_h), (out_s, out_h)):
+            out.send(src.at[:, cols], dst.at[:, cols])
     for rows, ref, dst in ((slice(0, n), left_s, left_h), (slice(n, 2 * n), right_s, right_h)):
         ref[...] = (nt(dkn_s[rows, :], w_ref[0]) + nt(dvn_s[rows, :], w_ref[1])).astype(BF)
         out.send(ref, dst)
-    out.send(dkn_s, dkn_h)
-    out.send(dvn_s, dvn_h)
-    out.send(dko_s, dko_h)
-    out.send(dvo_s, dvo_h)
-    dq_s[...] = (dqt_s[...].T * score_scale).astype(BF)
-    out.send(dq_s, dq_h)
-    okw = own_row_ok(co_ref, blocks, block_rows, (n, width))
-    out_s[...] = jnp.where(okw, ot_s[...].T, 0.0).astype(BF)
-    out.send(out_s, out_h)
     out.finish()
 
 
 def weight_kernel(blocks, block_rows, score_scale, counts_h, x_h, xl_h, xr_h, vs_h, vcot_h, w_h,
                   k_h, v_h, virt_h, stats_h, dq_h, dkn_h, dvn_h, dko_h, dvo_h,
                   keep_h, send_h, kown_h, vown_h,
-                  xs_ref, vs_ref, vcot_ref, w_ref, k_ref, v_ref, virt_ref, stats_ref, dq_ref, dk_ref, dv_ref,
-                  keep_s, send_s, wg_s, vg_s, vo_s, vgrad_s, dkw_s, dvw_s, counts_ref, sems):
+                  xs_ref, vcot_ref, w_ref, k_ref, v_ref, virt_ref, stats_ref, dko_ref, dvo_ref,
+                  xt_s, dqw_s, dkw_s, dvw_s, pack_s, counts_ref, sems):
     n, width = x_h.shape
-    virtual_rows = vs_ref.shape[0]
-    low, own, high = pl.ds(0, n), pl.ds(n, n), pl.ds(2 * n, n)
-    ready = loader((stats_h, k_h, v_h, virt_h.at[0], vcot_h, dko_h, dvo_h, dq_h,
-                    x_h, xl_h, xr_h, vs_h, w_h, counts_h, dkn_h.at[low], dkn_h.at[own], dvn_h.at[low], dvn_h.at[own]),
-                   (stats_ref, k_ref, v_ref, virt_ref, vcot_ref, dk_ref, dv_ref, dq_ref,
-                    xs_ref.at[own], xs_ref.at[low], xs_ref.at[high], vs_ref, w_ref, counts_ref,
-                    dkw_s.at[low], dkw_s.at[high], dvw_s.at[low], dvw_s.at[high]), sems)
-    out = Writer(sems, 18)
+    virtual_rows = vs_h.shape[0]
+    near, own, last = pl.ds(0, 2 * n), pl.ds(2 * n, n), pl.ds(3 * n, virtual_rows)
+    ready = loader((xl_h, xr_h, x_h, vs_h, stats_h, counts_h, k_h, v_h, virt_h.at[0], vcot_h, dko_h, dvo_h,
+                    dq_h, dkn_h, dvn_h, w_h),
+                   (xs_ref.at[pl.ds(0, n)], xs_ref.at[pl.ds(n, n)], xs_ref.at[own], xs_ref.at[last], stats_ref, counts_ref,
+                    k_ref, v_ref, virt_ref, vcot_ref, dko_ref, dvo_ref,
+                    dqw_s.at[pl.ds(0, n)], dkw_s.at[near], dvw_s.at[near], w_ref), sems)
+    out = Writer(sems, 16)
     pairs = width // 128
-    ready(0, 13)
+    ready(0, 1, 2, 3)
+    for c in range(0, width, 128):
+        xt_s[c:c + 128, :] = xs_ref[:, c:c + 128].T
+    ready(4, 5)
     ok = own_row_ok(counts_ref, blocks, block_rows, (n, 128))
     stats = stats_ref[...]
     peak = jnp.max(stats[:, 0:pairs], axis=0)
@@ -231,7 +244,8 @@
     def diagonal(square):
         return jnp.where(lane_low, square[:virtual_rows], square[virtual_rows:])
 
-    ready(1, 2, 3, 4, 5, 6)
+    ready(6, 7, 8, 9, 10, 11)
+    mixed = []
     for p in range(pairs):
         c = p * 128
         k_pair, v_pair = k_ref[:, c:c + 128], v_ref[:, c:c + 128]
@@ -239,94 +253,89 @@
         vcot = both_heads(vcot_ref[:, c:c + 128])
         scores = jnp.where(ok, nt(k_pair, vq * score_scale), NEG_FILL)
         attn = jnp.exp(scores - peak[p:p + 1]) * inv_total[p:p + 1]
-        attn_hi = attn.astype(BF)
-        attn_lo = (attn - attn_hi.astype(F32)).astype(BF)
+        attn_bf = attn.astype(BF)
         dw = nt(v_pair, vcot)
         ds = (attn * (dw - delta[p:p + 1]) * score_scale).astype(BF)
-        vo_s[:, c:c + 128] = diagonal(tn(attn_hi, v_pair) + tn(attn_lo, v_pair))
-        vgrad_s[0, :, c:c + 128] = diagonal(tn(ds, k_pair))
-        dkw_s[n:2 * n, c:c + 128] = (dk_ref[0:n, c:c + 128] + nn(ds, vq)).astype(BF)
-        dvw_s[n:2 * n, c:c + 128] = (dv_ref[0:n, c:c + 128] + nn(attn_hi, vcot)).astype(BF)
+        mixed.append(diagonal(tn(attn_bf, v_pair)))
+        dqw_s[n:n + virtual_rows, c:c + 128] = diagonal(tn(ds, k_pair)).astype(BF)
+        dkw_s[2 * n:3 * n, c:c + 128] = (dko_ref[0:n, c:c + 128] + nn(ds, vq)).astype(BF)
+        dvw_s[2 * n:3 * n, c:c + 128] = (dvo_ref[0:n, c:c + 128] + nn(attn_bf, vcot)).astype(BF)
+    dkw_s[3 * n:3 * n + virtual_rows, :] = dko_ref[n:n + virtual_rows, :].astype(BF)
+    dvw_s[3 * n:3 * n + virtual_rows, :] = dvo_ref[n:n + virtual_rows, :].astype(BF)
     out.send(dkw_s.at[own], kown_h)
     out.send(dvw_s.at[own], vown_h)
-    vgrad_s[1] = dk_ref[n:n + virtual_rows, :]
-    vgrad_s[2] = dv_ref[n:n + virtual_rows, :]
-    ready(7, 8, 9, 10, 11, 12, 14, 15, 16, 17)
-    vs = vs_ref[...]
-    vg = None
+    ready(12, 13, 14)
+    me = place()
+    row_groups = width // 64
+    for c in range(0, width, 256):
+        for t in range(3):
+            if t == 0:
+                wg = nn(xt_s[:, 2 * n:], dqw_s[:, c:c + 256])
+            else:
+                wg = nn(xt_s[...], (dkw_s if t == 1 else dvw_s)[:, c:c + 256])
+            for col in range(0, 256, 128):
+                for group in range(row_groups):
+                    at = jnp.bitwise_xor(me, (c + col) // 128 * row_groups + group)
+                    pack_s[at, t * 64:(t + 1) * 64, :] = wg[group * 64:(group + 1) * 64, col:col + 128].astype(BF)
+    ready(15)
+    vg = (nt(dqw_s[n:n + virtual_rows, :], w_ref[0]) + nt(dkw_s[3 * n:3 * n + virtual_rows, :], w_ref[1])
+          + nt(dvw_s[3 * n:3 * n + virtual_rows, :], w_ref[2]))
+    for p in range(pairs):
+        for group in range(row_groups):
+            at = jnp.bitwise_xor(me, p * row_groups + group)
+            rows = slice(group * 8, group * 8 + 8)
+            pack_s[at, 192:208, :] = jnp.concatenate(
+                [vg[rows, p * 128:(p + 1) * 128], mixed[p][rows]], axis=0).astype(BF)
+    out.send(pack_s.at[pl.ds(SHARDS // 2, SHARDS // 2)], send_h)
+    out.send(pack_s.at[pl.ds(0, SHARDS // 2)], keep_h)
+    out.finish()
+
+
+def node_kernel(w_h, dq_h, dk_h, dv_h, part_h, w_ref, dq_ref, dk_ref, dv_ref, part_s, sems):
+    ready = loader((w_h, dq_h, dk_h, dv_h), (w_ref, dq_ref, dk_ref, dv_ref), sems)
+    out = Writer(sems, 4)
+    ready(0, 1, 2, 3)
+    part_s[...] = nt(dq_ref[...], w_ref[0]) + nt(dk_ref[...], w_ref[1]) + nt(dv_ref[...], w_ref[2])
+    out.send(part_s, part_h)
+    out.finish()
+
+
+def unpack_kernel(second, part_h, *refs):
+    wg_h, vg_h, vo_h, part_ref, wg_s, vg_s, vo_s, vgb_s, vob_s, sems = refs[3 * second:]
+    row_groups = wg_s.shape[1] // 64
+    ready = loader((part_h,), (part_ref,), sems)
+    out = Writer(sems, 1)
+    me = jnp.bitwise_and(place(), SHARDS // 2 - 1)
+    core = jnp.bitwise_and(lax.axis_index("dp"), 1)
+    if second:
+        core = 1 - core
+    half = wg_s.shape[2]
+    columns = pl.ds(pl.multiple_of(core * half, half), half)
+    ready(0)
     for t in range(3):
-        part = vgrad_s[t]
-        hi = part.astype(BF)
-        lo = (part - hi.astype(F32)).astype(BF)
-        if t == 0:
-            wg = tn(xs_ref[n:2 * n, :], dq_ref[...])
-        else:
-            wg = tn(xs_ref[...], (dkw_s if t == 1 else dvw_s)[...])
-        wg_s[t] = wg + (tn(vs, hi) + tn(vs, lo))
-        back = nt(hi, w_ref[t]) + nt(lo, w_ref[t])
-        vg = back if vg is None else vg + back
-    vg_s[...] = vg
-    row_groups = width // 64
-    me = place()
-    for half, ref, dst in ((1, send_s, send_h), (0, keep_s, keep_h)):
-        for at in range(SHARDS // 2):
-            shard = jnp.bitwise_xor(me, half * (SHARDS // 2) + at)
-            cols = pl.ds(pl.multiple_of((shard // row_groups) * 128, 128), 128)
-            group = lax.rem(shard, row_groups)
-            for t in range(3):
-                rows = pl.ds(pl.multiple_of(group * 64, 64), 64)
-                ref[at, t * 64:(t + 1) * 64, :] = wg_s[t, rows, cols].astype(BF)
-            rows = pl.ds(pl.multiple_of(group * 8, 8), 8)
-            ref[at, 192:208, :] = jnp.concatenate([vg_s[rows, cols], vo_s[rows, cols]], axis=0).astype(BF)
-        out.send(ref, dst)
-    out.finish()
-
-
-def node_kernel(w_h, dq_h, dk_h, dv_h, from_right_h, from_left_h, grad_h,
-                w_ref, dq_ref, dk_ref, dv_ref, from_right, from_left, grad_s, sems):
-    ready = loader((w_h, dq_h, dk_h, dv_h, from_right_h, from_left_h),
-                   (w_ref, dq_ref, dk_ref, dv_ref, from_right, from_left), sems)
-    out = Writer(sems, 6)
-    ready(0, 1, 2, 3)
-    part = nt(dq_ref[...], w_ref[0]) + nt(dk_ref[...], w_ref[1]) + nt(dv_ref[...], w_ref[2])
-    ready(4, 5)
-    grad_s[...] = (part + from_right[...].astype(F32) + from_left[...].astype(F32)).astype(BF)
-    out.send(grad_s, grad_h)
-    out.finish()
-
-
-def unpack_kernel(p0_h, p1_h, wg_h, vg_h, vo_h, p0_ref, p1_ref, wg_s, vg_s, vo_s, vgb_s, vob_s, sems):
-    width = wg_s.shape[2]
-    row_groups = width // 64
-    ready = loader((p0_h, p1_h), (p0_ref, p1_ref), sems)
-    out = Writer(sems, 2)
-    ready(0, 1)
-    me = place()
-    for t in range(3):
-        for p in range(SHARDS):
-            ref, at = (p0_ref, p1_ref)[p // (SHARDS // 2)], p % (SHARDS // 2)
+        for p in range(SHARDS // 2):
             shard = jnp.bitwise_xor(me, p)
             cols = pl.ds(pl.multiple_of((shard // row_groups) * 128, 128), 128)
             group = lax.rem(shard, row_groups)
             rows = pl.ds(pl.multiple_of(group * 64, 64), 64)
-            wg_s[t, rows, cols] = ref[at, t * 64:(t + 1) * 64, :].astype(F32)
+            wg_s[t, rows, cols] = part_ref[p, t * 64:(t + 1) * 64, :].astype(F32)
             if t == 0:
                 rows = pl.ds(pl.multiple_of(group * 8, 8), 8)
-                both = ref[at, 192:208, :].astype(F32)
+                both = part_ref[p, 192:208, :].astype(F32)
                 vg_s[rows, cols] = both[0:8]
                 vo_s[rows, cols] = both[8:16]
-        out.send(wg_s.at[t], wg_h.at[t])
+        out.send(wg_s.at[t], wg_h.at[t, :, columns])
     vgb_s[...] = vg_s[...].astype(BF)
     vob_s[...] = vo_s[...].astype(BF)
-    out.send(vgb_s, vg_h)
-    out.send(vob_s, vo_h)
+    out.send(vgb_s, vg_h.at[:, columns])
+    out.send(vob_s, vo_h.at[:, columns])
     out.finish()
 
 
 ANY = pl.BlockSpec(memory_space=pl.ANY)
 
 
-def call(body, args, outs, scratch, sems, flops=1e8, name=None, vmem=VMEM_BYTES):
+def call(body, args, outs, scratch, sems, flops=1e8, name=None, vmem=VMEM_BYTES, aliases=None):
     return pl.pallas_call(
         body,
         out_shape=[jax.ShapeDtypeStruct(s, d) for s, d in outs],
@@ -335,6 +344,7 @@
         scratch_shapes=[pltpu.SMEM(s, d) if d == jnp.int32 else pltpu.VMEM(s, d) for s, d in scratch] + [pltpu.SemaphoreType.DMA((sems,))],
         compiler_params=pltpu.CompilerParams(vmem_limit_bytes=vmem),
         cost_estimate=pl.CostEstimate(flops=int(flops), bytes_accessed=4 << 20, transcendentals=0),
+        input_output_aliases=aliases or {},
         name=name,
     )(*args)
 
@@ -366,14 +376,15 @@
     return summed.astype(BF)
 
 
-def reduce_all(keep, send, node_step, middle):
+def reduce_all(keep, send, own_part, to_left, to_right):
     loop_size = lax.axis_size("loop")
     held = total([keep, swap(send, 0, 1)])
-    held, middle = together((held, middle))
+    held = together(held)
     quarters = [held[4 * j:4 * j + 4] for j in range(4)]
     got = [swap(quarters[3 - j], *bits) for j, bits in enumerate(PLANE)]
-    got, middle = together((got, node_step(*middle)))
-    held = together(total([quarters[0]] + got))
+    got, own_part = together((got, own_part))
+    held, to_left, to_right = together((total([quarters[0]] + got), to_left, to_right))
+    from_right, from_left = ring(to_left, -1), ring(to_right, 1)
     got = together([swap(held[3 - j], *bits) for j, bits in enumerate(LINE)])
     piece = total([held[0]] + got)
     bit = 8
@@ -381,11 +392,11 @@
         piece = total([piece, swap(piece, bit, 0)])
         bit *= 2
     piece = together(piece)
-    got = together([swap(piece, *bits) for bits in LINE])
+    got, from_right, from_left = together(([swap(piece, *bits) for bits in LINE], from_right, from_left))
     held = together(jnp.stack([piece] + got[::-1]))
-    got = together([swap(held, *bits) for bits in PLANE])
+    got, node_grad = together(([swap(held, *bits) for bits in PLANE], total([own_part, from_right, from_left])))
     held = together(jnp.concatenate([held] + got[::-1], axis=0))
-    return held, swap(held, 0, 1), middle
+    return held, swap(held, 0, 1), node_grad
 
 
 def local(node_states, virtual_states, projection, pattern, valid_counts, node_cotangent, virtual_cotangent):
@@ -399,7 +410,8 @@
     keys = 3 * n + virtual_rows
 
     shape = (blocks, block_rows, width)
-    valid = lax.broadcasted_iota(jnp.int32, shape, 1) < lax.broadcast_in_dim(valid_counts, shape, (0,))
+    place_in_block = lax.broadcasted_iota(jnp.int32, shape, 1) * width + lax.broadcasted_iota(jnp.int32, shape, 2)
+    valid = place_in_block < lax.broadcast_in_dim(valid_counts * width, shape, (0,))
     marked = jnp.where(valid, node_states.reshape(shape), jnp.asarray(ABSENT, BF)).reshape(n, width)
     x_left, x_right = ring(marked, 1), ring(marked, -1)
 
@@ -425,29 +437,30 @@
         [rows_bf] * 4 + [near_bf] * 2 + [mine_f] * 2,
         [rows_bf] * 2 + [((2, width, width), BF)] + [rows_bf] * 2
         + [keys_bf] * 2 + [((keys, n), F32), across, across] + [rows_bf] * 2 + [near_bf] * 2 + [mine_f] * 2 + [rows_bf] * 2
-        + [pattern_i, counts_i], 20,
+        + [((2, keys, n), F32)] * 2 + [((2, keys, n), BF)] * 2 + [pattern_i, counts_i], 40,
         flops=4e9, name="attention")
-    from_right, from_left = ring(to_left, -1), ring(to_right, 1)
-
-    window_bf = ((3 * n, width), BF)
+    to_left, to_right, stats = together((to_left, to_right, stats))
+
     half = ((SHARDS // 2, 3 * 64 + 16, 128), BF)
     keep, send, dk, dv = call(
         functools.partial(weight_kernel, blocks, block_rows, score_scale),
         (valid_counts, node_states, x_left, x_right, virtual_states, virtual_cotangent, projection, k, v, virt, stats,
          dq, dkn, dvn, dko, dvo),
         [half] * 2 + [rows_bf] * 2,
-        [window_bf, virt_bf, virt_bf, wide, rows_bf, rows_bf, virt_bf, stats_f, rows_bf, mine_f, mine_f]
-        + [half] * 2 + [((3, width, width), F32), virt_f, virt_f, ((3, virtual_rows, width), F32), window_bf, window_bf, counts_i], 24,
+        [keys_bf, virt_bf, wide, rows_bf, rows_bf, virt_bf, stats_f, mine_f, mine_f,
+         ((width, keys), BF), ((n + virtual_rows, width), BF), keys_bf, keys_bf, ((SHARDS, 3 * 64 + 16, 128), BF), counts_i], 20,
         flops=8e9, name="weight_grads")
-    def node_step(*args):
-        return call(node_kernel, args, [rows_bf], [wide] + [rows_bf] * 6, 7, flops=1e9, name="node_grads")[0]
-
-    send, from_right, from_left = together((send, from_right, from_left))
-    mine, other, node_grad = reduce_all(keep, send, node_step, (projection, dq, dk, dv, from_right, from_left))
-    weight_grads, virtual_grad, virtual_out = call(
-        unpack_kernel, (mine, other), [((3, width, width), F32), virt_bf, virt_bf],
-        [half, half, ((3, width, width), F32), virt_f, virt_f, virt_bf, virt_bf], 7, name="unpack",
+    own_part, = call(node_kernel, (projection, dq, dk, dv), [rows_f], [wide] + [rows_bf] * 3 + [rows_f], 5,
+                     flops=1e9, name="node_grads")
+    mine, other, node_grad = reduce_all(keep, send, own_part, to_left, to_right)
+    halves_f = ((virtual_rows, width // 2), F32)
+    unpack = functools.partial(
+        call, outs=[((3, width, width), F32), virt_bf, virt_bf],
+        scratch=[half, ((3, width, width // 2), F32), halves_f, halves_f] + [((virtual_rows, width // 2), BF)] * 2, sems=6,
         vmem=16 << 20)
+    results = unpack(functools.partial(unpack_kernel, 0), (mine,), name="unpack_mine")
+    weight_grads, virtual_grad, virtual_out = unpack(
+        functools.partial(unpack_kernel, 1), (other, *results), name="unpack_other", aliases={1: 0, 2: 1, 3: 2})
     return node_out, virtual_out, node_grad, virtual_grad, weight_grads
 
 

time: 96.7 us -> 90.4 us (0.935)
  waiting for transfers between devices: 29.7 us -> 23 us
  Pallas kernels: 29 us -> 27.2 us
    ppermute x14, waiting for transfers between devices: 25.7 us -> 21.1 us  [swap(): lax.ppermute(value, ('loop', 'dp'), [(s, s ^ other) for s in range(count)])]
    ppermute x4, waiting for transfers between devices: 3.97 us -> 1.86 us  [ring(): lax.ppermute(value, 'loop', [(s, (s + steps) % count) for s in range(coun...]
    pallas_call x5 -> x6, Pallas kernels: 29 us -> 27.2 us  [call(): pl.pallas_call(body, out_shape=[jax.ShapeDtypeStruct(s, d) for s, d in ou...]
    convert_element_type x3 -> x4, other arithmetic: 1.53 us -> 2.34 us  [total(): return summed.astype(BF)]
  transfers between devices with their start and end apart: 19 -> 19, of which waited for: 14 -> 13; matrix products, arithmetic and copies ran while one was open for 0% -> 1% of each run, Pallas kernels for 28% -> 21%
where the time goes in v3:
time: 90.4 us; the launch traced here: 89.4 us
  starting transfers between devices  32.7 us (36%)
  Pallas kernels  27.2 us (30%)
  waiting for transfers between devices  23 us (25%)
  other arithmetic  4.27 us (5%)
  local copies, waits for them, and re-layouts  1.54 us (2%)
    pallas_call x6, Pallas kernels, call(): pl.pallas_call(body, out_shape=[jax.ShapeDtypeStruct(s, d) for s, d in ou...  27.2 us
    ppermute x14, waiting for transfers between devices, swap(): lax.ppermute(value, ('loop', 'dp'), [(s, s ^ other) for s in range(count)])  21.1 us
    ppermute x14, starting transfers between devices, swap(): lax.ppermute(value, ('loop', 'dp'), [(s, s ^ other) for s in range(count)])  17 us
    ppermute x4, starting transfers between devices, ring(): lax.ppermute(value, 'loop', [(s, (s + steps) % count) for s in range(coun...  9.64 us
    all_to_all x1, starting transfers between devices, local(): stats = lax.all_to_all(stats, ('loop', 'dp'), 0, 0, tiled=True)  6.02 us
    convert_element_type x4, other arithmetic, total(): return summed.astype(BF)  2.34 us
    ppermute x4, waiting for transfers between devices, ring(): lax.ppermute(value, 'loop', [(s, (s + steps) % count) for s in range(coun...  1.86 us
  transfers between devices with their start and end apart: 19, of which 13 were waited for; matrix products, arithmetic and copies ran while one was open for 1% of the time, Pallas kernels for 21%

profile of v3, /device:TPU:0, one launch (start us, length us, event | category | flops | bytes accessed | tf_op | source)
XLA Modules:
  0.0 89.4 jit_solution(7562660196320774528)
XLA Ops:
  0.6 0.7 broadcast_multiply_fusion
  1.3 0.1 broadcast_bitcast_fusion.1
  1.4 1.1 %fusion = bf16[256,512]{1,0:T(8,128)(2,1)S(1)} fusion(bf16[256,512]{1,0:T(8,128)(2,1)} %x_h.3, s32[256]{0:T(256)S(1)} %broadcast_bitcast_fusion.1, s32[256]{0:T(256)S(1)} %broadcast_bitcast_fusion), kind=kLoop, calls=%fused_computation.4 | loop fusion | flops 393216 | bytes 526336 | tf_op jit(solution)/shard_map/jit(_where)/select_n | solution.py:415
  2.5 6.1 %collective-permute-start.1 = (bf16[256,512]{1,0:T(8,128)(2,1)S(1)}, bf16[256,512]{1,0:T(8,128)(2,1)S(1)}, u32[]{:S(2)}, u32[]{:S(2)}) collective-permute-start(bf16[256,512]{1,0:T(8,128)(2,1)S(1)} %fusion), channel_id=1, source_target_pairs={{0,28},{4,0},{8,4},{12,8},{16,12},{20,16},{24,20},{28,24},{1,29},{... | collective-permute-start | bytes 786440 | tf_op jit(solution)/shard_map/ppermute | solution.py:354
  8.6 0.0 collective-permute-start
  8.6 3.3 %project.1 = (bf16[256,512]{1,0:T(8,128)(2,1)}, bf16[256,512]{1,0:T(8,128)(2,1)}, bf16[256,512]{1,0:T(8,128)(2,1)}, bf16[3,64,512]{2,1,0:T(8,128)(2,1)}, f32[32,16,128]{2,1,0:T(8,128)}) custom-call(s32[2]{0:T(128)} %counts_h.3, bf16[256,512]{1,0:T(8,128)(2,1)} %x_h.3, bf16[3,512,512]{2,1,0:T(8,128)(2,1)} %w_h.7, bf16[64,512]{1,0:T(8,128)(2,1)} %vs_h.3, ...), custom_call_target="tpu_custom_call" | custom-call | flops 100000000 | bytes 4194304 | tf_op jit(solution)/shard_map/project/pallas_call | solution.py:339
  11.9 6.0 %all-to-all-start = ((f32[32,16,128]{2,1,0:T(8,128)}), f32[32,16,128]{2,1,0:T(8,128)S(1)}, u32[]{:S(2)}, u32[]{:S(2)}) async-start(f32[32,16,128]{2,1,0:T(8,128)} %get-tuple-element.57), calls=%async_computation | async-start | bytes 524288 | tf_op jit(solution)/shard_map/all_to_all | solution.py:429
  17.9 0.0 collective-permute-done.1.xr_h
  18.0 0.0 copy-start.4
  18.0 1.1 %collective-permute-done.xl_h = bf16[256,512]{1,0:T(8,128)(2,1)S(1)} collective-permute-done((bf16[256,512]{1,0:T(8,128)(2,1)S(1)}, bf16[256,512]{1,0:T(8,128)(2,1)S(1)}, u32[]{:S(2)}, u32[]{:S(2)}) %collective-permute-start) | collective-permute-done | bytes 262176 | tf_op jit(solution)/shard_map/ppermute | solution.py:354
  19.0 0.0 copy-start.5
  19.0 0.0 copy-done.4
  19.0 0.7 copy-done.5
  19.7 11.1 %attention.1 = (bf16[256,512]{1,0:T(8,128)(2,1)}, bf16[256,512]{1,0:T(8,128)(2,1)}, bf16[256,512]{1,0:T(8,128)(2,1)}, bf16[256,512]{1,0:T(8,128)(2,1)}, bf16[512...) custom-call(s32[2,5]{1,0:T(2,128)} %pat_h.1, s32[2]{0:T(128)} %counts_h.3, ...), custom_call_target="tpu_custom_call" | custom-call | flops 4000000000 | bytes 4194304 | tf_op jit(solution)/shard_map/attention/pallas_call | solution.py:339
  30.8 0.0 all-to-all-done.stats_h
  30.8 0.0 copy-start.1
  30.8 0.7 copy-done.1
  31.5 6.7 %weight_grads.1 = (bf16[16,208,128]{2,1,0:T(8,128)(2,1)}, bf16[16,208,128]{2,1,0:T(8,128)(2,1)}, bf16[256,512]{1,0:T(8,128)(2,1)}, bf16[256,512]{1,0:T(8,128)(2,1)}) custom-call(s32[2]{0:T(128)} %counts_h.3, bf16[256,512]{1,0:T(8,128)(2,1)} %x_h.3, bf16[256,512]{1,0:T(8,128)(2,1)} %copy-done.5, bf16[256,512]{1,0:T(8,128)(2,1)} %copy-done.4, ...), custom_call_target="tpu_custom_call" | custom-call | flops 8000000000 | bytes 4194304 | tf_op jit(solution)/shard_map/weight_grads/pallas_call | solution.py:339
  38.2 0.1 collective-permute-start.2
  38.3 2.6 %collective-permute-done.2 = bf16[16,208,128]{2,1,0:T(8,128)(2,1)S(1)} collective-permute-done((bf16[16,208,128]{2,1,0:T(8,128)(2,1)}, bf16[16,208,128]{2,1,0:T(8,128)(2,1)S(1)}, u32[]{:S(2)}, u32[]{:S(2)}) %collective-permute-start.2) | collective-permute-done | bytes 852000 | tf_op jit(solution)/shard_map/ppermute | solution.py:361
  40.9 1.4 %add_convert_fusion = bf16[16,208,128]{2,1,0:T(8,128)(2,1)S(1)} fusion(bf16[16,208,128]{2,1,0:T(8,128)(2,1)S(1)} %collective-permute-done.2, bf16[16,208,128]{2,1,0:T(8,128)(2,1)} %get-tuple-element.64), kind=kLoop, calls=%fused_computation | loop fusion | flops 1703936 | bytes 2555904 | tf_op jit(solution)/shard_map/convert_element_type | solution.py:376
  42.3 1.1 %collective-permute-start.5 = (bf16[4,208,128]{2,1,0:T(8,128)(2,1)S(1)}, bf16[4,208,128]{2,1,0:T(8,128)(2,1)S(1)}, u32[]{:S(2)}, u32[]{:S(2)}) collective-permute-start(bf16[4,208,128]{2,1,0:T(8,128)(2,1)S(1)} %get-tuple-element.95), channel_id=1, source_target_pairs={{0,4},{1,5},{2,6},{3,7},{4,0},{5,1},{6,2},{7,3},{8,12},{9,13},{10,... | collective-permute-start | bytes 638984 | tf_op jit(solution)/shard_map/ppermute | solution.py:361
  43.5 1.5 %collective-permute-start.4 = (bf16[4,208,128]{2,1,0:T(8,128)(2,1)S(1)}, bf16[4,208,128]{2,1,0:T(8,128)(2,1)S(1)}, u32[]{:S(2)}, u32[]{:S(2)}) collective-permute-start(bf16[4,208,128]{2,1,0:T(8,128)(2,1)S(1)} %get-tuple-element.96), channel_id=1, source_target_pairs={{0,2},{1,3},{2,0},{3,1},{4,6},{5,7},{6,4},{7,5},{8,10},{9,11},{10,... | collective-permute-start | bytes 638984 | tf_op jit(solution)/shard_map/ppermute | solution.py:361
  44.9 0.9 %collective-permute-start.3 = (bf16[4,208,128]{2,1,0:T(8,128)(2,1)S(1)}, bf16[4,208,128]{2,1,0:T(8,128)(2,1)S(1)}, u32[]{:S(2)}, u32[]{:S(2)}) collective-permute-start(bf16[4,208,128]{2,1,0:T(8,128)(2,1)S(1)} %get-tuple-element.97), channel_id=1, source_target_pairs={{0,6},{1,7},{2,4},{3,5},{4,2},{5,3},{6,0},{7,1},{8,14},{9,15},{10,... | collective-permute-start | bytes 638984 | tf_op jit(solution)/shard_map/ppermute | solution.py:361
  45.9 0.0 copy-start.3
  45.9 0.0 copy-start.2
  45.9 3.1 %node_grads.1 = f32[256,512]{1,0:T(8,128)} custom-call(bf16[3,512,512]{2,1,0:T(8,128)(2,1)} %w_h.7, bf16[256,512]{1,0:T(8,128)(2,1)} %get-tuple-element.59.dq_h, bf16[256,512]{1,0:T(8,128)(2,1)} %get-tuple-element.66.dk_h, bf16[256,512]{1,0:T(8,128)(2,1)} %get-tuple-element.67.dv_h), custom_call_target="tpu_custom_call" | custom-call | flops 1000000000 | bytes 4194304 | tf_op jit(solution)/shard_map/node_grads/pallas_call | solution.py:339
  49.0 0.0 copy-start
  49.0 0.7 collective-permute-done.5
  49.7 1.9 %collective-permute-done.4 = bf16[4,208,128]{2,1,0:T(8,128)(2,1)S(1)} collective-permute-done((bf16[4,208,128]{2,1,0:T(8,128)(2,1)S(1)}, bf16[4,208,128]{2,1,0:T(8,128)(2,1)S(1)}, u32[]{:S(2)}, u32[]{:S(2)}) %collective-permute-start.4) | collective-permute-done | bytes 213024 | tf_op jit(solution)/shard_map/ppermute | solution.py:361
  51.6 3.8 %collective-permute-done.3 = bf16[4,208,128]{2,1,0:T(8,128)(2,1)S(1)} collective-permute-done((bf16[4,208,128]{2,1,0:T(8,128)(2,1)S(1)}, bf16[4,208,128]{2,1,0:T(8,128)(2,1)S(1)}, u32[]{:S(2)}, u32[]{:S(2)}) %collective-permute-start.3) | collective-permute-done | bytes 213024 | tf_op jit(solution)/shard_map/ppermute | solution.py:361
  55.4 0.1 add_convert_fusion.2
  55.6 0.9 collective-permute-start.8
  56.4 2.4 %collective-permute-start.7 = (bf16[208,128]{1,0:T(8,128)(2,1)S(1)}, bf16[208,128]{1,0:T(8,128)(2,1)S(1)}, u32[]{:S(2)}, u32[]{:S(2)}) collective-permute-start(bf16[208,128]{1,0:T(8,128)(2,1)S(1)} %get-tuple-element.99), channel_id=1, source_target_pairs={{0,16},{1,17},{2,18},{3,19},{4,20},{5,21},{6,22},{7,23},{8,24},{9,... | collective-permute-start | bytes 159752 | tf_op jit(solution)/shard_map/ppermute | solution.py:361
  58.9 1.2 %collective-permute-start.6 = (bf16[208,128]{1,0:T(8,128)(2,1)S(1)}, bf16[208,128]{1,0:T(8,128)(2,1)S(1)}, u32[]{:S(2)}, u32[]{:S(2)}) collective-permute-start(bf16[208,128]{1,0:T(8,128)(2,1)S(1)} %get-tuple-element.100), channel_id=1, source_target_pairs={{0,24},{1,25},{2,26},{3,27},{4,28},{5,29},{6,30},{7,31},{8,16},{9,... | collective-permute-start | bytes 159752 | tf_op jit(solution)/shard_map/ppermute | solution.py:361
  60.0 0.0 copy-done.3
  60.0 3.6 %collective-permute-start.12 = (bf16[256,512]{1,0:T(8,128)(2,1)S(1)}, bf16[256,512]{1,0:T(8,128)(2,1)S(1)}, u32[]{:S(2)}, u32[]{:S(2)}) collective-permute-start(bf16[256,512]{1,0:T(8,128)(2,1)S(1)} %copy-done.3), channel_id=1, source_target_pairs={{0,28},{4,0},{8,4},{12,8},{16,12},{20,16},{24,20},{28,24},{1,29},{... | collective-permute-start | bytes 786440 | tf_op jit(solution)/shard_map/ppermute | solution.py:354
  63.6 0.0 copy-done.2
  63.6 0.0 collective-permute-start.13
  63.6 0.0 collective-permute-done.8
  63.6 0.0 collective-permute-done.7
  63.6 1.8 %collective-permute-done.6 = bf16[208,128]{1,0:T(8,128)(2,1)S(1)} collective-permute-done((bf16[208,128]{1,0:T(8,128)(2,1)S(1)}, bf16[208,128]{1,0:T(8,128)(2,1)S(1)}, u32[]{:S(2)}, u32[]{:S(2)}) %collective-permute-start.6) | collective-permute-done | bytes 53280 | tf_op jit(solution)/shard_map/ppermute | solution.py:361
  65.5 0.1 collective-permute-start.11
  65.5 1.1 %collective-permute-start.10 = (bf16[208,128]{1,0:T(8,128)(2,1)S(1)}, bf16[208,128]{1,0:T(8,128)(2,1)S(1)}, u32[]{:S(2)}, u32[]{:S(2)}) collective-permute-start(bf16[208,128]{1,0:T(8,128)(2,1)S(1)} %fusion.3), channel_id=1, source_target_pairs={{0,16},{1,17},{2,18},{3,19},{4,20},{5,21},{6,22},{7,23},{8,24},{9,... | collective-permute-start | bytes 159752 | tf_op jit(solution)/shard_map/ppermute | solution.py:361
  66.6 3.3 %collective-permute-start.9 = (bf16[208,128]{1,0:T(8,128)(2,1)S(1)}, bf16[208,128]{1,0:T(8,128)(2,1)S(1)}, u32[]{:S(2)}, u32[]{:S(2)}) collective-permute-start(bf16[208,128]{1,0:T(8,128)(2,1)S(1)} %fusion.3), channel_id=1, source_target_pairs={{0,24},{1,25},{2,26},{3,27},{4,28},{5,29},{6,30},{7,31},{8,16},{9,... | collective-permute-start | bytes 159752 | tf_op jit(solution)/shard_map/ppermute | solution.py:361
  69.9 0.8 collective-permute-done.11
  70.7 2.7 %collective-permute-done.10 = bf16[208,128]{1,0:T(8,128)(2,1)S(1)} collective-permute-done((bf16[208,128]{1,0:T(8,128)(2,1)S(1)}, bf16[208,128]{1,0:T(8,128)(2,1)S(1)}, u32[]{:S(2)}, u32[]{:S(2)}) %collective-permute-start.10) | collective-permute-done | bytes 53280 | tf_op jit(solution)/shard_map/ppermute | solution.py:361
  73.4 0.0 collective-permute-done.9
  73.4 0.0 collective-permute-done.12
  73.4 0.8 collective-permute-done.13
  74.2 2.9 %collective-permute-start.16 = (bf16[4,208,128]{2,1,0:T(8,128)(2,1)S(1)}, bf16[4,208,128]{2,1,0:T(8,128)(2,1)S(1)}, u32[]{:S(2)}, u32[]{:S(2)}) collective-permute-start(bf16[4,208,128]{2,1,0:T(8,128)(2,1)S(1)} %pad_maximum_fusion.1), channel_id=1, source_target_pairs={{0,4},{1,5},{2,6},{3,7},{4,0},{5,1},{6,2},{7,3},{8,12},{9,13},{10,... | collective-permute-start | bytes 638984 | tf_op jit(solution)/shard_map/ppermute | solution.py:361
  77.1 1.5 %collective-permute-start.15 = (bf16[4,208,128]{2,1,0:T(8,128)(2,1)S(1)}, bf16[4,208,128]{2,1,0:T(8,128)(2,1)S(1)}, u32[]{:S(2)}, u32[]{:S(2)}) collective-permute-start(bf16[4,208,128]{2,1,0:T(8,128)(2,1)S(1)} %pad_maximum_fusion.1), channel_id=1, source_target_pairs={{0,2},{1,3},{2,0},{3,1},{4,6},{5,7},{6,4},{7,5},{8,10},{9,11},{10,... | collective-permute-start | bytes 638984 | tf_op jit(solution)/shard_map/ppermute | solution.py:361
  78.6 0.1 collective-permute-start.14
  78.6 0.0 copy-done
  78.6 0.8 add_convert_fusion.1
  79.4 3.7 %collective-permute-done.16 = bf16[4,208,128]{2,1,0:T(8,128)(2,1)S(1)} collective-permute-done((bf16[4,208,128]{2,1,0:T(8,128)(2,1)S(1)}, bf16[4,208,128]{2,1,0:T(8,128)(2,1)S(1)}, u32[]{:S(2)}, u32[]{:S(2)}) %collective-permute-start.16) | collective-permute-done | bytes 213024 | tf_op jit(solution)/shard_map/ppermute | solution.py:361
  83.1 0.2 collective-permute-done.15
  83.3 2.1 %collective-permute-done.14 = bf16[4,208,128]{2,1,0:T(8,128)(2,1)S(1)} collective-permute-done((bf16[4,208,128]{2,1,0:T(8,128)(2,1)S(1)}, bf16[4,208,128]{2,1,0:T(8,128)(2,1)S(1)}, u32[]{:S(2)}, u32[]{:S(2)}) %collective-permute-start.14) | collective-permute-done | bytes 213024 | tf_op jit(solution)/shard_map/ppermute | solution.py:361
  85.4 0.1 pad_maximum_fusion.part_h
  85.5 0.1 collective-permute-start.17
  85.6 1.5 %unpack_mine.1 = (f32[3,512,512]{2,1,0:T(8,128)}, bf16[64,512]{1,0:T(8,128)(2,1)}, bf16[64,512]{1,0:T(8,128)(2,1)}) custom-call(bf16[16,208,128]{2,1,0:T(8,128)(2,1)S(1)} %pad_maximum_fusion.part_h), custom_call_target="tpu_custom_call" | custom-call | flops 100000000 | bytes 4194304 | tf_op jit(solution)/shard_map/unpack_mine/pallas_call | solution.py:339
  87.1 0.9 collective-permute-done.17.part_h
  87.9 1.5 %unpack_other.1 = (f32[3,512,512]{2,1,0:T(8,128)}, bf16[64,512]{1,0:T(8,128)(2,1)}, bf16[64,512]{1,0:T(8,128)(2,1)}) custom-call(bf16[16,208,128]{2,1,0:T(8,128)(2,1)S(1)} %collective-permute-done.17.part_h, f32[3,512,512]{2,1,0:T(8,128)} %get-tuple-element.88.refs_0_, ...), custom_call_target="tpu_custom_call", output_to_operand_aliasing={{0}: (1, {}), {1}: (2, {}), {2}: (3, {})} | custom-call | flops 100000000 | bytes 4194304 | tf_op jit(solution)/shard_map/unpack_other/pallas_call | solution.py:339
  (6 shorter events, 0.1 us)
Async XLA Ops:
  2.5 15.4 %collective-permute-start.1 = (bf16[256,512]{1,0:T(8,128)(2,1)S(1)}, bf16[256,512]{1,0:T(8,128)(2,1)S(1)}, u32[]{:S(2)}, u32[]{:S(2)}) collective-permute-start(bf16[256,512]{1,0:T(8,128)(2,1)S(1)} %fusion), channel_id=1, source_target_pairs={{0,28},{4,0},{8,4},{12,8},{16,12},{20,16},{24,20},{28,24},{1,29},{... | collective-permute-start | bytes 786440 | tf_op jit(solution)/shard_map/ppermute | solution.py:354
  8.6 10.5 %collective-permute-start = (bf16[256,512]{1,0:T(8,128)(2,1)S(1)}, bf16[256,512]{1,0:T(8,128)(2,1)S(1)}, u32[]{:S(2)}, u32[]{:S(2)}) collective-permute-start(bf16[256,512]{1,0:T(8,128)(2,1)S(1)} %fusion), channel_id=1, source_target_pairs={{0,4},{4,8},{8,12},{12,16},{16,20},{20,24},{24,28},{28,0},{1,5},{5... | collective-permute-start | bytes 786440 | tf_op jit(solution)/shard_map/ppermute | solution.py:354
  11.9 18.9 %all-to-all-start = ((f32[32,16,128]{2,1,0:T(8,128)}), f32[32,16,128]{2,1,0:T(8,128)S(1)}, u32[]{:S(2)}, u32[]{:S(2)}) async-start(f32[32,16,128]{2,1,0:T(8,128)} %get-tuple-element.57), calls=%async_computation | async-start | bytes 524288 | tf_op jit(solution)/shard_map/all_to_all | solution.py:429
  18.0 1.1 %copy-start.4 = (bf16[256,512]{1,0:T(8,128)(2,1)}, bf16[256,512]{1,0:T(8,128)(2,1)S(1)}, u32[]{:S(2)}) copy-start(bf16[256,512]{1,0:T(8,128)(2,1)S(1)} %collective-permute-done.1.xr_h) | copy-start | bytes 786436
  19.0 0.7 copy-start.5
  30.8 0.7 copy-start.1
  38.2 2.7 %collective-permute-start.2 = (bf16[16,208,128]{2,1,0:T(8,128)(2,1)}, bf16[16,208,128]{2,1,0:T(8,128)(2,1)S(1)}, u32[]{:S(2)}, u32[]{:S(2)}) collective-permute-start(bf16[16,208,128]{2,1,0:T(8,128)(2,1)} %get-tuple-element.65), channel_id=1, source_target_pairs={{0,1},{1,0},{2,3},{3,2},{4,5},{5,4},{6,7},{7,6},{8,9},{9,8},{10,11... | collective-permute-start | bytes 2555912 | tf_op jit(solution)/shard_map/ppermute | solution.py:361
  42.3 7.4 %collective-permute-start.5 = (bf16[4,208,128]{2,1,0:T(8,128)(2,1)S(1)}, bf16[4,208,128]{2,1,0:T(8,128)(2,1)S(1)}, u32[]{:S(2)}, u32[]{:S(2)}) collective-permute-start(bf16[4,208,128]{2,1,0:T(8,128)(2,1)S(1)} %get-tuple-element.95), channel_id=1, source_target_pairs={{0,4},{1,5},{2,6},{3,7},{4,0},{5,1},{6,2},{7,3},{8,12},{9,13},{10,... | collective-permute-start | bytes 638984 | tf_op jit(solution)/shard_map/ppermute | solution.py:361
  43.5 8.1 %collective-permute-start.4 = (bf16[4,208,128]{2,1,0:T(8,128)(2,1)S(1)}, bf16[4,208,128]{2,1,0:T(8,128)(2,1)S(1)}, u32[]{:S(2)}, u32[]{:S(2)}) collective-permute-start(bf16[4,208,128]{2,1,0:T(8,128)(2,1)S(1)} %get-tuple-element.96), channel_id=1, source_target_pairs={{0,2},{1,3},{2,0},{3,1},{4,6},{5,7},{6,4},{7,5},{8,10},{9,11},{10,... | collective-permute-start | bytes 638984 | tf_op jit(solution)/shard_map/ppermute | solution.py:361
  44.9 10.5 %collective-permute-start.3 = (bf16[4,208,128]{2,1,0:T(8,128)(2,1)S(1)}, bf16[4,208,128]{2,1,0:T(8,128)(2,1)S(1)}, u32[]{:S(2)}, u32[]{:S(2)}) collective-permute-start(bf16[4,208,128]{2,1,0:T(8,128)(2,1)S(1)} %get-tuple-element.97), channel_id=1, source_target_pairs={{0,6},{1,7},{2,4},{3,5},{4,2},{5,3},{6,0},{7,1},{8,14},{9,15},{10,... | collective-permute-start | bytes 638984 | tf_op jit(solution)/shard_map/ppermute | solution.py:361
  45.9 14.1 %copy-start.3 = (bf16[256,512]{1,0:T(8,128)(2,1)S(1)}, bf16[256,512]{1,0:T(8,128)(2,1)}, u32[]{:S(2)}) copy-start(bf16[256,512]{1,0:T(8,128)(2,1)} %get-tuple-element.77) | copy-start | bytes 786436
  45.9 17.7 %copy-start.2 = (bf16[256,512]{1,0:T(8,128)(2,1)S(1)}, bf16[256,512]{1,0:T(8,128)(2,1)}, u32[]{:S(2)}) copy-start(bf16[256,512]{1,0:T(8,128)(2,1)} %get-tuple-element.78) | copy-start | bytes 786436
  49.0 29.6 %copy-start = (f32[256,512]{1,0:T(8,128)S(1)}, f32[256,512]{1,0:T(8,128)}, u32[]{:S(2)}) copy-start(f32[256,512]{1,0:T(8,128)} %node_grads.1) | copy-start | bytes 1572868
  55.6 8.0 %collective-permute-start.8 = (bf16[208,128]{1,0:T(8,128)(2,1)S(1)}, bf16[208,128]{1,0:T(8,128)(2,1)S(1)}, u32[]{:S(2)}, u32[]{:S(2)}) collective-permute-start(bf16[208,128]{1,0:T(8,128)(2,1)S(1)} %get-tuple-element.98), channel_id=1, source_target_pairs={{0,8},{1,9},{2,10},{3,11},{4,12},{5,13},{6,14},{7,15},{8,0},{9,1},... | collective-permute-start | bytes 159752 | tf_op jit(solution)/shard_map/ppermute | solution.py:361
  56.4 7.2 %collective-permute-start.7 = (bf16[208,128]{1,0:T(8,128)(2,1)S(1)}, bf16[208,128]{1,0:T(8,128)(2,1)S(1)}, u32[]{:S(2)}, u32[]{:S(2)}) collective-permute-start(bf16[208,128]{1,0:T(8,128)(2,1)S(1)} %get-tuple-element.99), channel_id=1, source_target_pairs={{0,16},{1,17},{2,18},{3,19},{4,20},{5,21},{6,22},{7,23},{8,24},{9,... | collective-permute-start | bytes 159752 | tf_op jit(solution)/shard_map/ppermute | solution.py:361
  58.9 6.6 %collective-permute-start.6 = (bf16[208,128]{1,0:T(8,128)(2,1)S(1)}, bf16[208,128]{1,0:T(8,128)(2,1)S(1)}, u32[]{:S(2)}, u32[]{:S(2)}) collective-permute-start(bf16[208,128]{1,0:T(8,128)(2,1)S(1)} %get-tuple-element.100), channel_id=1, source_target_pairs={{0,24},{1,25},{2,26},{3,27},{4,28},{5,29},{6,30},{7,31},{8,16},{9,... | collective-permute-start | bytes 159752 | tf_op jit(solution)/shard_map/ppermute | solution.py:361
  60.0 13.3 %collective-permute-start.12 = (bf16[256,512]{1,0:T(8,128)(2,1)S(1)}, bf16[256,512]{1,0:T(8,128)(2,1)S(1)}, u32[]{:S(2)}, u32[]{:S(2)}) collective-permute-start(bf16[256,512]{1,0:T(8,128)(2,1)S(1)} %copy-done.3), channel_id=1, source_target_pairs={{0,28},{4,0},{8,4},{12,8},{16,12},{20,16},{24,20},{28,24},{1,29},{... | collective-permute-start | bytes 786440 | tf_op jit(solution)/shard_map/ppermute | solution.py:354
  63.6 10.6 %collective-permute-start.13 = (bf16[256,512]{1,0:T(8,128)(2,1)S(1)}, bf16[256,512]{1,0:T(8,128)(2,1)S(1)}, u32[]{:S(2)}, u32[]{:S(2)}) collective-permute-start(bf16[256,512]{1,0:T(8,128)(2,1)S(1)} %copy-done.2), channel_id=1, source_target_pairs={{0,4},{4,8},{8,12},{12,16},{16,20},{20,24},{24,28},{28,0},{1,5},{5... | collective-permute-start | bytes 786440 | tf_op jit(solution)/shard_map/ppermute | solution.py:354
  65.5 5.2 %collective-permute-start.11 = (bf16[208,128]{1,0:T(8,128)(2,1)S(1)}, bf16[208,128]{1,0:T(8,128)(2,1)S(1)}, u32[]{:S(2)}, u32[]{:S(2)}) collective-permute-start(bf16[208,128]{1,0:T(8,128)(2,1)S(1)} %fusion.3), channel_id=1, source_target_pairs={{0,8},{1,9},{2,10},{3,11},{4,12},{5,13},{6,14},{7,15},{8,0},{9,1},... | collective-permute-start | bytes 159752 | tf_op jit(solution)/shard_map/ppermute | solution.py:361
  65.5 7.8 %collective-permute-start.10 = (bf16[208,128]{1,0:T(8,128)(2,1)S(1)}, bf16[208,128]{1,0:T(8,128)(2,1)S(1)}, u32[]{:S(2)}, u32[]{:S(2)}) collective-permute-start(bf16[208,128]{1,0:T(8,128)(2,1)S(1)} %fusion.3), channel_id=1, source_target_pairs={{0,16},{1,17},{2,18},{3,19},{4,20},{5,21},{6,22},{7,23},{8,24},{9,... | collective-permute-start | bytes 159752 | tf_op jit(solution)/shard_map/ppermute | solution.py:361
  66.6 6.7 %collective-permute-start.9 = (bf16[208,128]{1,0:T(8,128)(2,1)S(1)}, bf16[208,128]{1,0:T(8,128)(2,1)S(1)}, u32[]{:S(2)}, u32[]{:S(2)}) collective-permute-start(bf16[208,128]{1,0:T(8,128)(2,1)S(1)} %fusion.3), channel_id=1, source_target_pairs={{0,24},{1,25},{2,26},{3,27},{4,28},{5,29},{6,30},{7,31},{8,16},{9,... | collective-permute-start | bytes 159752 | tf_op jit(solution)/shard_map/ppermute | solution.py:361
  74.2 8.9 %collective-permute-start.16 = (bf16[4,208,128]{2,1,0:T(8,128)(2,1)S(1)}, bf16[4,208,128]{2,1,0:T(8,128)(2,1)S(1)}, u32[]{:S(2)}, u32[]{:S(2)}) collective-permute-start(bf16[4,208,128]{2,1,0:T(8,128)(2,1)S(1)} %pad_maximum_fusion.1), channel_id=1, source_target_pairs={{0,4},{1,5},{2,6},{3,7},{4,0},{5,1},{6,2},{7,3},{8,12},{9,13},{10,... | collective-permute-start | bytes 638984 | tf_op jit(solution)/shard_map/ppermute | solution.py:361
  77.1 6.2 %collective-permute-start.15 = (bf16[4,208,128]{2,1,0:T(8,128)(2,1)S(1)}, bf16[4,208,128]{2,1,0:T(8,128)(2,1)S(1)}, u32[]{:S(2)}, u32[]{:S(2)}) collective-permute-start(bf16[4,208,128]{2,1,0:T(8,128)(2,1)S(1)} %pad_maximum_fusion.1), channel_id=1, source_target_pairs={{0,2},{1,3},{2,0},{3,1},{4,6},{5,7},{6,4},{7,5},{8,10},{9,11},{10,... | collective-permute-start | bytes 638984 | tf_op jit(solution)/shard_map/ppermute | solution.py:361
  78.6 6.8 %collective-permute-start.14 = (bf16[4,208,128]{2,1,0:T(8,128)(2,1)S(1)}, bf16[4,208,128]{2,1,0:T(8,128)(2,1)S(1)}, u32[]{:S(2)}, u32[]{:S(2)}) collective-permute-start(bf16[4,208,128]{2,1,0:T(8,128)(2,1)S(1)} %pad_maximum_fusion.1), channel_id=1, source_target_pairs={{0,6},{1,7},{2,4},{3,5},{4,2},{5,3},{6,0},{7,1},{8,14},{9,15},{10,... | collective-permute-start | bytes 638984 | tf_op jit(solution)/shard_map/ppermute | solution.py:361
  85.5 2.4 %collective-permute-start.17 = (bf16[16,208,128]{2,1,0:T(8,128)(2,1)S(1)}, bf16[16,208,128]{2,1,0:T(8,128)(2,1)S(1)}, u32[]{:S(2)}, u32[]{:S(2)}) collective-permute-start(bf16[16,208,128]{2,1,0:T(8,128)(2,1)S(1)} %pad_maximum_fusion.part_h), channel_id=1, source_target_pairs={{0,1},{1,0},{2,3},{3,2},{4,5},{5,4},{6,7},{7,6},{8,9},{9,8},{10,11... | collective-permute-start | bytes 2555912 | tf_op jit(solution)/shard_map/ppermute | solution.py:361

commit v4 on v3

--- a/solution.py
+++ b/solution.py
@@ -120,22 +120,11 @@
     out.finish()
 
 
-def attention_kernel(blocks, block_rows, score_scale, pat_h, co_h, xl_h, xr_h,
-                     w_h, q_h, k_h, v_h, g_h, virt_h,
-                     out_h, dq_h, left_h, right_h, dkn_h, dvn_h, dko_h, dvo_h,
-                     xl_ref, xr_ref, w_ref, q_ref, g_ref,
-                     key_s, val_s, bias_s, ot_s, dqt_s, out_s, dq_s, dkn_s, dvn_s, dko_s, dvo_s, left_s, right_s, s_s, dw_s, wt_s, ds_s, pat_ref, co_ref, sems):
-    n, width = q_ref.shape
-    virtual_rows, keys = virt_h.shape[1], key_s.shape[0]
+def fill_bias(blocks, block_rows, pat_ref, co_ref, xs_ref, bias_s):
+    n = blocks * block_rows
     loop_here, loop_size, lanes = lax.axis_index("loop"), lax.axis_size("loop"), lax.axis_size("dp")
-    own, virt = pl.ds(n, n), pl.ds(3 * n, virtual_rows)
-    ready = loader((xl_h, xr_h, w_h.at[1], w_h.at[2], k_h, v_h, virt_h.at[1], virt_h.at[2], q_h, g_h, pat_h, co_h),
-                   (xl_ref, xr_ref, w_ref.at[0], w_ref.at[1], key_s.at[own], val_s.at[own],
-                    key_s.at[virt], val_s.at[virt], q_ref, g_ref, pat_ref, co_ref), sems)
-    out = Writer(sems, 12)
     row = lax.broadcasted_iota(jnp.int32, (block_rows, block_rows), 0)
-    bias_s[3 * n:3 * n + virtual_rows, :] = jnp.zeros((virtual_rows, n), F32)
-    ready(0, 1, 10, 11)
+    bias_s[3 * n:, :] = jnp.zeros((bias_s.shape[0] - 3 * n, n), F32)
     for i in range(blocks):
         slots = []
         for j in range(pat_ref.shape[1]):
@@ -147,23 +136,21 @@
             listed = slots[0] == b
             for s in slots[1:]:
                 listed = jnp.logical_or(listed, s == b)
-            at, inner = b // blocks, b % blocks
-            if at == 1:
+            inner = b % blocks
+            first = (0, 2 * n, n)[b // blocks] + inner * block_rows
+            rows = slice(first, first + block_rows)
+            if b // blocks == 1:
                 okb = row < jnp.where(listed, co_ref[inner], 0)
             else:
-                x_ref = (xl_ref, None, xr_ref)[at]
-                mark = x_ref[inner * block_rows:(inner + 1) * block_rows, 0:128].astype(F32)[:, 0:1]
+                mark = xs_ref[rows, 0:128].astype(F32)[:, 0:1]
                 okb = jnp.broadcast_to(mark, (block_rows, block_rows)) < jnp.where(listed, 0.5 * ABSENT, -ABSENT)
-            bias_s[b * block_rows:(b + 1) * block_rows, i * block_rows:(i + 1) * block_rows] = jnp.where(
-                okb, 0.0, NEG_FILL)
-    ready(2, 3)
-    for at, ref in ((0, xl_ref), (2, xr_ref)):
-        x = ref[...]
-        key_s[at * n:(at + 1) * n, :] = nn(x, w_ref[0]).astype(BF)
-        val_s[at * n:(at + 1) * n, :] = nn(x, w_ref[1]).astype(BF)
-    ready(4, 5, 6, 7, 8, 9)
-    ok = own_row_ok(co_ref, blocks, block_rows, (n, 128))
-    for c in range(0, width, 128):
+            bias_s[rows, i * block_rows:(i + 1) * block_rows] = jnp.where(okb, 0.0, NEG_FILL)
+
+
+def attend(ok, score_scale, bias_s, key_s, val_s, q_ref, g_ref, s_s, dw_s, wt_s, ds_s, emit):
+    n, keys = q_ref.shape[0], key_s.shape[0]
+    step = 64
+    for c in range(0, q_ref.shape[1], 128):
         k_pair, v_pair = key_s[:, c:c + 128], val_s[:, c:c + 128]
         q_pair = q_ref[:, c:c + 128]
         g_pair = jnp.where(ok, g_ref[:, c:c + 128], jnp.zeros((n, 128), BF))
@@ -172,67 +159,118 @@
         for half, (qm, gm) in enumerate(masked):
             s_s[half] = nt(k_pair, qm) + bias_s[...]
             dw_s[half] = nt(v_pair, gm)
-        dk_pair = dv_pair = None
+        dk = dv = None
+        out_t, dq_t = [], []
         for half, (qm, gm) in enumerate(masked):
             peak = jnp.full((8, n), NEG_FILL, F32)
-            for r in range(0, keys, 64):
-                peak = jnp.maximum(peak, jnp.max(s_s[half, r:r + 64, :].reshape(64 // 8, 8, n), axis=0))
+            for r in range(0, keys, step):
+                peak = jnp.maximum(peak, jnp.max(s_s[half, r:r + step, :].reshape(step // 8, 8, n), axis=0))
             peak = jnp.max(peak, axis=0, keepdims=True)
             total8 = delta8 = jnp.zeros((8, n), F32)
-            for r in range(0, keys, 64):
-                e = jnp.exp(s_s[half, r:r + 64, :] - peak)
-                s_s[half, r:r + 64, :] = e
-                total8 = total8 + jnp.sum(e.reshape(64 // 8, 8, n), axis=0)
-                delta8 = delta8 + jnp.sum((e * dw_s[half, r:r + 64, :]).reshape(64 // 8, 8, n), axis=0)
+            for r in range(0, keys, step):
+                e = jnp.exp(s_s[half, r:r + step, :] - peak)
+                s_s[half, r:r + step, :] = e
+                total8 = total8 + jnp.sum(e.reshape(step // 8, 8, n), axis=0)
+                delta8 = delta8 + jnp.sum((e * dw_s[half, r:r + step, :]).reshape(step // 8, 8, n), axis=0)
             inv = 1.0 / jnp.sum(total8, axis=0, keepdims=True)
             delta = jnp.sum(delta8, axis=0, keepdims=True) * inv
-            for r in range(0, keys, 64):
-                a = s_s[half, r:r + 64, :] * inv
-                wt_s[half, r:r + 64, :] = a.astype(BF)
-                ds_s[half, r:r + 64, :] = (a * (dw_s[half, r:r + 64, :] - delta)).astype(BF)
+            for r in range(0, keys, step):
+                a = s_s[half, r:r + step, :] * inv
+                wt_s[half, r:r + step, :] = a.astype(BF)
+                ds_s[half, r:r + step, :] = (a * (dw_s[half, r:r + step, :] - delta)).astype(BF)
             wt, ds = wt_s[half], ds_s[half]
-            at = c + half * 64
-            ot_s[at:at + 64, :] = nn(v_t[half * 64:half * 64 + 64], wt)
-            dqt_s[at:at + 64, :] = nn(k_t[half * 64:half * 64 + 64], ds)
-            dk, dv = nn(ds, qm), nn(wt, gm)
-            dk_pair = dk if dk_pair is None else dk_pair + dk
-            dv_pair = dv if dv_pair is None else dv_pair + dv
-        for near, mine, part in ((dkn_s, dko_s, dk_pair), (dvn_s, dvo_s, dv_pair)):
-            near[0:n, c:c + 128] = part[0:n].astype(BF)
-            near[n:2 * n, c:c + 128] = part[2 * n:3 * n].astype(BF)
-            mine[0:n, c:c + 128] = part[n:2 * n]
-            mine[n:n + virtual_rows, c:c + 128] = part[3 * n:3 * n + virtual_rows]
-        dq_s[:, c:c + 128] = (dqt_s[c:c + 128, :] * score_scale).astype(BF).T
-        out_s[:, c:c + 128] = jnp.where(ok, ot_s[c:c + 128, :].astype(BF).T, jnp.zeros((n, 128), BF))
-        cols = pl.ds(c, 128)
-        for src, dst in ((dkn_s, dkn_h), (dvn_s, dvn_h), (dko_s, dko_h), (dvo_s, dvo_h), (dq_s, dq_h), (out_s, out_h)):
-            out.send(src.at[:, cols], dst.at[:, cols])
-    for rows, ref, dst in ((slice(0, n), left_s, left_h), (slice(n, 2 * n), right_s, right_h)):
-        ref[...] = (nt(dkn_s[rows, :], w_ref[0]) + nt(dvn_s[rows, :], w_ref[1])).astype(BF)
-        out.send(ref, dst)
+            out_t.append(nn(v_t[half * 64:half * 64 + 64], wt))
+            dq_t.append(nn(k_t[half * 64:half * 64 + 64], ds))
+            dk_half, dv_half = nn(ds, qm), nn(wt, gm)
+            dk = dk_half if dk is None else dk + dk_half
+            dv = dv_half if dv is None else dv + dv_half
+        dq = (jnp.concatenate(dq_t, axis=0) * score_scale).astype(BF).T
+        mixture = jnp.concatenate(out_t, axis=0).astype(BF).T
+        emit(c, dk, dv, dq, jnp.where(ok, mixture, jnp.zeros((n, 128), BF)))
+
+
+def low_kernel(blocks, block_rows, score_scale, pat_h, co_h, xl_h, xr_h, w_h, q_h, k_h, v_h, g_h, virt_h,
+               out_h, dq_h, dkn_h, dvn_h, dko_h, dvo_h,
+               xs_ref, w_ref, q_ref, g_ref, key_s, val_s, bias_s, s_s, dw_s, wt_s, ds_s,
+               out_s, dq_s, dkn_s, dvn_s, dko_s, dvo_s, pat_ref, co_ref, sems):
+    n, part = q_ref.shape
+    cols = pl.ds(0, part)
+    own, last = pl.ds(2 * n, n), pl.ds(3 * n, virt_h.shape[1])
+    ready = loader((xl_h, xr_h, pat_h, co_h, w_h.at[1, :, cols], w_h.at[2, :, cols],
+                    k_h.at[:, cols], v_h.at[:, cols], virt_h.at[1, :, cols], virt_h.at[2, :, cols],
+                    q_h.at[:, cols], g_h.at[:, cols]),
+                   (xs_ref.at[pl.ds(0, n)], xs_ref.at[pl.ds(n, n)], pat_ref, co_ref, w_ref.at[0], w_ref.at[1],
+                    key_s.at[own], val_s.at[own], key_s.at[last], val_s.at[last], q_ref, g_ref), sems)
+    out = Writer(sems, 12)
+    ready(0, 1, 2, 3)
+    fill_bias(blocks, block_rows, pat_ref, co_ref, xs_ref, bias_s)
+    ready(4, 5)
+    key_s[0:2 * n, :] = nn(xs_ref[...], w_ref[0]).astype(BF)
+    val_s[0:2 * n, :] = nn(xs_ref[...], w_ref[1]).astype(BF)
+    ready(6, 7, 8, 9, 10, 11)
+    ok = own_row_ok(co_ref, blocks, block_rows, (n, 128))
+
+    def emit(c, dk, dv, dq, mixture):
+        here = pl.ds(c, 128)
+        for value, ref, dst in ((dk[0:2 * n].astype(BF), dkn_s, dkn_h), (dv[0:2 * n].astype(BF), dvn_s, dvn_h),
+                                (dk[2 * n:], dko_s, dko_h), (dv[2 * n:], dvo_s, dvo_h),
+                                (dq, dq_s, dq_h), (mixture, out_s, out_h)):
+            ref[:, c:c + 128] = value
+            out.send(ref.at[:, here], dst.at[:, here])
+
+    attend(ok, score_scale, bias_s, key_s, val_s, q_ref, g_ref, s_s, dw_s, wt_s, ds_s, emit)
     out.finish()
 
 
-def weight_kernel(blocks, block_rows, score_scale, counts_h, x_h, xl_h, xr_h, vs_h, vcot_h, w_h,
-                  k_h, v_h, virt_h, stats_h, dq_h, dkn_h, dvn_h, dko_h, dvo_h,
-                  keep_h, send_h, kown_h, vown_h,
-                  xs_ref, vcot_ref, w_ref, k_ref, v_ref, virt_ref, stats_ref, dko_ref, dvo_ref,
-                  xt_s, dqw_s, dkw_s, dvw_s, pack_s, counts_ref, sems):
+def high_kernel(blocks, block_rows, score_scale, pat_h, co_h, xl_h, xr_h, x_h, w_h, q_h, k_h, v_h, g_h, virt_h,
+                vs_h, vcot_h, stats_h, dq_low_h, dkn_low_h, dvn_low_h, dko_low_h, dvo_low_h, out_low_h,
+                out_h, send_h, keep_h, dq_h, dk_h, dv_h,
+                xs_ref, w_ref, q_ref, g_ref, k_ref, v_ref, virt_ref, vcot_ref, stats_ref,
+                key_s, val_s, bias_s, s_s, dw_s, wt_s, ds_s,
+                out_s, dko_s, dvo_s, xt_s, dqw_s, dkw_s, dvw_s, pack_s, pat_ref, co_ref, sems):
     n, width = x_h.shape
+    part = q_ref.shape[1]
     virtual_rows = vs_h.shape[0]
+    low, high = pl.ds(0, width - part), pl.ds(width - part, part)
     near, own, last = pl.ds(0, 2 * n), pl.ds(2 * n, n), pl.ds(3 * n, virtual_rows)
-    ready = loader((xl_h, xr_h, x_h, vs_h, stats_h, counts_h, k_h, v_h, virt_h.at[0], vcot_h, dko_h, dvo_h,
-                    dq_h, dkn_h, dvn_h, w_h),
-                   (xs_ref.at[pl.ds(0, n)], xs_ref.at[pl.ds(n, n)], xs_ref.at[own], xs_ref.at[last], stats_ref, counts_ref,
-                    k_ref, v_ref, virt_ref, vcot_ref, dko_ref, dvo_ref,
-                    dqw_s.at[pl.ds(0, n)], dkw_s.at[near], dvw_s.at[near], w_ref), sems)
-    out = Writer(sems, 16)
-    pairs = width // 128
+    first = pl.ds(0, n)
+    ready = loader((xl_h, xr_h, pat_h, co_h, w_h.at[1], w_h.at[2],
+                    k_h.at[:, high], v_h.at[:, high], virt_h.at[1, :, high], virt_h.at[2, :, high],
+                    q_h.at[:, high], g_h.at[:, high],
+                    x_h, vs_h, w_h.at[0], k_h, v_h, virt_h.at[0], vcot_h, stats_h,
+                    dq_low_h, dkn_low_h, dvn_low_h, dko_low_h, dvo_low_h),
+                   (xs_ref.at[pl.ds(0, n)], xs_ref.at[pl.ds(n, n)], pat_ref, co_ref, w_ref.at[1], w_ref.at[2],
+                    key_s.at[own], val_s.at[own], key_s.at[last], val_s.at[last], q_ref, g_ref,
+                    xs_ref.at[own], xs_ref.at[last], w_ref.at[0], k_ref, v_ref, virt_ref, vcot_ref, stats_ref,
+                    dqw_s.at[first, low], dkw_s.at[near, low], dvw_s.at[near, low], dko_s.at[:, low], dvo_s.at[:, low]),
+                   sems)
+    out = Writer(sems, 25)
     ready(0, 1, 2, 3)
+    fill_bias(blocks, block_rows, pat_ref, co_ref, xs_ref, bias_s)
+    ready(4, 5)
+    key_s[0:2 * n, :] = nn(xs_ref[0:2 * n, :], w_ref[1, :, width - part:]).astype(BF)
+    val_s[0:2 * n, :] = nn(xs_ref[0:2 * n, :], w_ref[2, :, width - part:]).astype(BF)
+    ready(6, 7, 8, 9, 10, 11, 12, 13)
+    ok = own_row_ok(co_ref, blocks, block_rows, (n, 128))
     for c in range(0, width, 128):
         xt_s[c:c + 128, :] = xs_ref[:, c:c + 128].T
-    ready(4, 5)
-    ok = own_row_ok(counts_ref, blocks, block_rows, (n, 128))
+
+    def emit(c, dk, dv, dq, mixture):
+        here = slice(width - part + c, width - part + c + 128)
+        dkw_s[0:2 * n, here] = dk[0:2 * n].astype(BF)
+        dvw_s[0:2 * n, here] = dv[0:2 * n].astype(BF)
+        dko_s[:, here] = dk[2 * n:]
+        dvo_s[:, here] = dv[2 * n:]
+        dqw_s[0:n, here] = dq
+        out_s[:, c:c + 128] = mixture
+        out.send(out_s.at[:, pl.ds(c, 128)], out_h.at[:, pl.ds(width - part + c, 128)])
+
+    attend(ok, score_scale, bias_s, key_s, val_s, q_ref, g_ref, s_s, dw_s, wt_s, ds_s, emit)
+    ready(*range(14, 25))
+    out.send(dkw_s.at[near], dk_h.at[near])
+    out.send(dvw_s.at[near], dv_h.at[near])
+    out.send(dqw_s.at[first], dq_h)
+    pairs = width // 128
     stats = stats_ref[...]
     peak = jnp.max(stats[:, 0:pairs], axis=0)
     factor = jnp.exp(stats[:, 0:pairs] - peak[None])
@@ -244,7 +282,6 @@
     def diagonal(square):
         return jnp.where(lane_low, square[:virtual_rows], square[virtual_rows:])
 
-    ready(6, 7, 8, 9, 10, 11)
     mixed = []
     for p in range(pairs):
         c = p * 128
@@ -258,13 +295,12 @@
         ds = (attn * (dw - delta[p:p + 1]) * score_scale).astype(BF)
         mixed.append(diagonal(tn(attn_bf, v_pair)))
         dqw_s[n:n + virtual_rows, c:c + 128] = diagonal(tn(ds, k_pair)).astype(BF)
-        dkw_s[2 * n:3 * n, c:c + 128] = (dko_ref[0:n, c:c + 128] + nn(ds, vq)).astype(BF)
-        dvw_s[2 * n:3 * n, c:c + 128] = (dvo_ref[0:n, c:c + 128] + nn(attn_bf, vcot)).astype(BF)
-    dkw_s[3 * n:3 * n + virtual_rows, :] = dko_ref[n:n + virtual_rows, :].astype(BF)
-    dvw_s[3 * n:3 * n + virtual_rows, :] = dvo_ref[n:n + virtual_rows, :].astype(BF)
-    out.send(dkw_s.at[own], kown_h)
-    out.send(dvw_s.at[own], vown_h)
-    ready(12, 13, 14)
+        dkw_s[2 * n:3 * n, c:c + 128] = (dko_s[0:n, c:c + 128] + nn(ds, vq)).astype(BF)
+        dvw_s[2 * n:3 * n, c:c + 128] = (dvo_s[0:n, c:c + 128] + nn(attn_bf, vcot)).astype(BF)
+    dkw_s[3 * n:3 * n + virtual_rows, :] = dko_s[n:n + virtual_rows, :].astype(BF)
+    dvw_s[3 * n:3 * n + virtual_rows, :] = dvo_s[n:n + virtual_rows, :].astype(BF)
+    out.send(dkw_s.at[own], dk_h.at[own])
+    out.send(dvw_s.at[own], dv_h.at[own])
     me = place()
     row_groups = width // 64
     for c in range(0, width, 256):
@@ -277,7 +313,6 @@
                 for group in range(row_groups):
                     at = jnp.bitwise_xor(me, (c + col) // 128 * row_groups + group)
                     pack_s[at, t * 64:(t + 1) * 64, :] = wg[group * 64:(group + 1) * 64, col:col + 128].astype(BF)
-    ready(15)
     vg = (nt(dqw_s[n:n + virtual_rows, :], w_ref[0]) + nt(dkw_s[3 * n:3 * n + virtual_rows, :], w_ref[1])
           + nt(dvw_s[3 * n:3 * n + virtual_rows, :], w_ref[2]))
     for p in range(pairs):
@@ -291,12 +326,19 @@
     out.finish()
 
 
-def node_kernel(w_h, dq_h, dk_h, dv_h, part_h, w_ref, dq_ref, dk_ref, dv_ref, part_s, sems):
+def node_kernel(w_h, dq_h, dk_h, dv_h, left_h, right_h, part_h, w_ref, dq_ref, dk_ref, dv_ref,
+                left_s, right_s, part_s, sems):
+    n = dq_ref.shape[0]
     ready = loader((w_h, dq_h, dk_h, dv_h), (w_ref, dq_ref, dk_ref, dv_ref), sems)
     out = Writer(sems, 4)
     ready(0, 1, 2, 3)
-    part_s[...] = nt(dq_ref[...], w_ref[0]) + nt(dk_ref[...], w_ref[1]) + nt(dv_ref[...], w_ref[2])
-    out.send(part_s, part_h)
+    for at, ref, dst in ((0, left_s, left_h), (1, right_s, right_h), (2, part_s, part_h)):
+        rows = slice(at * n, (at + 1) * n)
+        grad = nt(dk_ref[rows, :], w_ref[1]) + nt(dv_ref[rows, :], w_ref[2])
+        if at == 2:
+            grad = grad + nt(dq_ref[...], w_ref[0])
+        ref[...] = grad.astype(ref.dtype)
+        out.send(ref, dst)
     out.finish()
 
 
@@ -365,8 +407,22 @@
     return lax.optimization_barrier(tree)
 
 
-PLANE = ((1, 2), (0, 2), (1, 0))
-LINE = ((6, 0), (4, 0), (2, 0))
+PLANE = ((3, 1, 2), (1, 1, 0), (2, 0, 2))
+LINE = ((3, 6, 0), (2, 4, 0), (1, 2, 0))
+
+
+def scatter(held, links):
+    rows = held.shape[0] // 4
+    return [swap(held[at * rows:(at + 1) * rows], *bits) for at, *bits in links]
+
+
+def gather(held, links):
+    return [swap(held, *bits) for _, *bits in links]
+
+
+def in_order(held, got, links):
+    parts = dict(zip([at for at, *_ in links], got))
+    return jnp.concatenate([held] + [parts[at] for at in (1, 2, 3)], axis=0)
 
 
 def total(parts):
@@ -380,22 +436,20 @@
     loop_size = lax.axis_size("loop")
     held = total([keep, swap(send, 0, 1)])
     held = together(held)
-    quarters = [held[4 * j:4 * j + 4] for j in range(4)]
-    got = [swap(quarters[3 - j], *bits) for j, bits in enumerate(PLANE)]
-    got, own_part = together((got, own_part))
-    held, to_left, to_right = together((total([quarters[0]] + got), to_left, to_right))
+    got, own_part, to_left, to_right = together((scatter(held, PLANE), own_part, to_left, to_right))
+    held, to_left, to_right = together((total([held[:held.shape[0] // 4]] + got), to_left, to_right))
     from_right, from_left = ring(to_left, -1), ring(to_right, 1)
-    got = together([swap(held[3 - j], *bits) for j, bits in enumerate(LINE)])
-    piece = total([held[0]] + got)
+    got = together(scatter(held, LINE))
+    piece = total([held[:1]] + got)
     bit = 8
     while bit < loop_size:
         piece = total([piece, swap(piece, bit, 0)])
         bit *= 2
     piece = together(piece)
-    got, from_right, from_left = together(([swap(piece, *bits) for bits in LINE], from_right, from_left))
-    held = together(jnp.stack([piece] + got[::-1]))
-    got, node_grad = together(([swap(held, *bits) for bits in PLANE], total([own_part, from_right, from_left])))
-    held = together(jnp.concatenate([held] + got[::-1], axis=0))
+    got, from_right, from_left = together((gather(piece, LINE), from_right, from_left))
+    held = together(in_order(piece, got, LINE))
+    got, node_grad = together((gather(held, PLANE), total([own_part, from_right, from_left])))
+    held = together(in_order(held, got, PLANE))
     return held, swap(held, 0, 1), node_grad
 
 
@@ -428,30 +482,34 @@
         [rows_bf, wide, virt_bf, virt_bf] + [rows_bf] * 3 + [triple, stats_f, counts_i], 12, name="project")
     stats = lax.all_to_all(stats, ("loop", "dp"), 0, 0, tiled=True)
 
-    keys_bf = ((keys, width), BF)
-    across = ((width, n), F32)
-    near_bf, mine_f = ((2 * n, width), BF), ((n + virtual_rows, width), F32)
-    node_out, dq, to_left, to_right, dkn, dvn, dko, dvo = call(
-        functools.partial(attention_kernel, blocks, block_rows, score_scale),
-        (pattern, valid_counts, x_left, x_right, projection, q, k, v, node_cotangent, virt),
-        [rows_bf] * 4 + [near_bf] * 2 + [mine_f] * 2,
-        [rows_bf] * 2 + [((2, width, width), BF)] + [rows_bf] * 2
-        + [keys_bf] * 2 + [((keys, n), F32), across, across] + [rows_bf] * 2 + [near_bf] * 2 + [mine_f] * 2 + [rows_bf] * 2
-        + [((2, keys, n), F32)] * 2 + [((2, keys, n), BF)] * 2 + [pattern_i, counts_i], 40,
-        flops=4e9, name="attention")
-    to_left, to_right, stats = together((to_left, to_right, stats))
-
+    part, rest = width // 4 * 3, width // 4
+    keys_bf, keys_part, keys_rest = ((keys, width), BF), ((keys, part), BF), ((keys, rest), BF)
+    rows_rest = ((n, rest), BF)
+    rows_part, near_part, mine_part = ((n, part), BF), ((2 * n, part), BF), ((n + virtual_rows, part), F32)
+    mine_f = ((n + virtual_rows, width), F32)
+    passes = [((keys, n), F32)] + [((2, keys, n), F32)] * 2 + [((2, keys, n), BF)] * 2
+    window = (pattern, valid_counts, x_left, x_right)
+    half_out, *low = call(
+        functools.partial(low_kernel, blocks, block_rows, score_scale),
+        (*window, projection, q, k, v, node_cotangent, virt),
+        [rows_bf, rows_part, near_part, near_part, mine_part, mine_part],
+        [((2 * n, width), BF), ((2, width, part), BF), rows_part, rows_part, keys_part, keys_part] + passes
+        + [rows_part, rows_part, near_part, near_part, mine_part, mine_part, pattern_i, counts_i], 30,
+        flops=1e10, name="attention_low")
     half = ((SHARDS // 2, 3 * 64 + 16, 128), BF)
-    keep, send, dk, dv = call(
-        functools.partial(weight_kernel, blocks, block_rows, score_scale),
-        (valid_counts, node_states, x_left, x_right, virtual_states, virtual_cotangent, projection, k, v, virt, stats,
-         dq, dkn, dvn, dko, dvo),
-        [half] * 2 + [rows_bf] * 2,
-        [keys_bf, virt_bf, wide, rows_bf, rows_bf, virt_bf, stats_f, mine_f, mine_f,
-         ((width, keys), BF), ((n + virtual_rows, width), BF), keys_bf, keys_bf, ((SHARDS, 3 * 64 + 16, 128), BF), counts_i], 20,
-        flops=8e9, name="weight_grads")
-    own_part, = call(node_kernel, (projection, dq, dk, dv), [rows_f], [wide] + [rows_bf] * 3 + [rows_f], 5,
-                     flops=1e9, name="node_grads")
+    window_bf = ((3 * n, width), BF)
+    node_out, send, keep, dq, dk, dv = call(
+        functools.partial(high_kernel, blocks, block_rows, score_scale),
+        (*window, node_states, projection, q, k, v, node_cotangent, virt, virtual_states, virtual_cotangent, stats, *low,
+         half_out),
+        [rows_bf, half, half, rows_bf, window_bf, window_bf],
+        [keys_bf, wide, rows_rest, rows_rest, rows_bf, rows_bf, virt_bf, virt_bf, stats_f, keys_rest, keys_rest] + passes
+        + [rows_rest, mine_f, mine_f, ((width, keys), BF), ((n + virtual_rows, width), BF), keys_bf, keys_bf,
+           ((SHARDS, 3 * 64 + 16, 128), BF), pattern_i, counts_i], 36,
+        flops=1e10, name="attention_high", aliases={19: 0})
+    to_left, to_right, own_part = call(
+        node_kernel, (projection, dq, dk, dv), [rows_bf, rows_bf, rows_f],
+        [wide, rows_bf, window_bf, window_bf, rows_bf, rows_bf, rows_f], 7, flops=1e9, name="node_grads")
     mine, other, node_grad = reduce_all(keep, send, own_part, to_left, to_right)
     halves_f = ((virtual_rows, width // 2), F32)
     unpack = functools.partial(

time: 90.4 us -> 89.5 us (0.990)
    ppermute x14, waiting for transfers between devices: 21.1 us -> 20 us  [swap(): lax.ppermute(value, ('loop', 'dp'), [(s, s ^ other) for s in range(count)])]
  transfers between devices with their start and end apart: 19 -> 19, of which waited for: 13 -> 13; matrix products, arithmetic and copies ran while one was open for 1% -> 1% of each run, Pallas kernels for 21% -> 19%
where the time goes in v4:
time: 89.5 us; the launch traced here: 88.7 us
  starting transfers between devices  32.6 us (36%)
  Pallas kernels  27.1 us (30%)
  waiting for transfers between devices  22.4 us (25%)
  other arithmetic  4.27 us (5%)
  local copies, waits for them, and re-layouts  1.55 us (2%)
    pallas_call x6, Pallas kernels, call(): pl.pallas_call(body, out_shape=[jax.ShapeDtypeStruct(s, d) for s, d in ou...  27.1 us
    ppermute x14, waiting for transfers between devices, swap(): lax.ppermute(value, ('loop', 'dp'), [(s, s ^ other) for s in range(count)])  20 us
    ppermute x14, starting transfers between devices, swap(): lax.ppermute(value, ('loop', 'dp'), [(s, s ^ other) for s in range(count)])  16.9 us
    ppermute x4, starting transfers between devices, ring(): lax.ppermute(value, 'loop', [(s, (s + steps) % count) for s in range(coun...  9.64 us
    all_to_all x1, starting transfers between devices, local(): stats = lax.all_to_all(stats, ('loop', 'dp'), 0, 0, tiled=True)  6.02 us
    convert_element_type x4, other arithmetic, total(): return summed.astype(BF)  2.34 us
    ppermute x4, waiting for transfers between devices, ring(): lax.ppermute(value, 'loop', [(s, (s + steps) % count) for s in range(coun...  2.08 us
  transfers between devices with their start and end apart: 19, of which 13 were waited for; matrix products, arithmetic and copies ran while one was open for 1% of the time, Pallas kernels for 19%

profile of v4, /device:TPU:0, one launch (start us, length us, event | category | flops | bytes accessed | tf_op | source)
XLA Modules:
  0.0 88.7 jit_solution(12886073007641412807)
XLA Ops:
  0.6 0.7 broadcast_multiply_fusion
  1.3 0.1 broadcast_bitcast_fusion.1
  1.4 1.1 %fusion = bf16[256,512]{1,0:T(8,128)(2,1)S(1)} fusion(bf16[256,512]{1,0:T(8,128)(2,1)} %x_h.3, s32[256]{0:T(256)S(1)} %broadcast_bitcast_fusion.1, s32[256]{0:T(256)S(1)} %broadcast_bitcast_fusion), kind=kLoop, calls=%fused_computation.4 | loop fusion | flops 393216 | bytes 526336 | tf_op jit(solution)/shard_map/jit(_where)/select_n | solution.py:469
  2.5 6.1 %collective-permute-start.1 = (bf16[256,512]{1,0:T(8,128)(2,1)S(1)}, bf16[256,512]{1,0:T(8,128)(2,1)S(1)}, u32[]{:S(2)}, u32[]{:S(2)}) collective-permute-start(bf16[256,512]{1,0:T(8,128)(2,1)S(1)} %fusion), channel_id=1, source_target_pairs={{0,28},{4,0},{8,4},{12,8},{16,12},{20,16},{24,20},{28,24},{1,29},{... | collective-permute-start | bytes 786440 | tf_op jit(solution)/shard_map/ppermute | solution.py:396
  8.6 0.0 collective-permute-start
  8.6 3.3 %project.1 = (bf16[256,512]{1,0:T(8,128)(2,1)}, bf16[256,512]{1,0:T(8,128)(2,1)}, bf16[256,512]{1,0:T(8,128)(2,1)}, bf16[3,64,512]{2,1,0:T(8,128)(2,1)}, f32[32,16,128]{2,1,0:T(8,128)}) custom-call(s32[2]{0:T(128)} %co_h.3, bf16[256,512]{1,0:T(8,128)(2,1)} %x_h.3, bf16[3,512,512]{2,1,0:T(8,128)(2,1)} %w_h.7, bf16[64,512]{1,0:T(8,128)(2,1)} %vs_h.3, ...), custom_call_target="tpu_custom_call" | custom-call | flops 100000000 | bytes 4194304 | tf_op jit(solution)/shard_map/project/pallas_call | solution.py:381
  11.9 6.0 %all-to-all-start = ((f32[32,16,128]{2,1,0:T(8,128)}), f32[32,16,128]{2,1,0:T(8,128)S(1)}, u32[]{:S(2)}, u32[]{:S(2)}) async-start(f32[32,16,128]{2,1,0:T(8,128)} %get-tuple-element.56), calls=%async_computation | async-start | bytes 524288 | tf_op jit(solution)/shard_map/all_to_all | solution.py:483
  18.0 0.0 collective-permute-done.1.xr_h
  18.0 0.0 copy-start.2
  18.0 1.1 %collective-permute-done.xl_h = bf16[256,512]{1,0:T(8,128)(2,1)S(1)} collective-permute-done((bf16[256,512]{1,0:T(8,128)(2,1)S(1)}, bf16[256,512]{1,0:T(8,128)(2,1)S(1)}, u32[]{:S(2)}, u32[]{:S(2)}) %collective-permute-start) | collective-permute-done | bytes 262176 | tf_op jit(solution)/shard_map/ppermute | solution.py:396
  19.0 0.0 copy-start.3
  19.0 0.0 copy-done.2
  19.0 0.7 copy-done.3
  19.7 8.5 %attention_low.1 = (bf16[256,512]{1,0:T(8,128)(2,1)}, bf16[256,384]{1,0:T(8,128)(2,1)}, bf16[512,384]{1,0:T(8,128)(2,1)}, bf16[512,384]{1,0:T(8,128)(2,1)}, f32[320,384]{1,0:T(8,128)}, /*index=5*/f32[320,384]{1,0:T(8,128)}) custom-call(s32[2,5]{1,0:T(2,128)} %pat_h.3, s32[2]{0:T(128)} %co_h.3, bf16[256,512]{1,0:T(8,128)(2,1)} %copy-done.3, ...), custom_call_target="tpu_custom_call" | custom-call | flops 10000000000 | bytes 4194304 | tf_op jit(solution)/shard_map/attention_low/pallas_call | solution.py:381
  28.2 0.3 all-to-all-done.stats_h
  28.5 0.0 copy-start.1
  28.6 0.7 copy-done.1
  29.3 8.4 %attention_high.1 = (bf16[256,512]{1,0:T(8,128)(2,1)}, bf16[16,208,128]{2,1,0:T(8,128)(2,1)}, bf16[16,208,128]{2,1,0:T(8,128)(2,1)}, bf16[256,512]{1,0:T(8,128)(...) custom-call(s32[2,5]{1,0:T(2,128)} %pat_h.3, s32[2]{0:T(128)} %co_h.3, ...), custom_call_target="tpu_custom_call", output_to_operand_aliasing={{0}: (19, {})} | custom-call | flops 10000000000 | bytes 4194304 | tf_op jit(solution)/shard_map/attention_high/pallas_call | solution.py:381
  37.7 0.1 collective-permute-start.2
  37.7 2.6 %collective-permute-done.2 = bf16[16,208,128]{2,1,0:T(8,128)(2,1)S(1)} collective-permute-done((bf16[16,208,128]{2,1,0:T(8,128)(2,1)}, bf16[16,208,128]{2,1,0:T(8,128)(2,1)S(1)}, u32[]{:S(2)}, u32[]{:S(2)}) %collective-permute-start.2) | collective-permute-done | bytes 852000 | tf_op jit(solution)/shard_map/ppermute | solution.py:403
  40.3 1.4 %add_convert_fusion = bf16[16,208,128]{2,1,0:T(8,128)(2,1)S(1)} fusion(bf16[16,208,128]{2,1,0:T(8,128)(2,1)S(1)} %collective-permute-done.2, bf16[16,208,128]{2,1,0:T(8,128)(2,1)} %get-tuple-element.64), kind=kLoop, calls=%fused_computation | loop fusion | flops 1703936 | bytes 2555904 | tf_op jit(solution)/shard_map/convert_element_type | solution.py:432
  41.7 1.2 %collective-permute-start.5 = (bf16[4,208,128]{2,1,0:T(8,128)(2,1)S(1)}, bf16[4,208,128]{2,1,0:T(8,128)(2,1)S(1)}, u32[]{:S(2)}, u32[]{:S(2)}) collective-permute-start(bf16[4,208,128]{2,1,0:T(8,128)(2,1)S(1)} %get-tuple-element.99), channel_id=1, source_target_pairs={{0,2},{1,3},{2,0},{3,1},{4,6},{5,7},{6,4},{7,5},{8,10},{9,11},{10,... | collective-permute-start | bytes 638984 | tf_op jit(solution)/shard_map/ppermute | solution.py:403
  42.9 1.1 %collective-permute-start.4 = (bf16[4,208,128]{2,1,0:T(8,128)(2,1)S(1)}, bf16[4,208,128]{2,1,0:T(8,128)(2,1)S(1)}, u32[]{:S(2)}, u32[]{:S(2)}) collective-permute-start(bf16[4,208,128]{2,1,0:T(8,128)(2,1)S(1)} %get-tuple-element.100), channel_id=1, source_target_pairs={{0,4},{1,5},{2,6},{3,7},{4,0},{5,1},{6,2},{7,3},{8,12},{9,13},{10,... | collective-permute-start | bytes 638984 | tf_op jit(solution)/shard_map/ppermute | solution.py:403
  44.0 1.3 %collective-permute-start.3 = (bf16[4,208,128]{2,1,0:T(8,128)(2,1)S(1)}, bf16[4,208,128]{2,1,0:T(8,128)(2,1)S(1)}, u32[]{:S(2)}, u32[]{:S(2)}) collective-permute-start(bf16[4,208,128]{2,1,0:T(8,128)(2,1)S(1)} %get-tuple-element.101), channel_id=1, source_target_pairs={{0,6},{1,7},{2,4},{3,5},{4,2},{5,3},{6,0},{7,1},{8,14},{9,15},{10,... | collective-permute-start | bytes 638984 | tf_op jit(solution)/shard_map/ppermute | solution.py:403
  45.3 3.9 %node_grads.1 = (bf16[256,512]{1,0:T(8,128)(2,1)}, bf16[256,512]{1,0:T(8,128)(2,1)}, f32[256,512]{1,0:T(8,128)}) custom-call(bf16[3,512,512]{2,1,0:T(8,128)(2,1)} %w_h.7, bf16[256,512]{1,0:T(8,128)(2,1)} %get-tuple-element.66.dq_h, bf16[768,512]{1,0:T(8,128)(2,1)} %get-tuple-element.67.dk_h, bf16[768,512]{1,0:T(8,128)(2,1)} %get-tuple-element.68.dv_h), custom_call_target="tpu_custom_call" | custom-call | flops 1000000000 | bytes 4194304 | tf_op jit(solution)/shard_map/node_grads/pallas_call | solution.py:381
  49.2 0.0 copy-start
  49.2 0.7 collective-permute-done.5
  49.9 4.6 %collective-permute-done.4 = bf16[4,208,128]{2,1,0:T(8,128)(2,1)S(1)} collective-permute-done((bf16[4,208,128]{2,1,0:T(8,128)(2,1)S(1)}, bf16[4,208,128]{2,1,0:T(8,128)(2,1)S(1)}, u32[]{:S(2)}, u32[]{:S(2)}) %collective-permute-start.4) | collective-permute-done | bytes 213024 | tf_op jit(solution)/shard_map/ppermute | solution.py:403
  54.5 0.0 collective-permute-done.3
  54.5 0.1 add_convert_fusion.2
  54.7 0.8 collective-permute-start.8
  55.5 2.4 %collective-permute-start.7 = (bf16[1,208,128]{2,1,0:T(8,128)(2,1)S(1)}, bf16[1,208,128]{2,1,0:T(8,128)(2,1)S(1)}, u32[]{:S(2)}, u32[]{:S(2)}) collective-permute-start(bf16[1,208,128]{2,1,0:T(8,128)(2,1)S(1)} %get-tuple-element.103), channel_id=1, source_target_pairs={{0,16},{1,17},{2,18},{3,19},{4,20},{5,21},{6,22},{7,23},{8,24},{9,... | collective-permute-start | bytes 159752 | tf_op jit(solution)/shard_map/ppermute | solution.py:403
  57.9 1.2 %collective-permute-start.6 = (bf16[1,208,128]{2,1,0:T(8,128)(2,1)S(1)}, bf16[1,208,128]{2,1,0:T(8,128)(2,1)S(1)}, u32[]{:S(2)}, u32[]{:S(2)}) collective-permute-start(bf16[1,208,128]{2,1,0:T(8,128)(2,1)S(1)} %get-tuple-element.104), channel_id=1, source_target_pairs={{0,24},{1,25},{2,26},{3,27},{4,28},{5,29},{6,30},{7,31},{8,16},{9,... | collective-permute-start | bytes 159752 | tf_op jit(solution)/shard_map/ppermute | solution.py:403
  59.1 3.6 %collective-permute-start.12 = (bf16[256,512]{1,0:T(8,128)(2,1)}, bf16[256,512]{1,0:T(8,128)(2,1)S(1)}, u32[]{:S(2)}, u32[]{:S(2)}) collective-permute-start(bf16[256,512]{1,0:T(8,128)(2,1)} %get-tuple-element.81), channel_id=1, source_target_pairs={{0,28},{4,0},{8,4},{12,8},{16,12},{20,16},{24,20},{28,24},{1,29},{... | collective-permute-start | bytes 786440 | tf_op jit(solution)/shard_map/ppermute | solution.py:396
  62.7 0.0 collective-permute-start.13
  62.7 0.0 collective-permute-done.8
  62.7 0.0 collective-permute-done.7
  62.7 1.8 %collective-permute-done.6 = bf16[1,208,128]{2,1,0:T(8,128)(2,1)S(1)} collective-permute-done((bf16[1,208,128]{2,1,0:T(8,128)(2,1)S(1)}, bf16[1,208,128]{2,1,0:T(8,128)(2,1)S(1)}, u32[]{:S(2)}, u32[]{:S(2)}) %collective-permute-start.6) | collective-permute-done | bytes 53280 | tf_op jit(solution)/shard_map/ppermute | solution.py:403
  64.5 0.1 collective-permute-start.11
  64.6 1.1 %collective-permute-start.10 = (bf16[1,208,128]{2,1,0:T(8,128)(2,1)S(1)}, bf16[1,208,128]{2,1,0:T(8,128)(2,1)S(1)}, u32[]{:S(2)}, u32[]{:S(2)}) collective-permute-start(bf16[1,208,128]{2,1,0:T(8,128)(2,1)S(1)} %add_convert_fusion.3), channel_id=1, source_target_pairs={{0,16},{1,17},{2,18},{3,19},{4,20},{5,21},{6,22},{7,23},{8,24},{9,... | collective-permute-start | bytes 159752 | tf_op jit(solution)/shard_map/ppermute | solution.py:403
  65.7 3.3 %collective-permute-start.9 = (bf16[1,208,128]{2,1,0:T(8,128)(2,1)S(1)}, bf16[1,208,128]{2,1,0:T(8,128)(2,1)S(1)}, u32[]{:S(2)}, u32[]{:S(2)}) collective-permute-start(bf16[1,208,128]{2,1,0:T(8,128)(2,1)S(1)} %add_convert_fusion.3), channel_id=1, source_target_pairs={{0,24},{1,25},{2,26},{3,27},{4,28},{5,29},{6,30},{7,31},{8,16},{9,... | collective-permute-start | bytes 159752 | tf_op jit(solution)/shard_map/ppermute | solution.py:403
  69.0 0.8 collective-permute-done.11
  69.8 2.7 %collective-permute-done.10 = bf16[1,208,128]{2,1,0:T(8,128)(2,1)S(1)} collective-permute-done((bf16[1,208,128]{2,1,0:T(8,128)(2,1)S(1)}, bf16[1,208,128]{2,1,0:T(8,128)(2,1)S(1)}, u32[]{:S(2)}, u32[]{:S(2)}) %collective-permute-start.10) | collective-permute-done | bytes 53280 | tf_op jit(solution)/shard_map/ppermute | solution.py:403
  72.4 0.0 collective-permute-done.9
  72.4 0.0 collective-permute-done.12
  72.4 1.0 %collective-permute-done.13 = bf16[256,512]{1,0:T(8,128)(2,1)S(1)} collective-permute-done((bf16[256,512]{1,0:T(8,128)(2,1)}, bf16[256,512]{1,0:T(8,128)(2,1)S(1)}, u32[]{:S(2)}, u32[]{:S(2)}) %collective-permute-start.13) | collective-permute-done | bytes 262176 | tf_op jit(solution)/shard_map/ppermute | solution.py:396
  73.5 1.0 %collective-permute-start.16 = (bf16[4,208,128]{2,1,0:T(8,128)(2,1)S(1)}, bf16[4,208,128]{2,1,0:T(8,128)(2,1)S(1)}, u32[]{:S(2)}, u32[]{:S(2)}) collective-permute-start(bf16[4,208,128]{2,1,0:T(8,128)(2,1)S(1)} %pad_maximum_fusion.1), channel_id=1, source_target_pairs={{0,2},{1,3},{2,0},{3,1},{4,6},{5,7},{6,4},{7,5},{8,10},{9,11},{10,... | collective-permute-start | bytes 638984 | tf_op jit(solution)/shard_map/ppermute | solution.py:403
  74.5 2.4 %collective-permute-start.15 = (bf16[4,208,128]{2,1,0:T(8,128)(2,1)S(1)}, bf16[4,208,128]{2,1,0:T(8,128)(2,1)S(1)}, u32[]{:S(2)}, u32[]{:S(2)}) collective-permute-start(bf16[4,208,128]{2,1,0:T(8,128)(2,1)S(1)} %pad_maximum_fusion.1), channel_id=1, source_target_pairs={{0,4},{1,5},{2,6},{3,7},{4,0},{5,1},{6,2},{7,3},{8,12},{9,13},{10,... | collective-permute-start | bytes 638984 | tf_op jit(solution)/shard_map/ppermute | solution.py:403
  77.0 0.9 collective-permute-start.14
  77.8 0.0 copy-done
  77.8 0.8 add_convert_fusion.1
  78.6 2.0 %collective-permute-done.16 = bf16[4,208,128]{2,1,0:T(8,128)(2,1)S(1)} collective-permute-done((bf16[4,208,128]{2,1,0:T(8,128)(2,1)S(1)}, bf16[4,208,128]{2,1,0:T(8,128)(2,1)S(1)}, u32[]{:S(2)}, u32[]{:S(2)}) %collective-permute-start.16) | collective-permute-done | bytes 213024 | tf_op jit(solution)/shard_map/ppermute | solution.py:403
  80.6 2.3 %collective-permute-done.15 = bf16[4,208,128]{2,1,0:T(8,128)(2,1)S(1)} collective-permute-done((bf16[4,208,128]{2,1,0:T(8,128)(2,1)S(1)}, bf16[4,208,128]{2,1,0:T(8,128)(2,1)S(1)}, u32[]{:S(2)}, u32[]{:S(2)}) %collective-permute-start.15) | collective-permute-done | bytes 213024 | tf_op jit(solution)/shard_map/ppermute | solution.py:403
  82.9 1.8 %collective-permute-done.14 = bf16[4,208,128]{2,1,0:T(8,128)(2,1)S(1)} collective-permute-done((bf16[4,208,128]{2,1,0:T(8,128)(2,1)S(1)}, bf16[4,208,128]{2,1,0:T(8,128)(2,1)S(1)}, u32[]{:S(2)}, u32[]{:S(2)}) %collective-permute-start.14) | collective-permute-done | bytes 213024 | tf_op jit(solution)/shard_map/ppermute | solution.py:403
  84.7 0.1 pad_maximum_fusion.part_h
  84.8 0.1 collective-permute-start.17
  84.9 1.5 %unpack_mine.1 = (f32[3,512,512]{2,1,0:T(8,128)}, bf16[64,512]{1,0:T(8,128)(2,1)}, bf16[64,512]{1,0:T(8,128)(2,1)}) custom-call(bf16[16,208,128]{2,1,0:T(8,128)(2,1)S(1)} %pad_maximum_fusion.part_h), custom_call_target="tpu_custom_call" | custom-call | flops 100000000 | bytes 4194304 | tf_op jit(solution)/shard_map/unpack_mine/pallas_call | solution.py:381
  86.4 0.9 collective-permute-done.17.part_h
  87.2 1.5 %unpack_other.1 = (f32[3,512,512]{2,1,0:T(8,128)}, bf16[64,512]{1,0:T(8,128)(2,1)}, bf16[64,512]{1,0:T(8,128)(2,1)}) custom-call(bf16[16,208,128]{2,1,0:T(8,128)(2,1)S(1)} %collective-permute-done.17.part_h, f32[3,512,512]{2,1,0:T(8,128)} %get-tuple-element.92.refs_0_, ...), custom_call_target="tpu_custom_call", output_to_operand_aliasing={{0}: (1, {}), {1}: (2, {}), {2}: (3, {})} | custom-call | flops 100000000 | bytes 4194304 | tf_op jit(solution)/shard_map/unpack_other/pallas_call | solution.py:381
  (6 shorter events, 0.1 us)
Async XLA Ops:
  2.5 15.4 %collective-permute-start.1 = (bf16[256,512]{1,0:T(8,128)(2,1)S(1)}, bf16[256,512]{1,0:T(8,128)(2,1)S(1)}, u32[]{:S(2)}, u32[]{:S(2)}) collective-permute-start(bf16[256,512]{1,0:T(8,128)(2,1)S(1)} %fusion), channel_id=1, source_target_pairs={{0,28},{4,0},{8,4},{12,8},{16,12},{20,16},{24,20},{28,24},{1,29},{... | collective-permute-start | bytes 786440 | tf_op jit(solution)/shard_map/ppermute | solution.py:396
  8.6 10.5 %collective-permute-start = (bf16[256,512]{1,0:T(8,128)(2,1)S(1)}, bf16[256,512]{1,0:T(8,128)(2,1)S(1)}, u32[]{:S(2)}, u32[]{:S(2)}) collective-permute-start(bf16[256,512]{1,0:T(8,128)(2,1)S(1)} %fusion), channel_id=1, source_target_pairs={{0,4},{4,8},{8,12},{12,16},{16,20},{20,24},{24,28},{28,0},{1,5},{5... | collective-permute-start | bytes 786440 | tf_op jit(solution)/shard_map/ppermute | solution.py:396
  11.9 16.6 %all-to-all-start = ((f32[32,16,128]{2,1,0:T(8,128)}), f32[32,16,128]{2,1,0:T(8,128)S(1)}, u32[]{:S(2)}, u32[]{:S(2)}) async-start(f32[32,16,128]{2,1,0:T(8,128)} %get-tuple-element.56), calls=%async_computation | async-start | bytes 524288 | tf_op jit(solution)/shard_map/all_to_all | solution.py:483
  18.0 1.1 %copy-start.2 = (bf16[256,512]{1,0:T(8,128)(2,1)}, bf16[256,512]{1,0:T(8,128)(2,1)S(1)}, u32[]{:S(2)}) copy-start(bf16[256,512]{1,0:T(8,128)(2,1)S(1)} %collective-permute-done.1.xr_h) | copy-start | bytes 786436
  19.0 0.7 copy-start.3
  28.5 0.7 copy-start.1
  37.7 2.7 %collective-permute-start.2 = (bf16[16,208,128]{2,1,0:T(8,128)(2,1)}, bf16[16,208,128]{2,1,0:T(8,128)(2,1)S(1)}, u32[]{:S(2)}, u32[]{:S(2)}) collective-permute-start(bf16[16,208,128]{2,1,0:T(8,128)(2,1)} %get-tuple-element.65), channel_id=1, source_target_pairs={{0,1},{1,0},{2,3},{3,2},{4,5},{5,4},{6,7},{7,6},{8,9},{9,8},{10,11... | collective-permute-start | bytes 2555912 | tf_op jit(solution)/shard_map/ppermute | solution.py:403
  41.7 8.2 %collective-permute-start.5 = (bf16[4,208,128]{2,1,0:T(8,128)(2,1)S(1)}, bf16[4,208,128]{2,1,0:T(8,128)(2,1)S(1)}, u32[]{:S(2)}, u32[]{:S(2)}) collective-permute-start(bf16[4,208,128]{2,1,0:T(8,128)(2,1)S(1)} %get-tuple-element.99), channel_id=1, source_target_pairs={{0,2},{1,3},{2,0},{3,1},{4,6},{5,7},{6,4},{7,5},{8,10},{9,11},{10,... | collective-permute-start | bytes 638984 | tf_op jit(solution)/shard_map/ppermute | solution.py:403
  42.9 11.6 %collective-permute-start.4 = (bf16[4,208,128]{2,1,0:T(8,128)(2,1)S(1)}, bf16[4,208,128]{2,1,0:T(8,128)(2,1)S(1)}, u32[]{:S(2)}, u32[]{:S(2)}) collective-permute-start(bf16[4,208,128]{2,1,0:T(8,128)(2,1)S(1)} %get-tuple-element.100), channel_id=1, source_target_pairs={{0,4},{1,5},{2,6},{3,7},{4,0},{5,1},{6,2},{7,3},{8,12},{9,13},{10,... | collective-permute-start | bytes 638984 | tf_op jit(solution)/shard_map/ppermute | solution.py:403
  44.0 10.5 %collective-permute-start.3 = (bf16[4,208,128]{2,1,0:T(8,128)(2,1)S(1)}, bf16[4,208,128]{2,1,0:T(8,128)(2,1)S(1)}, u32[]{:S(2)}, u32[]{:S(2)}) collective-permute-start(bf16[4,208,128]{2,1,0:T(8,128)(2,1)S(1)} %get-tuple-element.101), channel_id=1, source_target_pairs={{0,6},{1,7},{2,4},{3,5},{4,2},{5,3},{6,0},{7,1},{8,14},{9,15},{10,... | collective-permute-start | bytes 638984 | tf_op jit(solution)/shard_map/ppermute | solution.py:403
  49.2 28.6 %copy-start = (f32[256,512]{1,0:T(8,128)S(1)}, f32[256,512]{1,0:T(8,128)}, u32[]{:S(2)}) copy-start(f32[256,512]{1,0:T(8,128)} %get-tuple-element.86) | copy-start | bytes 1572868
  54.7 8.0 %collective-permute-start.8 = (bf16[1,208,128]{2,1,0:T(8,128)(2,1)S(1)}, bf16[1,208,128]{2,1,0:T(8,128)(2,1)S(1)}, u32[]{:S(2)}, u32[]{:S(2)}) collective-permute-start(bf16[1,208,128]{2,1,0:T(8,128)(2,1)S(1)} %get-tuple-element.102), channel_id=1, source_target_pairs={{0,8},{1,9},{2,10},{3,11},{4,12},{5,13},{6,14},{7,15},{8,0},{9,1},... | collective-permute-start | bytes 159752 | tf_op jit(solution)/shard_map/ppermute | solution.py:403
  55.5 7.2 %collective-permute-start.7 = (bf16[1,208,128]{2,1,0:T(8,128)(2,1)S(1)}, bf16[1,208,128]{2,1,0:T(8,128)(2,1)S(1)}, u32[]{:S(2)}, u32[]{:S(2)}) collective-permute-start(bf16[1,208,128]{2,1,0:T(8,128)(2,1)S(1)} %get-tuple-element.103), channel_id=1, source_target_pairs={{0,16},{1,17},{2,18},{3,19},{4,20},{5,21},{6,22},{7,23},{8,24},{9,... | collective-permute-start | bytes 159752 | tf_op jit(solution)/shard_map/ppermute | solution.py:403
  57.9 6.6 %collective-permute-start.6 = (bf16[1,208,128]{2,1,0:T(8,128)(2,1)S(1)}, bf16[1,208,128]{2,1,0:T(8,128)(2,1)S(1)}, u32[]{:S(2)}, u32[]{:S(2)}) collective-permute-start(bf16[1,208,128]{2,1,0:T(8,128)(2,1)S(1)} %get-tuple-element.104), channel_id=1, source_target_pairs={{0,24},{1,25},{2,26},{3,27},{4,28},{5,29},{6,30},{7,31},{8,16},{9,... | collective-permute-start | bytes 159752 | tf_op jit(solution)/shard_map/ppermute | solution.py:403
  59.1 13.3 %collective-permute-start.12 = (bf16[256,512]{1,0:T(8,128)(2,1)}, bf16[256,512]{1,0:T(8,128)(2,1)S(1)}, u32[]{:S(2)}, u32[]{:S(2)}) collective-permute-start(bf16[256,512]{1,0:T(8,128)(2,1)} %get-tuple-element.81), channel_id=1, source_target_pairs={{0,28},{4,0},{8,4},{12,8},{16,12},{20,16},{24,20},{28,24},{1,29},{... | collective-permute-start | bytes 786440 | tf_op jit(solution)/shard_map/ppermute | solution.py:396
  62.7 10.8 %collective-permute-start.13 = (bf16[256,512]{1,0:T(8,128)(2,1)}, bf16[256,512]{1,0:T(8,128)(2,1)S(1)}, u32[]{:S(2)}, u32[]{:S(2)}) collective-permute-start(bf16[256,512]{1,0:T(8,128)(2,1)} %get-tuple-element.82), channel_id=1, source_target_pairs={{0,4},{4,8},{8,12},{12,16},{16,20},{20,24},{24,28},{28,0},{1,5},{5... | collective-permute-start | bytes 786440 | tf_op jit(solution)/shard_map/ppermute | solution.py:396
  64.5 5.2 %collective-permute-start.11 = (bf16[1,208,128]{2,1,0:T(8,128)(2,1)S(1)}, bf16[1,208,128]{2,1,0:T(8,128)(2,1)S(1)}, u32[]{:S(2)}, u32[]{:S(2)}) collective-permute-start(bf16[1,208,128]{2,1,0:T(8,128)(2,1)S(1)} %add_convert_fusion.3), channel_id=1, source_target_pairs={{0,8},{1,9},{2,10},{3,11},{4,12},{5,13},{6,14},{7,15},{8,0},{9,1},... | collective-permute-start | bytes 159752 | tf_op jit(solution)/shard_map/ppermute | solution.py:403
  64.6 7.8 %collective-permute-start.10 = (bf16[1,208,128]{2,1,0:T(8,128)(2,1)S(1)}, bf16[1,208,128]{2,1,0:T(8,128)(2,1)S(1)}, u32[]{:S(2)}, u32[]{:S(2)}) collective-permute-start(bf16[1,208,128]{2,1,0:T(8,128)(2,1)S(1)} %add_convert_fusion.3), channel_id=1, source_target_pairs={{0,16},{1,17},{2,18},{3,19},{4,20},{5,21},{6,22},{7,23},{8,24},{9,... | collective-permute-start | bytes 159752 | tf_op jit(solution)/shard_map/ppermute | solution.py:403
  65.7 6.7 %collective-permute-start.9 = (bf16[1,208,128]{2,1,0:T(8,128)(2,1)S(1)}, bf16[1,208,128]{2,1,0:T(8,128)(2,1)S(1)}, u32[]{:S(2)}, u32[]{:S(2)}) collective-permute-start(bf16[1,208,128]{2,1,0:T(8,128)(2,1)S(1)} %add_convert_fusion.3), channel_id=1, source_target_pairs={{0,24},{1,25},{2,26},{3,27},{4,28},{5,29},{6,30},{7,31},{8,16},{9,... | collective-permute-start | bytes 159752 | tf_op jit(solution)/shard_map/ppermute | solution.py:403
  73.5 7.1 %collective-permute-start.16 = (bf16[4,208,128]{2,1,0:T(8,128)(2,1)S(1)}, bf16[4,208,128]{2,1,0:T(8,128)(2,1)S(1)}, u32[]{:S(2)}, u32[]{:S(2)}) collective-permute-start(bf16[4,208,128]{2,1,0:T(8,128)(2,1)S(1)} %pad_maximum_fusion.1), channel_id=1, source_target_pairs={{0,2},{1,3},{2,0},{3,1},{4,6},{5,7},{6,4},{7,5},{8,10},{9,11},{10,... | collective-permute-start | bytes 638984 | tf_op jit(solution)/shard_map/ppermute | solution.py:403
  74.5 8.4 %collective-permute-start.15 = (bf16[4,208,128]{2,1,0:T(8,128)(2,1)S(1)}, bf16[4,208,128]{2,1,0:T(8,128)(2,1)S(1)}, u32[]{:S(2)}, u32[]{:S(2)}) collective-permute-start(bf16[4,208,128]{2,1,0:T(8,128)(2,1)S(1)} %pad_maximum_fusion.1), channel_id=1, source_target_pairs={{0,4},{1,5},{2,6},{3,7},{4,0},{5,1},{6,2},{7,3},{8,12},{9,13},{10,... | collective-permute-start | bytes 638984 | tf_op jit(solution)/shard_map/ppermute | solution.py:403
  77.0 7.7 %collective-permute-start.14 = (bf16[4,208,128]{2,1,0:T(8,128)(2,1)S(1)}, bf16[4,208,128]{2,1,0:T(8,128)(2,1)S(1)}, u32[]{:S(2)}, u32[]{:S(2)}) collective-permute-start(bf16[4,208,128]{2,1,0:T(8,128)(2,1)S(1)} %pad_maximum_fusion.1), channel_id=1, source_target_pairs={{0,6},{1,7},{2,4},{3,5},{4,2},{5,3},{6,0},{7,1},{8,14},{9,15},{10,... | collective-permute-start | bytes 638984 | tf_op jit(solution)/shard_map/ppermute | solution.py:403
  84.8 2.4 %collective-permute-start.17 = (bf16[16,208,128]{2,1,0:T(8,128)(2,1)S(1)}, bf16[16,208,128]{2,1,0:T(8,128)(2,1)S(1)}, u32[]{:S(2)}, u32[]{:S(2)}) collective-permute-start(bf16[16,208,128]{2,1,0:T(8,128)(2,1)S(1)} %pad_maximum_fusion.part_h), channel_id=1, source_target_pairs={{0,1},{1,0},{2,3},{3,2},{4,5},{5,4},{6,7},{7,6},{8,9},{9,8},{10,11... | collective-permute-start | bytes 2555912 | tf_op jit(solution)/shard_map/ppermute | solution.py:403
